TPU v7x, 32 devices: a whole 2x2x4 slice. The times are simulated.
32 devices in a mesh: wide: 4 (over x, core), narrow: 8 (over z, y).
Axes of the slice: x: 2, y: 2, z: 4, core: 2. Of those that a mesh axis runs over, the one named last changes fastest.
Arguments:
- node_feats: bfloat16 [28672, 256], P('narrow'), may hold values from -6 to 6
- grad_out: bfloat16 [28672, 256], P('narrow'), may hold values from -6 to 6
- tile_weight: bfloat16 [4, 8, 32, 128, 128], P('wide', 'narrow'), may hold values from -0.25 to 0.25
- tile_row: int32 [4, 8, 32], P('wide', 'narrow'), may hold values from 0 to 27
- src_block: int32 [4, 8, 32], P('wide', 'narrow'), may hold values from 0 to 27, as said below
- tile_count: int32 [4, 8, 8], P('wide', 'narrow'), may hold values from 1 to 4, as said below
- w_self: bfloat16 [256, 256], replicated, may hold values from -0.375 to 0.375
- w_out: bfloat16 [256, 256], replicated, may hold values from -0.375 to 0.375
- w_in: bfloat16 [256, 256], replicated, may hold values from -0.375 to 0.375
Outputs:
- hidden: bfloat16 [28672, 256], P('narrow')
- grad_feats: bfloat16 [28672, 256], P('narrow')
- grad_w_self: float32 [256, 256], replicated
- grad_w_out: float32 [256, 256], replicated
- grad_w_in: float32 [256, 256], replicated
Inputs may be any that keep to these rules, and one draw needn't show every extreme that they name: `src_block`: on each device the 4 slots of one owner name different blocks. `tile_count`: the live slots of an owner are its first ones.
All inputs are finite; a program needn't handle non-finite values.
Results may differ from a plain program's by a relative error of at most 0.0057.
Values may be sent and summed in bfloat16 or wider, within the bound.
No kernel may reach another device: no remote copies, remote signals or barrier semaphores. Data moves between devices by JAX's collectives and lax.ppermute only.
A program may use at most 128 MiB of HBM per device.

v0:
```python
import jax
import jax.numpy as jnp
from jax import lax
from jax.sharding import PartitionSpec as P


def block_sum(index, terms, blocks):
    onehot = (jnp.arange(blocks, dtype=jnp.int32)[:, None] == index[None, :]).astype(jnp.float32)
    merged = terms.reshape(terms.shape[0], terms.shape[1] * terms.shape[2])
    summed = jnp.dot(onehot, merged, precision=lax.Precision.HIGHEST)
    return summed.reshape(blocks * terms.shape[1], terms.shape[2])


def ahead_terms(tiles, sources):
    return jnp.einsum("sij,sjd->sid", tiles, sources, preferred_element_type=jnp.float32)


def behind_terms(tiles, sources):
    return jnp.einsum("sji,sjd->sid", tiles, sources, preferred_element_type=jnp.float32)


def body(node_feats, grad_out, tile_weight, tile_row, src_block, tile_count, w_self, w_out, w_in):
    peers = lax.axis_size("narrow")
    slots = tile_row.shape[-1]
    cap = slots // peers
    width = node_feats.shape[1]
    side = tile_weight.shape[-1]
    blocks = node_feats.shape[0] // side
    row_local = tile_row.reshape(slots)
    sources = src_block.reshape(slots)
    slot_ids = jnp.arange(slots, dtype=jnp.int32)
    live = slot_ids % cap < jnp.repeat(tile_count.reshape(peers), cap)
    tiles = tile_weight.reshape(slots, side, side) * live[:, None, None].astype(jnp.bfloat16)
    wanted = lax.all_to_all(sources, "narrow", split_axis=0, concat_axis=0, tiled=True)
    feat_blocks = node_feats.reshape(blocks, side, width)
    fetched = lax.all_to_all(feat_blocks[wanted], "narrow", split_axis=0, concat_axis=0, tiled=True)
    own_rows = feat_blocks[row_local]
    back_recv = lax.all_to_all(
        behind_terms(tiles, own_rows), "narrow", split_axis=0, concat_axis=0, tiled=True
    )
    out_part = block_sum(row_local, ahead_terms(tiles, fetched), blocks)
    in_part = block_sum(wanted, back_recv, blocks)
    agg_out, agg_in = lax.psum((out_part, in_part), "wide")
    agg_out = agg_out.astype(jnp.bfloat16)
    agg_in = agg_in.astype(jnp.bfloat16)
    pre = (
        jnp.dot(node_feats, w_self, preferred_element_type=jnp.float32)
        + jnp.dot(agg_out, w_out, preferred_element_type=jnp.float32)
        + jnp.dot(agg_in, w_in, preferred_element_type=jnp.float32)
    )
    sigma = jax.nn.sigmoid(pre)
    hidden = (pre * sigma).astype(jnp.bfloat16)
    grad_pre = (grad_out.astype(jnp.float32) * sigma * (1.0 + pre * (1.0 - sigma))).astype(
        jnp.bfloat16
    )
    over_rows = (((0,), (0,)), ((), ()))
    over_cols = (((1,), (1,)), ((), ()))
    part_self = lax.dot_general(node_feats, grad_pre, over_rows, preferred_element_type=jnp.float32)
    part_out = lax.dot_general(agg_out, grad_pre, over_rows, preferred_element_type=jnp.float32)
    part_in = lax.dot_general(agg_in, grad_pre, over_rows, preferred_element_type=jnp.float32)
    grad_agg_out = lax.dot_general(
        grad_pre, w_out, over_cols, preferred_element_type=jnp.float32
    ).astype(jnp.bfloat16)
    grad_agg_in = lax.dot_general(
        grad_pre, w_in, over_cols, preferred_element_type=jnp.float32
    ).astype(jnp.bfloat16)
    grad_self = lax.dot_general(grad_pre, w_self, over_cols, preferred_element_type=jnp.float32)
    grad_ws, grad_wo, grad_wi = lax.psum((part_self, part_out, part_in), "narrow")
    gout_rows, gin_rows = (grad_agg_out, grad_agg_in)
    gin_blocks = gin_rows.reshape(blocks, side, width)
    gout_blocks = gout_rows.reshape(blocks, side, width)
    fetched_grad = lax.all_to_all(
        gin_blocks[wanted], "narrow", split_axis=0, concat_axis=0, tiled=True
    )
    own_grad = gout_blocks[row_local]
    grad_back = lax.all_to_all(
        behind_terms(tiles, own_grad), "narrow", split_axis=0, concat_axis=0, tiled=True
    )
    total = block_sum(row_local, ahead_terms(tiles, fetched_grad), blocks) + block_sum(
        wanted, grad_back, blocks
    )
    grad_feats = (lax.psum(total, "wide") + grad_self).astype(jnp.bfloat16)
    return (hidden, grad_feats, grad_ws, grad_wo, grad_wi)


def solution(mesh):
    return jax.shard_map(
        body,
        mesh=mesh,
        in_specs=(
            P("narrow", None),
            P("narrow", None),
            P("wide", "narrow", None, None, None),
            P("wide", "narrow", None),
            P("wide", "narrow", None),
            P("wide", "narrow", None),
            P(),
            P(),
            P(),
        ),
        out_specs=(P("narrow", None), P("narrow", None), P(), P(), P()),
        check_vma=False,
    )
```

profile of v0, /device:TPU:0, one launch (start us, length us, event | category | flops | bytes accessed | tf_op | source)
XLA Modules:
  0.0 622.1 jit_solution(10104542623833901594)
XLA Ops:
  7.2 0.0 copy-start
  7.2 0.5 broadcast.82
  7.7 1.4 reduce.8
  9.0 0.1 all_to_all.20
  9.1 13.5 %all_to_all.32 = s32[8,4,1]{1,2,0:T(1,128)S(1)} all-to-all(s32[8,4,1]{1,2,0:T(1,128)S(1)} %bitcast.67), channel_id=1, replica_groups=mesh['wide'=4,'narrow'=8] {'narrow'}, dimensions={0} | all-to-all | bytes 256 | tf_op jit(solution)/shard_map/all_to_all | solution.py:34
  22.7 0.7 reduce.9
  23.3 0.1 all_to_all.22
  23.4 0.0 copy-done
  23.4 2.0 gather_fusion
  25.5 4.5 all-to-all-start.1
  30.0 0.0 copy-done.12
  30.0 0.1 broadcast_in_dim.2
  30.1 0.1 reshape.133
  30.2 0.0 copy-start.4
  30.2 2.0 gather_fusion.1
  32.2 4.7 fusion.9
  36.9 40.2 %all-to-all-done.1 = bf16[32,128,256]{2,1,0:T(8,128)(2,1)} async-done(((bf16[32,128,256]{2,1,0:T(8,128)(2,1)}), bf16[32,128,256]{2,1,0:T(8,128)(2,1)}, u32[]{:S(2)}, u32[]{:S(2)}) %all-to-all-start.1) | async-done | bytes 2097184 | tf_op jit(solution)/shard_map/all_to_all | solution.py:36
  77.1 4.6 all-to-all-start.2
  81.6 2.4 fusion.24
  84.1 0.1 eq.23
  84.1 2.3 fusion.10
  86.5 2.4 copy.26
  88.9 4.1 fusion.17
  93.0 4.8 reshape.136
  97.8 76.3 %all-to-all-done.2 = f32[32,128,256]{2,1,0:T(8,128)} async-done(((f32[32,128,256]{2,1,0:T(8,128)}), f32[32,128,256]{2,1,0:T(8,128)}, u32[]{:S(2)}, u32[]{:S(2)}) %all-to-all-start.2) | async-done | bytes 4194336 | tf_op jit(solution)/shard_map/all_to_all | solution.py:38
  174.2 4.6 copy.27
  178.8 4.1 fusion.15
  182.9 4.8 reshape.139
  187.7 128.9 %all-reduce.9 = (bf16[3584,256]{1,0:T(8,128)(2,1)}, bf16[3584,256]{1,0:T(8,128)(2,1)}) all-reduce(f32[3584,256]{1,0:T(8,128)} %reshape.136, f32[3584,256]{1,0:T(8,128)} %reshape.139), channel_id=1, replica_groups=mesh['wide'=4,'narrow'=8] {'wide'}, use_global_device_ids=true, to_apply=%region_0.1 | all-reduce | flops 1835008 | bytes 11010048 | tf_op jit(solution)/shard_map/psum | solution.py:43
  316.6 3.4 convolution_add_fusion.3
  320.0 0.4 copy-done.14
  320.4 3.3 multiply_convert_fusion
  323.7 1.9 convolution_convert_fusion.1
  325.6 0.0 copy-done.1
  325.6 3.5 gather_fusion.2
  329.2 4.9 all-to-all-start.3
  334.1 3.4 convolution_convert_fusion
  337.5 3.5 gather_fusion.3
  341.1 4.7 fusion.7
  345.7 37.2 %all-to-all-done.3 = bf16[32,128,256]{2,1,0:T(8,128)(2,1)} async-done(((bf16[32,128,256]{2,1,0:T(8,128)(2,1)}), bf16[32,128,256]{2,1,0:T(8,128)(2,1)}, u32[]{:S(2)}, u32[]{:S(2)}) %all-to-all-start.3) | async-done | bytes 2097184 | tf_op jit(solution)/shard_map/all_to_all | solution.py:72
  382.9 4.6 all-to-all-start.4
  387.5 0.0 all-reduce.8.cloned.1.call-start
  387.6 0.0 copy-start.5
  387.6 3.6 fusion.25
  391.2 1.4 fusion.26
  392.6 1.4 convolution_bitcast_fusion
  393.9 0.0 all-reduce.8.cloned.1.call-update
  394.0 0.3 all-reduce.6.cloned.1.call-start
  394.2 2.3 fusion.8
  396.6 2.4 copy.28
  399.0 4.1 fusion.16
  403.1 88.1 %all-to-all-done.4 = f32[32,128,256]{2,1,0:T(8,128)} async-done(((f32[32,128,256]{2,1,0:T(8,128)}), f32[32,128,256]{2,1,0:T(8,128)}, u32[]{:S(2)}, u32[]{:S(2)}) %all-to-all-start.4) | async-done | bytes 4194336 | tf_op jit(solution)/shard_map/all_to_all | solution.py:76
  491.2 4.8 copy.29
  495.9 0.0 copy-done.3
  495.9 4.2 convolution_add_fusion
  500.2 4.8 add.73
  505.0 0.0 all-reduce.6.cloned.1.call-update
  505.0 25.9 %all-reduce.8.cloned.1.call-done = (f32[256,256]{0,1:T(8,128)}, f32[256,256]{1,0:T(8,128)}, f32[256,256]{1,0:T(8,128)}) async-done(((f32[256,256]{0,1:T(8,128)}, f32[256,256]{1,0:T(8,128)}, f32[256,256]{1,0:T(8,128)}), (f32[256,256]{0,1:T(8,128)}, f32[256,256]{1,0:T(8,128)}, f32[256,256]{1,0:T(8,128)})) %all-reduce.8.cloned.1.call-update) | async-done | bytes 786448 | tf_op jit(solution)/shard_map/psum | solution.py:68
  531.0 1.8 copy.23
  532.7 76.6 %all-reduce.6.cloned.1.call-done = f32[3584,256]{1,0:T(8,128)} async-done(((f32[3584,256]{1,0:T(8,128)}), f32[3584,256]{1,0:T(8,128)}) %all-reduce.6.cloned.1.call-update) | async-done | bytes 3670032 | tf_op jit(solution)/shard_map/psum | solution.py:82
  609.4 4.5 fusion
  613.9 0.7 copy.38
  614.6 0.0 copy-done.8
  614.6 0.7 copy.39
  (26 shorter events, 0.1 us)
Async XLA Ops:
  7.2 16.3 %copy-start = (bf16[3584,256]{1,0:T(8,128)(2,1)S(1)}, bf16[3584,256]{1,0:T(8,128)(2,1)}, u32[]{:S(2)}) copy-start(bf16[3584,256]{1,0:T(8,128)(2,1)} %param.9) | copy-start | bytes 5505028
  25.5 4.5 copy-start.12
  25.5 4.7 copy-start.11
  25.5 51.6 %all-to-all-start.1 = ((bf16[32,128,256]{2,1,0:T(8,128)(2,1)}), bf16[32,128,256]{2,1,0:T(8,128)(2,1)}, u32[]{:S(2)}, u32[]{:S(2)}) async-start(bf16[32,128,256]{2,1,0:T(8,128)(2,1)} %gather_fusion), calls=%async_computation.1 | async-start | bytes 4194304 | tf_op jit(solution)/shard_map/all_to_all | solution.py:36
  30.2 2.1 copy-start.4
  36.9 44.7 %copy-start.7 = (bf16[256,256]{1,0:T(8,128)(2,1)S(1)}, bf16[256,256]{1,0:T(8,128)(2,1)}, u32[]{:S(2)}) copy-start(bf16[256,256]{1,0:T(8,128)(2,1)} %param.15) | copy-start | bytes 393220
  77.1 97.1 %all-to-all-start.2 = ((f32[32,128,256]{2,1,0:T(8,128)}), f32[32,128,256]{2,1,0:T(8,128)}, u32[]{:S(2)}, u32[]{:S(2)}) async-start(f32[32,128,256]{2,1,0:T(8,128)} %fusion.9), calls=%async_computation.2 | async-start | bytes 8388608 | tf_op jit(solution)/shard_map/all_to_all | solution.py:38
  187.7 128.9 %copy-start.6 = (bf16[256,256]{1,0:T(8,128)(2,1)S(1)}, bf16[256,256]{1,0:T(8,128)(2,1)}, u32[]{:S(2)}) copy-start(bf16[256,256]{1,0:T(8,128)(2,1)} %param.16) | copy-start | bytes 393220
  316.6 3.4 copy-start.10
  316.6 3.4 copy-start.13
  316.6 3.8 copy-start.14
  323.7 1.9 copy-start.1
  329.2 53.8 %all-to-all-start.3 = ((bf16[32,128,256]{2,1,0:T(8,128)(2,1)}), bf16[32,128,256]{2,1,0:T(8,128)(2,1)}, u32[]{:S(2)}, u32[]{:S(2)}) async-start(bf16[32,128,256]{2,1,0:T(8,128)(2,1)} %gather_fusion.2), calls=%async_computation.3 | async-start | bytes 4194304 | tf_op jit(solution)/shard_map/all_to_all | solution.py:72
  382.9 108.2 %all-to-all-start.4 = ((f32[32,128,256]{2,1,0:T(8,128)}), f32[32,128,256]{2,1,0:T(8,128)}, u32[]{:S(2)}, u32[]{:S(2)}) async-start(f32[32,128,256]{2,1,0:T(8,128)} %fusion.7), calls=%async_computation.4 | async-start | bytes 8388608 | tf_op jit(solution)/shard_map/all_to_all | solution.py:76
  387.5 143.4 %all-reduce.8.cloned.1.call-start = ((), (), s32[]{:S(2)}) async-start(), calls=%async_computation.6 | async-start | bytes 1572864 | tf_op jit(solution)/shard_map/psum | solution.py:68
  387.6 3.6 copy-start.2
  387.6 3.6 copy-start.5
  394.0 215.4 %all-reduce.6.cloned.1.call-start = ((), (), s32[]{:S(2)}) async-start(), calls=%async_computation.5 | async-start | bytes 7340032 | tf_op jit(solution)/shard_map/psum | solution.py:82
  491.2 4.8 copy-start.3
  532.7 81.1 %copy-start.9 = (f32[256,256]{1,0:T(8,128)S(1)}, f32[256,256]{1,0:T(8,128)}, u32[]{:S(2)}) copy-start(f32[256,256]{1,0:T(8,128)} %get-tuple-element.30) | copy-start | bytes 786436
  532.7 81.8 %copy-start.8 = (f32[256,256]{1,0:T(8,128)S(1)}, f32[256,256]{1,0:T(8,128)}, u32[]{:S(2)}) copy-start(f32[256,256]{1,0:T(8,128)} %get-tuple-element.31) | copy-start | bytes 786436
Sparse Core Ops, SparseCore 0:
  394.1 136.8 all-reduce.7
  533.4 75.8 all-reduce.5
where the time goes:
time: 623 us; the launch traced here: 622 us
  waiting for transfers between devices  344 us (55%)
  blocking collectives  142 us (23%)
  matrix products  55.8 us (9%)
  local copies, waits for them, and re-layouts  44.4 us (7%)
  starting transfers between devices  18.8 us (3%)
  between operations  14.2 us (2%)
    psum x1, blocking collectives, body(): agg_out, agg_in = lax.psum((out_part, in_part), 'wide')  129 us
    all_to_all x1, waiting for transfers between devices, body(): lax.all_to_all(behind_terms(tiles, own_grad), 'narrow', split_axis=0, con...  88.1 us
    psum x1, waiting for transfers between devices, body(): grad_feats = (lax.psum(total, 'wide') + grad_self).astype(jnp.bfloat16)  76.6 us
    all_to_all x1, waiting for transfers between devices, body(): lax.all_to_all(behind_terms(tiles, own_rows), 'narrow', split_axis=0, con...  76.3 us
    all_to_all x1, waiting for transfers between devices, body(): lax.all_to_all(feat_blocks[wanted], 'narrow', split_axis=0, concat_axis=0...  40.2 us
    all_to_all x1, waiting for transfers between devices, body(): lax.all_to_all(gin_blocks[wanted], 'narrow', split_axis=0, concat_axis=0,...  37.2 us
    psum x1, waiting for transfers between devices, body(): lax.psum((part_self, part_out, part_in), 'narrow')  25.9 us
    unnamed x38, local copies, waits for them, and re-layouts  18.4 us
  transfers between devices with their start and end apart: 6, of which 6 were waited for; matrix products, arithmetic and copies ran while one was open for 11% of the time, Pallas kernels for 0%

commit v1 on v0

v1 whole, which is shorter than its diff:
```python
import functools

import jax
import jax.numpy as jnp
from jax import lax
from jax.experimental import pallas as pl
from jax.experimental.pallas import tpu as pltpu
from jax.sharding import PartitionSpec as P

BF = jnp.bfloat16
F32 = jnp.float32
META = 16
CORES = 2


def dims(wide, narrow):
    z = 4 if narrow % 4 == 0 else 1
    return wide // CORES, z, narrow // z


def x_shift(a, k, wide):
    return lax.ppermute(a, "wide", [(i, (i + CORES * k) % wide) for i in range(wide)])


def core_swap(a, wide):
    return lax.ppermute(a, "wide", [(i, i ^ 1) for i in range(wide)])


def core_send(a, source, wide):
    return lax.ppermute(a, "wide", [(i, i ^ 1) for i in range(wide) if i % CORES == source])


def z_shift(a, zs, ys):
    return lax.ppermute(
        a, "narrow", [(z * ys + y, (z + 1) % zs * ys + y) for z in range(zs) for y in range(ys)]
    )


def y_shift(a, zs, ys):
    return lax.ppermute(
        a, "narrow", [(z * ys + y, z * ys + (y + 1) % ys) for z in range(zs) for y in range(ys)]
    )


def gather_narrow(piece, zs, ys):
    pieces = {}
    held = piece
    for k in range(zs):
        pieces[k, 0] = held
        if k < zs - 1:
            held = z_shift(held, zs, ys)
    for k in range(zs):
        for j in range(1, ys):
            pieces[k, j] = y_shift(pieces[k, j - 1], zs, ys)
    return [pieces[k, j] for k in range(zs) for j in range(ys)]


def aggregate_kernel(
    wide, narrow, cap, blocks, side, rr, xx, order, core, *refs
):
    half = blocks // CORES
    rows = refs[:wide]
    cols = refs[wide : 2 * wide]
    mine = refs[2 * wide : 2 * wide + narrow]
    other = refs[2 * wide + narrow : 2 * wide + 2 * narrow]
    out_ref, tiles, feats, acc, tile_sem, feat_sem = refs[2 * wide + 2 * narrow :]

    def tile_copy(source, w):
        return pltpu.make_async_copy(source[w], tiles.at[w], tile_sem.at[w])

    @pl.when(core[0] == 0)
    def _():
        for w in range(wide):
            tile_copy(rows, w).start()

    @pl.when(core[0] == 1)
    def _():
        for w in range(wide):
            tile_copy(cols, w).start()

    copies = []
    for q in range(narrow):
        for h, source in enumerate((mine, other)):
            copy = pltpu.make_async_copy(
                source[q],
                feats.at[pl.ds(q * blocks + h * half, half)],
                feat_sem.at[q * CORES + h],
            )
            copy.start()
            copies.append(copy)
    acc[...] = jnp.zeros_like(acc)
    for w in range(wide):
        tile_copy(rows, w).wait()
    for q in range(narrow):
        copies[CORES * q].wait()
        copies[CORES * q + 1].wait()
        owner = order[q]

        def step(w, carry):
            base = (w * narrow + owner) * cap
            terms = []
            for i in range(cap):
                terms.append(
                    jnp.dot(
                        tiles[w, owner, i * side : (i + 1) * side, :],
                        feats[q * blocks + xx[base + i]],
                        preferred_element_type=F32,
                    )
                )
            for i in range(cap):
                row = rr[base + i]
                acc[row] = acc[row] + terms[i]
            return carry

        lax.fori_loop(0, wide, step, 0)
    for b in range(blocks):
        out_ref[b * side : (b + 1) * side, :] = acc[b].astype(BF)


def aggregate(rr, xx, order, core, rows, cols, mine, other, blocks, side, cap):
    wide, narrow = len(rows), len(mine)
    width = mine[0].shape[-1]
    any_spec = pl.BlockSpec(memory_space=pl.ANY)
    smem = pl.BlockSpec(memory_space=pltpu.SMEM)
    return pl.pallas_call(
        functools.partial(aggregate_kernel, wide, narrow, cap, blocks, side),
        out_shape=jax.ShapeDtypeStruct((blocks * side, width), BF),
        in_specs=[smem] * 4 + [any_spec] * (2 * wide + 2 * narrow),
        out_specs=pl.BlockSpec(memory_space=pltpu.VMEM),
        scratch_shapes=[
            pltpu.VMEM((wide,) + rows[0].shape, BF),
            pltpu.VMEM((narrow * blocks, side, width), BF),
            pltpu.VMEM((blocks + 1, side, width), F32),
            pltpu.SemaphoreType.DMA((wide,)),
            pltpu.SemaphoreType.DMA((CORES * narrow,)),
        ],
        compiler_params=pltpu.CompilerParams(vmem_limit_bytes=56 << 20),
    )(rr, xx, order, core, *rows, *cols, *mine, *other)


def linear_sum(parts, weights, dims_):
    total = None
    for part, weight in zip(parts, weights):
        term = lax.dot_general(part, weight, dims_, preferred_element_type=F32)
        total = term if total is None else total + term
    return total


PLAIN = (((1,), (0,)), ((), ()))


def layer_kernel(parts, *refs):
    ins = refs[:parts]
    cotangent = refs[parts]
    weights = refs[parts + 1 : 2 * parts + 1]
    hidden_ref, grad_ref = refs[2 * parts + 1 :]
    pre = linear_sum([r[...] for r in ins], [r[...] for r in weights], PLAIN)
    sigma = 1.0 / (1.0 + jnp.exp(-pre))
    hidden_ref[...] = (pre * sigma).astype(BF)
    grad_ref[...] = (cotangent[...].astype(F32) * sigma * (1.0 + pre * (1.0 - sigma))).astype(BF)


def final_kernel(parts, *refs):
    ins = refs[:parts]
    weights = refs[parts : 2 * parts]
    out_ref = refs[2 * parts]
    out_ref[...] = linear_sum([r[...] for r in ins], [r[...] for r in weights], PLAIN).astype(BF)


def row_specs(arrays, step):
    return [pl.BlockSpec((step, a.shape[1]), lambda i: (i, 0)) for a in arrays]


def whole_specs(arrays):
    return [pl.BlockSpec(a.shape, lambda i: (0, 0)) for a in arrays]


def layer(ins, cotangent, weights, step):
    rows, width = cotangent.shape
    shape = jax.ShapeDtypeStruct((rows, width), BF)
    return pl.pallas_call(
        functools.partial(layer_kernel, len(ins)),
        grid=(rows // step,),
        out_shape=(shape, shape),
        in_specs=row_specs(list(ins) + [cotangent], step) + whole_specs(weights),
        out_specs=tuple(row_specs([cotangent, cotangent], step)),
        compiler_params=pltpu.CompilerParams(vmem_limit_bytes=40 << 20),
    )(*ins, cotangent, *weights)


def final(ins, weights, step):
    rows, width = ins[0].shape[0], weights[0].shape[1]
    return pl.pallas_call(
        functools.partial(final_kernel, len(ins)),
        grid=(rows // step,),
        out_shape=jax.ShapeDtypeStruct((rows, width), BF),
        in_specs=row_specs(ins, step) + whole_specs(weights),
        out_specs=pl.BlockSpec((step, width), lambda i: (i, 0)),
        compiler_params=pltpu.CompilerParams(vmem_limit_bytes=40 << 20),
    )(*ins, *weights)


def body(node_feats, grad_out, tile_weight, tile_row, src_block, tile_count, w_self, w_out, w_in):
    wide, narrow = lax.axis_size("wide"), lax.axis_size("narrow")
    xs, zs, ys = dims(wide, narrow)
    slots = tile_row.shape[-1]
    cap = slots // narrow
    nodes, width = node_feats.shape
    side = tile_weight.shape[-1]
    blocks = nodes // side
    half = blocks // CORES
    cols = width // xs
    step = nodes // 7
    w_id, n_id = lax.axis_index("wide"), lax.axis_index("narrow")
    core, x_id = w_id % CORES, w_id // CORES
    z_id, y_id = n_id // ys, n_id % ys

    tiles = tile_weight.reshape(narrow, cap, side, side)
    live = jnp.arange(cap, dtype=jnp.int32)[None, :] < tile_count.reshape(narrow, 1)
    facts = jnp.stack(
        [
            tile_row.reshape(narrow, cap).astype(BF),
            src_block.reshape(narrow, cap).astype(BF),
            live.astype(BF),
        ],
        axis=1,
    )
    facts = jnp.pad(facts, ((0, 0), (0, META - 3), (0, side - cap)))

    def packed(t):
        return jnp.concatenate([t.reshape(narrow, cap * side, side), facts], axis=1)

    row_own = packed(tiles)
    col_own = lax.all_to_all(
        packed(tiles.swapaxes(2, 3)), "narrow", split_axis=0, concat_axis=0, tiled=True
    )
    row_sets = [row_own] + [x_shift(row_own, k, wide) for k in range(1, xs)]
    col_sets = [col_own] + [x_shift(col_own, k, wide) for k in range(1, xs)]
    row_sets += [core_send(a, 1, wide) for a in row_sets]
    col_sets += [core_send(a, 0, wide) for a in col_sets]

    def fact(sets, i):
        return jnp.stack([a[:, cap * side + i, :cap] for a in sets]).astype(jnp.int32)

    row_f = [fact(row_sets, i) for i in range(3)]
    col_f = [fact(col_sets, i) for i in range(3)]
    first = core == 0
    to_block = jnp.where(first, row_f[0], col_f[1])
    from_block = jnp.where(first, row_f[1], col_f[0])
    alive = jnp.where(first, row_f[2], col_f[2])
    rr = jnp.where(alive > 0, to_block, blocks).reshape(-1)
    xx = (jnp.where(from_block // half == core, 0, half) + from_block % half).reshape(-1)
    q = jnp.arange(narrow, dtype=jnp.int32)
    order = ((z_id - q // ys) % zs * ys + (y_id - q % ys) % ys).astype(jnp.int32)
    core_arr = core.reshape(1).astype(jnp.int32)

    def spread(a):
        piece = lax.dynamic_slice(a, (core * half * side, x_id * cols), (half * side, cols))
        mine = gather_narrow(piece.reshape(half, side, cols), zs, ys)
        other = [core_swap(p, wide) for p in mine]
        own = aggregate(
            rr, xx, order, core_arr, row_sets, col_sets, mine, other, blocks, side, cap
        )
        here = [own] + [x_shift(own, k, wide) for k in range(1, xs)]
        return own, here + [core_swap(p, wide) for p in here]

    def weight_parts(first_w, second_w):
        own_w = jnp.where(first, first_w, second_w)
        oth_w = jnp.where(first, second_w, first_w)
        at = [(x_id - k) % xs * cols for k in range(xs)]
        return [
            lax.dynamic_slice(w, (a, 0), (cols, width)) for w in (own_w, oth_w) for a in at
        ]

    own, aggs = spread(node_feats)
    hidden, grad_pre = layer(
        [node_feats] + aggs, grad_out, [w_self] + weight_parts(w_out, w_in), step
    )
    over_rows = (((0,), (0,)), ((), ()))
    share = width // wide
    feat_part = lax.dynamic_slice(node_feats, (0, w_id * share), (nodes, share))
    grad_part = jnp.concatenate(
        [
            lax.dot_general(own, grad_pre, over_rows, preferred_element_type=F32),
            lax.dot_general(feat_part, grad_pre, over_rows, preferred_element_type=F32),
        ],
        axis=0,
    )
    for pairs in narrow_swaps(narrow):
        grad_part = grad_part + lax.ppermute(grad_part, "narrow", pairs)
    x_parts = [grad_part] + [x_shift(grad_part, k, wide) for k in range(1, xs)]
    stack = jnp.stack(x_parts)
    stack = jnp.stack([stack, core_swap(stack, wide)])
    stack = jnp.where(first, stack, stack[::-1])
    chip = (x_id - jnp.arange(xs)) % xs
    stack = stack[:, chip] if xs > 1 else stack
    agg_grads = stack[:, :, :cols].reshape(CORES, width, width)
    grad_ws = stack[:, :, cols:].swapaxes(0, 1).reshape(width, width)

    _, backs = spread(grad_pre)
    grad_feats = final(
        [grad_pre] + backs, [w_self.T] + weight_parts(w_in.T, w_out.T), step
    )
    return (hidden, grad_feats, grad_ws, agg_grads[0], agg_grads[1])


def narrow_swaps(narrow):
    bit = 1
    while bit < narrow:
        yield [(i, i ^ bit) for i in range(narrow)]
        bit *= 2


def solution(mesh):
    return jax.shard_map(
        body,
        mesh=mesh,
        in_specs=(
            P("narrow", None),
            P("narrow", None),
            P("wide", "narrow", None, None, None),
            P("wide", "narrow", None),
            P("wide", "narrow", None),
            P("wide", "narrow", None),
            P(),
            P(),
            P(),
        ),
        out_specs=(P("narrow", None), P("narrow", None), P(), P(), P()),
        check_vma=False,
    )
```

time: 623 us -> 306 us (0.49)
  waiting for transfers between devices: 344 us -> 163 us
  blocking collectives: 142 us -> 0 us
  matrix products: 55.8 us -> 1.21 us
  Pallas kernels: 0 us -> 37.6 us
  starting transfers between devices: 18.8 us -> 40.5 us
  between operations: 14.2 us -> 1.22 us
  other arithmetic: 2.04 us -> 11.5 us
    all_to_all x4 -> x1, waiting for transfers between devices: 242 us -> 25 us  [body(): lax.all_to_all(packed(tiles.swapaxes(2, 3)), 'narrow', split_axis=0, conc...]
    ppermute x0 -> x47, waiting for transfers between devices: none -> 138 us  [the longest x6 56.2 us: z_shift(): lax.ppermute(a, 'narrow', [(z * ys + y, (z + 1) % zs * ys + y) for z in r...]
    psum x1 -> x0, blocking collectives: 129 us -> none  [body(): agg_out, agg_in = lax.psum((out_part, in_part), 'wide')]
    psum x2 -> x0, waiting for transfers between devices: 103 us -> none  [the longest x1 76.6 us: body(): grad_feats = (lax.psum(total, 'wide') + grad_self).astype(jnp.bfloat16)]
    dot_general x17 -> x2, matrix products: 55.8 us -> 1.21 us  [the longest x1 0.74 us: body(): lax.dot_general(feat_part, grad_pre, over_rows, preferred_element_type=F32)]
    pallas_call x0 -> x4, Pallas kernels: none -> 37.6 us  [the longest x2 23.4 us: aggregate(): pl.pallas_call(functools.partial(aggregate_kernel, wide, narrow, cap, blo...]
    ppermute x0 -> x47, starting transfers between devices: none -> 33.1 us  [the longest x8 9.79 us: y_shift(): lax.ppermute(a, 'narrow', [(z * ys + y, z * ys + (y + 1) % ys) for z in r...]
    slice x0 -> x30, local copies, waits for them, and re-layouts: none -> 23 us  [the longest x28 19.5 us: fact(): a[:, cap * side + i, :cap]]
  transfers between devices with their start and end apart: 6 -> 48, of which waited for: 6 -> 18; matrix products, arithmetic and copies ran while one was open for 11% -> 16% of each run, Pallas kernels for 0% -> 4%
where the time goes in v1:
time: 306 us; the launch traced here: 304 us
  waiting for transfers between devices  163 us (53%)
  local copies, waits for them, and re-layouts  49.3 us (16%)
  starting transfers between devices  40.5 us (13%)
  Pallas kernels  37.6 us (12%)
  other arithmetic  11.5 us (4%)
    ppermute x6, waiting for transfers between devices, z_shift(): lax.ppermute(a, 'narrow', [(z * ys + y, (z + 1) % zs * ys + y) for z in r...  56.2 us
    ppermute x8, waiting for transfers between devices, y_shift(): lax.ppermute(a, 'narrow', [(z * ys + y, z * ys + (y + 1) % ys) for z in r...  35.6 us
    ppermute x5, waiting for transfers between devices, x_shift(): lax.ppermute(a, 'wide', [(i, (i + CORES * k) % wide) for i in range(wide)])  28.2 us
    all_to_all x1, waiting for transfers between devices, body(): lax.all_to_all(packed(tiles.swapaxes(2, 3)), 'narrow', split_axis=0, conc...  25 us
    pallas_call x2, Pallas kernels, aggregate(): pl.pallas_call(functools.partial(aggregate_kernel, wide, narrow, cap, blo...  23.4 us
    slice x28, local copies, waits for them, and re-layouts, fact(): a[:, cap * side + i, :cap]  19.5 us
    ppermute x3, waiting for transfers between devices, body(): grad_part = grad_part + lax.ppermute(grad_part, 'narrow', pairs)  16.6 us
    unnamed x63, local copies, waits for them, and re-layouts  11.9 us
  transfers between devices with their start and end apart: 48, of which 18 were waited for; matrix products, arithmetic and copies ran while one was open for 16% of the time, Pallas kernels for 4%

profile of v1, /device:TPU:0, one launch (start us, length us, event | category | flops | bytes accessed | tf_op | source)
XLA Modules:
  0.0 304.0 jit_solution(18385977152889858414)
XLA Ops:
  1.5 0.8 compare_convert_fusion
  2.3 1.6 copy.137
  4.0 1.1 pad_maximum_fusion
  5.1 7.4 %all-to-all-start = ((bf16[8,528,128]{2,1,0:T(8,128)(2,1)}), bf16[8,528,128]{2,1,0:T(8,128)(2,1)S(1)}, u32[]{:S(2)}, u32[]{:S(2)}) async-start(bf16[8,528,128]{2,1,0:T(8,128)(2,1)} %get-tuple-element.44), calls=%async_computation | async-start | bytes 2162688 | tf_op jit(solution)/shard_map/all_to_all | solution.py:234
  12.6 1.5 collective-permute-start
  14.1 25.0 %all-to-all-done.refs_4_ = bf16[8,528,128]{2,1,0:T(8,128)(2,1)S(1)} async-done(((bf16[8,528,128]{2,1,0:T(8,128)(2,1)}), bf16[8,528,128]{2,1,0:T(8,128)(2,1)S(1)}, u32[]{:S(2)}, u32[]{:S(2)}) %all-to-all-start) | async-done | bytes 1081376 | tf_op jit(solution)/shard_map/all_to_all | solution.py:234
  39.0 1.5 collective-permute-start.3
  40.5 1.3 collective-permute-start.1
  41.8 1.3 collective-permute-start.2
  43.2 1.9 dynamic_slice.33
  45.1 13.4 %collective-permute-done.7.refs_10_ = bf16[14,128,128]{2,1,0:T(8,128)(2,1)} collective-permute-done((bf16[14,128,128]{2,1,0:T(8,128)(2,1)}, bf16[14,128,128]{2,1,0:T(8,128)(2,1)}, u32[]{:S(2)}, u32[]{:S(2)}) %collective-permute-start.7) | collective-permute-done | bytes 458784 | tf_op jit(solution)/shard_map/ppermute | solution.py:34
  60.6 4.9 %collective-permute-start.4 = (bf16[8,528,128]{2,1,0:T(8,128)(2,1)S(1)}, bf16[8,528,128]{2,1,0:T(8,128)(2,1)}, u32[]{:S(2)}, u32[]{:S(2)}) collective-permute-start(bf16[8,528,128]{2,1,0:T(8,128)(2,1)S(1)} %all-to-all-done.refs_4_), channel_id=1, source_target_pairs={{0,8},{16,24},{1,9},{17,25},{2,10},{18,26},{3,11},{19,27},{4,12},{... | collective-permute-start | bytes 3244040 | tf_op jit(solution)/shard_map/ppermute | solution.py:30
  65.5 2.3 collective-permute-start.5
  68.4 4.6 %collective-permute-done.9.refs_12_ = bf16[14,128,128]{2,1,0:T(8,128)(2,1)} collective-permute-done((bf16[14,128,128]{2,1,0:T(8,128)(2,1)}, bf16[14,128,128]{2,1,0:T(8,128)(2,1)}, u32[]{:S(2)}, u32[]{:S(2)}) %collective-permute-start.9) | collective-permute-done | bytes 458784 | tf_op jit(solution)/shard_map/ppermute | solution.py:34
  73.0 1.4 collective-permute-start.6
  74.9 0.9 fusion.27
  81.6 0.9 fusion.28
  84.4 2.1 collective-permute-done.6.refs_9_
  86.5 1.4 collective-permute-start.8
  87.9 1.5 collective-permute-done.11.refs_14_
  90.1 1.4 collective-permute-start.12
  91.5 0.8 fusion.30
  93.0 1.4 fusion.31
  94.5 1.3 copy.157
  98.5 1.4 fusion.32
  100.7 9.3 %collective-permute-done.10.refs_13_ = bf16[14,128,128]{2,1,0:T(8,128)(2,1)} collective-permute-done((bf16[14,128,128]{2,1,0:T(8,128)(2,1)}, bf16[14,128,128]{2,1,0:T(8,128)(2,1)}, u32[]{:S(2)}, u32[]{:S(2)}) %collective-permute-start.10) | collective-permute-done | bytes 458784 | tf_op jit(solution)/shard_map/ppermute | solution.py:40
  110.1 8.8 %collective-permute-done.12.refs_15_ = bf16[14,128,128]{2,1,0:T(8,128)(2,1)} collective-permute-done((bf16[14,128,128]{2,1,0:T(8,128)(2,1)S(1)}, bf16[14,128,128]{2,1,0:T(8,128)(2,1)}, u32[]{:S(2)}, u32[]{:S(2)}) %collective-permute-start.12) | collective-permute-done | bytes 458784 | tf_op jit(solution)/shard_map/ppermute | solution.py:40
  118.8 1.3 fusion.11
  126.1 1.4 select_select_fusion
  128.9 1.3 fusion.15.xx
  130.3 11.7 %shard_map.128.refs_1_ = bf16[3584,128]{1,0:T(8,128)(2,1)} custom-call(s32[128]{0:T(128)} %select_n.174.rr, s32[128]{0:T(128)} %fusion.15.xx, s32[8]{0:T(128)} %fusion.17.order, s32[1]{0:T(128)} %bitcast.26.core, bf16[8,528,128]{2,1,0:T(8,128)(2,1)} %copy-done.11, bf16[8,528,128]{2,1,0:T(8,128)(2,1)} %copy-done.12, ...), custom_call_target="tpu_custom_call" | custom-call | tf_op jit(solution)/shard_map/pallas_call | solution.py:125
  143.3 22.1 %collective-permute-done.21.refs_2_ = bf16[3584,128]{1,0:T(8,128)(2,1)S(1)} collective-permute-done((bf16[3584,128]{1,0:T(8,128)(2,1)}, bf16[3584,128]{1,0:T(8,128)(2,1)S(1)}, u32[]{:S(2)}, u32[]{:S(2)}) %collective-permute-start.21) | collective-permute-done | bytes 917536 | tf_op jit(solution)/shard_map/ppermute | solution.py:22
  165.6 1.3 copy.162
  166.8 1.0 copy.163
  169.1 0.9 copy-done.7
  170.0 1.5 copy-done.1
  171.5 1.5 copy-done.4
  173.0 1.2 copy-done.6
  174.2 1.2 copy-done.8
  175.4 7.1 %shard_map.129 = (bf16[3584,256]{1,0:T(8,128)(2,1)}, bf16[3584,256]{1,0:T(8,128)(2,1)S(1)}) custom-call(bf16[3584,256]{1,0:T(8,128)(2,1)S(1)} %copy-done.1, bf16[3584,128]{1,0:T(8,128)(2,1)S(1)} %copy-done, bf16[3584,128]{1,0:T(8,128)(2,1)S(1)} %copy-done.6, bf16[3584,128]{1,0:T(8,128)(2,1)S(1)} %copy-done.8, ...), custom_call_target="tpu_custom_call" | custom-call | tf_op jit(solution)/shard_map/pallas_call | solution.py:181
  182.6 14.5 %collective-permute-done.25.refs_10_ = bf16[14,128,128]{2,1,0:T(8,128)(2,1)} collective-permute-done((bf16[14,128,128]{2,1,0:T(8,128)(2,1)S(1)}, bf16[14,128,128]{2,1,0:T(8,128)(2,1)}, u32[]{:S(2)}, u32[]{:S(2)}) %collective-permute-start.25) | collective-permute-done | bytes 458784 | tf_op jit(solution)/shard_map/ppermute | solution.py:34
  197.1 1.4 collective-permute-start.24
  198.5 12.5 %collective-permute-done.27.refs_12_ = bf16[14,128,128]{2,1,0:T(8,128)(2,1)} collective-permute-done((bf16[14,128,128]{2,1,0:T(8,128)(2,1)}, bf16[14,128,128]{2,1,0:T(8,128)(2,1)}, u32[]{:S(2)}, u32[]{:S(2)}) %collective-permute-start.27) | collective-permute-done | bytes 458784 | tf_op jit(solution)/shard_map/ppermute | solution.py:34
  211.1 1.4 collective-permute-start.26
  214.4 9.7 %collective-permute-done.29.refs_14_ = bf16[14,128,128]{2,1,0:T(8,128)(2,1)} collective-permute-done((bf16[14,128,128]{2,1,0:T(8,128)(2,1)}, bf16[14,128,128]{2,1,0:T(8,128)(2,1)}, u32[]{:S(2)}, u32[]{:S(2)}) %collective-permute-start.29) | collective-permute-done | bytes 458784 | tf_op jit(solution)/shard_map/ppermute | solution.py:34
  224.1 1.4 collective-permute-start.30
  226.7 8.0 %collective-permute-done.28.refs_13_ = bf16[14,128,128]{2,1,0:T(8,128)(2,1)} collective-permute-done((bf16[14,128,128]{2,1,0:T(8,128)(2,1)}, bf16[14,128,128]{2,1,0:T(8,128)(2,1)}, u32[]{:S(2)}, u32[]{:S(2)}) %collective-permute-start.28) | collective-permute-done | bytes 458784 | tf_op jit(solution)/shard_map/ppermute | solution.py:40
  234.7 7.3 %collective-permute-done.30.refs_15_ = bf16[14,128,128]{2,1,0:T(8,128)(2,1)} collective-permute-done((bf16[14,128,128]{2,1,0:T(8,128)(2,1)}, bf16[14,128,128]{2,1,0:T(8,128)(2,1)}, u32[]{:S(2)}, u32[]{:S(2)}) %collective-permute-start.30) | collective-permute-done | bytes 458784 | tf_op jit(solution)/shard_map/ppermute | solution.py:40
  242.7 1.5 collective-permute-start.42
  246.1 11.7 %shard_map.130.refs_1_ = bf16[3584,128]{1,0:T(8,128)(2,1)} custom-call(s32[128]{0:T(128)} %select_n.174.rr, s32[128]{0:T(128)} %fusion.15.xx, s32[8]{0:T(128)} %fusion.17.order, s32[1]{0:T(128)} %bitcast.26.core, bf16[8,528,128]{2,1,0:T(8,128)(2,1)} %copy-done.11, bf16[8,528,128]{2,1,0:T(8,128)(2,1)} %copy-done.12, ...), custom_call_target="tpu_custom_call" | custom-call | tf_op jit(solution)/shard_map/pallas_call | solution.py:125
  258.6 7.3 %collective-permute-done.43 = f32[192,256]{1,0:T(8,128)S(1)} collective-permute-done((f32[192,256]{1,0:T(8,128)S(1)}, f32[192,256]{1,0:T(8,128)S(1)}, u32[]{:S(2)}, u32[]{:S(2)}) %collective-permute-start.43) | collective-permute-done | bytes 196640 | tf_op jit(solution)/shard_map/ppermute | solution.py:290
  265.8 2.4 collective-permute-start.44
  268.3 9.3 %collective-permute-done.44 = f32[192,256]{1,0:T(8,128)S(1)} collective-permute-done((f32[192,256]{1,0:T(8,128)S(1)}, f32[192,256]{1,0:T(8,128)S(1)}, u32[]{:S(2)}, u32[]{:S(2)}) %collective-permute-start.44) | collective-permute-done | bytes 196640 | tf_op jit(solution)/shard_map/ppermute | solution.py:290
  277.6 1.5 collective-permute-start.45
  279.2 6.1 %collective-permute-done.45 = f32[192,256]{1,0:T(8,128)S(1)} collective-permute-done((f32[192,256]{1,0:T(8,128)S(1)}, f32[192,256]{1,0:T(8,128)S(1)}, u32[]{:S(2)}, u32[]{:S(2)}) %collective-permute-start.45) | collective-permute-done | bytes 196640 | tf_op jit(solution)/shard_map/ppermute | solution.py:22
  285.3 0.8 fusion.25
  286.8 1.0 dynamic-slice_bitcast_fusion
  287.8 0.9 collective-permute-done.46
  288.7 1.0 pad_maximum_fusion.2
  289.7 0.9 reverse_select_fusion
  290.7 2.6 gather_fusion
  293.3 1.7 slice.130
  295.0 1.9 fusion.33
  296.8 7.1 %shard_map.131 = bf16[3584,256]{1,0:T(8,128)(2,1)} custom-call(bf16[3584,256]{1,0:T(8,128)(2,1)S(1)} %get-tuple-element.8.refs_0_, bf16[3584,128]{1,0:T(8,128)(2,1)S(1)} %copy-done.3, bf16[3584,128]{1,0:T(8,128)(2,1)} %collective-permute-done.39.refs_2_, bf16[3584,128]{1,0:T(8,128)(2,1)} %collective-permute-done.40.refs_3_, ...), custom_call_target="tpu_custom_call" | custom-call | tf_op jit(solution)/shard_map/pallas_call | solution.py:193
  (177 shorter events, 34.0 us)
Async XLA Ops:
  5.1 35.4 %copy-start.11 = (bf16[8,528,128]{2,1,0:T(8,128)(2,1)}, bf16[8,528,128]{2,1,0:T(8,128)(2,1)S(1)}, u32[]{:S(2)}) copy-start(bf16[8,528,128]{2,1,0:T(8,128)(2,1)S(1)} %get-tuple-element.45.refs_0_) | copy-start | bytes 3244036
  5.1 39.9 %copy-start.28 = (s32[1,1,32]{2,1,0:T(1,128)S(1)}, s32[1,1,32]{2,1,0:T(1,128)}, u32[]{:S(2)}) copy-start(s32[1,1,32]{2,1,0:T(1,128)} %param.13) | copy-start | bytes 388
  5.1 39.9 %copy-start.29 = (s32[1,1,32]{2,1,0:T(1,128)S(1)}, s32[1,1,32]{2,1,0:T(1,128)}, u32[]{:S(2)}) copy-start(s32[1,1,32]{2,1,0:T(1,128)} %param.12) | copy-start | bytes 388
  5.1 62.6 %copy-start.27 = (s32[1,1,8]{2,1,0:T(1,128)S(1)}, s32[1,1,8]{2,1,0:T(1,128)}, u32[]{:S(2)}) copy-start(s32[1,1,8]{2,1,0:T(1,128)} %param.14) | copy-start | bytes 100
  5.1 33.9 %all-to-all-start = ((bf16[8,528,128]{2,1,0:T(8,128)(2,1)}), bf16[8,528,128]{2,1,0:T(8,128)(2,1)S(1)}, u32[]{:S(2)}, u32[]{:S(2)}) async-start(bf16[8,528,128]{2,1,0:T(8,128)(2,1)} %get-tuple-element.44), calls=%async_computation | async-start | bytes 2162688 | tf_op jit(solution)/shard_map/all_to_all | solution.py:234
  12.6 29.3 %collective-permute-start = (bf16[8,528,128]{2,1,0:T(8,128)(2,1)S(1)}, bf16[8,528,128]{2,1,0:T(8,128)(2,1)S(1)}, u32[]{:S(2)}, u32[]{:S(2)}) collective-permute-start(bf16[8,528,128]{2,1,0:T(8,128)(2,1)S(1)} %get-tuple-element.45.refs_0_), channel_id=1, source_target_pairs={{0,16},{8,24},{16,0},{24,8},{1,17},{9,25},{17,1},{25,9},{2,18},{10... | collective-permute-start | bytes 3244040 | tf_op jit(solution)/shard_map/ppermute | solution.py:22
  39.0 91.2 %copy-start.10 = (bf16[8,528,128]{2,1,0:T(8,128)(2,1)}, bf16[8,528,128]{2,1,0:T(8,128)(2,1)S(1)}, u32[]{:S(2)}) copy-start(bf16[8,528,128]{2,1,0:T(8,128)(2,1)S(1)} %all-to-all-done.refs_4_) | copy-start | bytes 3244036
  39.0 26.5 %collective-permute-start.3 = (bf16[8,528,128]{2,1,0:T(8,128)(2,1)S(1)}, bf16[8,528,128]{2,1,0:T(8,128)(2,1)}, u32[]{:S(2)}, u32[]{:S(2)}) collective-permute-start(bf16[8,528,128]{2,1,0:T(8,128)(2,1)S(1)} %all-to-all-done.refs_4_), channel_id=1, source_target_pairs={{0,16},{8,24},{16,0},{24,8},{1,17},{9,25},{17,1},{25,9},{2,18},{10... | collective-permute-start | bytes 3244040 | tf_op jit(solution)/shard_map/ppermute | solution.py:22
  40.5 33.9 %collective-permute-start.1 = (bf16[8,528,128]{2,1,0:T(8,128)(2,1)S(1)}, bf16[8,528,128]{2,1,0:T(8,128)(2,1)}, u32[]{:S(2)}, u32[]{:S(2)}) collective-permute-start(bf16[8,528,128]{2,1,0:T(8,128)(2,1)S(1)} %get-tuple-element.45.refs_0_), channel_id=1, source_target_pairs={{8,0},{24,16},{9,1},{25,17},{10,2},{26,18},{11,3},{27,19},{12,4},{... | collective-permute-start | bytes 3244040 | tf_op jit(solution)/shard_map/ppermute | solution.py:30
  41.8 88.4 %copy-start.12 = (bf16[8,528,128]{2,1,0:T(8,128)(2,1)}, bf16[8,528,128]{2,1,0:T(8,128)(2,1)S(1)}, u32[]{:S(2)}) copy-start(bf16[8,528,128]{2,1,0:T(8,128)(2,1)S(1)} %collective-permute-done.refs_1_) | copy-start | bytes 3244036
  41.8 33.1 %collective-permute-start.2 = (bf16[8,528,128]{2,1,0:T(8,128)(2,1)S(1)}, bf16[8,528,128]{2,1,0:T(8,128)(2,1)}, u32[]{:S(2)}, u32[]{:S(2)}) collective-permute-start(bf16[8,528,128]{2,1,0:T(8,128)(2,1)S(1)} %collective-permute-done.refs_1_), channel_id=1, source_target_pairs={{8,0},{24,16},{9,1},{25,17},{10,2},{26,18},{11,3},{27,19},{12,4},{... | collective-permute-start | bytes 3244040 | tf_op jit(solution)/shard_map/ppermute | solution.py:30
  45.0 13.4 %collective-permute-start.7 = (bf16[14,128,128]{2,1,0:T(8,128)(2,1)}, bf16[14,128,128]{2,1,0:T(8,128)(2,1)}, u32[]{:S(2)}, u32[]{:S(2)}) collective-permute-start(bf16[14,128,128]{2,1,0:T(8,128)(2,1)} %bitcast.27.refs_8_), channel_id=1, source_target_pairs={{0,2},{1,3},{2,4},{3,5},{4,6},{5,7},{6,0},{7,1},{8,10},{9,11},{10,... | collective-permute-start | bytes 1376264 | tf_op jit(solution)/shard_map/ppermute | solution.py:34
  58.4 14.5 %collective-permute-start.9 = (bf16[14,128,128]{2,1,0:T(8,128)(2,1)}, bf16[14,128,128]{2,1,0:T(8,128)(2,1)}, u32[]{:S(2)}, u32[]{:S(2)}) collective-permute-start(bf16[14,128,128]{2,1,0:T(8,128)(2,1)} %collective-permute-done.7.refs_10_), channel_id=1, source_target_pairs={{0,2},{1,3},{2,4},{3,5},{4,6},{5,7},{6,0},{7,1},{8,10},{9,11},{10,... | collective-permute-start | bytes 1376264 | tf_op jit(solution)/shard_map/ppermute | solution.py:34
  60.6 28.8 %collective-permute-start.4 = (bf16[8,528,128]{2,1,0:T(8,128)(2,1)S(1)}, bf16[8,528,128]{2,1,0:T(8,128)(2,1)}, u32[]{:S(2)}, u32[]{:S(2)}) collective-permute-start(bf16[8,528,128]{2,1,0:T(8,128)(2,1)S(1)} %all-to-all-done.refs_4_), channel_id=1, source_target_pairs={{0,8},{16,24},{1,9},{17,25},{2,10},{18,26},{3,11},{19,27},{4,12},{... | collective-permute-start | bytes 3244040 | tf_op jit(solution)/shard_map/ppermute | solution.py:30
  65.5 24.6 %collective-permute-start.5 = (bf16[8,528,128]{2,1,0:T(8,128)(2,1)}, bf16[8,528,128]{2,1,0:T(8,128)(2,1)}, u32[]{:S(2)}, u32[]{:S(2)}) collective-permute-start(bf16[8,528,128]{2,1,0:T(8,128)(2,1)} %collective-permute-done.3.refs_5_), channel_id=1, source_target_pairs={{0,8},{16,24},{1,9},{17,25},{2,10},{18,26},{3,11},{19,27},{4,12},{... | collective-permute-start | bytes 3244040 | tf_op jit(solution)/shard_map/ppermute | solution.py:30
  73.0 13.5 %collective-permute-start.6 = (bf16[14,128,128]{2,1,0:T(8,128)(2,1)}, bf16[14,128,128]{2,1,0:T(8,128)(2,1)}, u32[]{:S(2)}, u32[]{:S(2)}) collective-permute-start(bf16[14,128,128]{2,1,0:T(8,128)(2,1)} %bitcast.27.refs_8_), channel_id=1, source_target_pairs={{0,1},{1,0},{2,3},{3,2},{4,5},{5,4},{6,7},{7,6},{8,9},{9,8},{10,11... | collective-permute-start | bytes 1376264 | tf_op jit(solution)/shard_map/ppermute | solution.py:40
  74.4 13.5 %collective-permute-start.13 = (bf16[14,128,128]{2,1,0:T(8,128)(2,1)}, bf16[14,128,128]{2,1,0:T(8,128)(2,1)S(1)}, u32[]{:S(2)}, u32[]{:S(2)}) collective-permute-start(bf16[14,128,128]{2,1,0:T(8,128)(2,1)} %bitcast.27.refs_8_), channel_id=1, source_target_pairs={{0,8},{8,0},{16,24},{24,16},{1,9},{9,1},{17,25},{25,17},{2,10},{10... | collective-permute-start | bytes 1376264 | tf_op jit(solution)/shard_map/ppermute | solution.py:26
  74.9 14.5 %collective-permute-start.11 = (bf16[14,128,128]{2,1,0:T(8,128)(2,1)}, bf16[14,128,128]{2,1,0:T(8,128)(2,1)S(1)}, u32[]{:S(2)}, u32[]{:S(2)}) collective-permute-start(bf16[14,128,128]{2,1,0:T(8,128)(2,1)} %collective-permute-done.9.refs_12_), channel_id=1, source_target_pairs={{0,2},{1,3},{2,4},{3,5},{4,6},{5,7},{6,0},{7,1},{8,10},{9,11},{10,... | collective-permute-start | bytes 1376264 | tf_op jit(solution)/shard_map/ppermute | solution.py:34
  86.5 13.6 %collective-permute-start.8 = (bf16[14,128,128]{2,1,0:T(8,128)(2,1)}, bf16[14,128,128]{2,1,0:T(8,128)(2,1)S(1)}, u32[]{:S(2)}, u32[]{:S(2)}) collective-permute-start(bf16[14,128,128]{2,1,0:T(8,128)(2,1)} %collective-permute-done.7.refs_10_), channel_id=1, source_target_pairs={{0,1},{1,0},{2,3},{3,2},{4,5},{5,4},{6,7},{7,6},{8,9},{9,8},{10,11... | collective-permute-start | bytes 1376264 | tf_op jit(solution)/shard_map/ppermute | solution.py:40
  87.9 42.3 %copy-start.17 = (bf16[14,128,128]{2,1,0:T(8,128)(2,1)}, bf16[14,128,128]{2,1,0:T(8,128)(2,1)S(1)}, u32[]{:S(2)}) copy-start(bf16[14,128,128]{2,1,0:T(8,128)(2,1)S(1)} %collective-permute-done.13.refs_16_) | copy-start | bytes 1376260
  87.9 12.7 %collective-permute-start.15 = (bf16[14,128,128]{2,1,0:T(8,128)(2,1)}, bf16[14,128,128]{2,1,0:T(8,128)(2,1)}, u32[]{:S(2)}, u32[]{:S(2)}) collective-permute-start(bf16[14,128,128]{2,1,0:T(8,128)(2,1)} %collective-permute-done.7.refs_10_), channel_id=1, source_target_pairs={{0,8},{8,0},{16,24},{24,16},{1,9},{9,1},{17,25},{25,17},{2,10},{10... | collective-permute-start | bytes 1376264 | tf_op jit(solution)/shard_map/ppermute | solution.py:26
  89.4 40.9 %copy-start.18 = (bf16[14,128,128]{2,1,0:T(8,128)(2,1)}, bf16[14,128,128]{2,1,0:T(8,128)(2,1)S(1)}, u32[]{:S(2)}) copy-start(bf16[14,128,128]{2,1,0:T(8,128)(2,1)S(1)} %collective-permute-done.11.refs_14_) | copy-start | bytes 1376260
  89.4 10.7 %collective-permute-start.14 = (bf16[14,128,128]{2,1,0:T(8,128)(2,1)}, bf16[14,128,128]{2,1,0:T(8,128)(2,1)}, u32[]{:S(2)}, u32[]{:S(2)}) collective-permute-start(bf16[14,128,128]{2,1,0:T(8,128)(2,1)} %collective-permute-done.6.refs_9_), channel_id=1, source_target_pairs={{0,8},{8,0},{16,24},{24,16},{1,9},{9,1},{17,25},{25,17},{2,10},{10... | collective-permute-start | bytes 1376264 | tf_op jit(solution)/shard_map/ppermute | solution.py:26
  89.4 20.6 %collective-permute-start.10 = (bf16[14,128,128]{2,1,0:T(8,128)(2,1)}, bf16[14,128,128]{2,1,0:T(8,128)(2,1)}, u32[]{:S(2)}, u32[]{:S(2)}) collective-permute-start(bf16[14,128,128]{2,1,0:T(8,128)(2,1)} %collective-permute-done.9.refs_12_), channel_id=1, source_target_pairs={{0,1},{1,0},{2,3},{3,2},{4,5},{5,4},{6,7},{7,6},{8,9},{9,8},{10,11... | collective-permute-start | bytes 1376264 | tf_op jit(solution)/shard_map/ppermute | solution.py:40
  90.1 28.7 %collective-permute-start.12 = (bf16[14,128,128]{2,1,0:T(8,128)(2,1)S(1)}, bf16[14,128,128]{2,1,0:T(8,128)(2,1)}, u32[]{:S(2)}, u32[]{:S(2)}) collective-permute-start(bf16[14,128,128]{2,1,0:T(8,128)(2,1)S(1)} %collective-permute-done.11.refs_14_), channel_id=1, source_target_pairs={{0,1},{1,0},{2,3},{3,2},{4,5},{5,4},{6,7},{7,6},{8,9},{9,8},{10,11... | collective-permute-start | bytes 1376264 | tf_op jit(solution)/shard_map/ppermute | solution.py:40
  100.0 20.2 %copy-start.26 = (bf16[8,1,4]{0,2,1:T(4,128)(2,1)}, bf16[8,1,4]{0,2,1:T(4,128)(2,1)S(1)}, u32[]{:S(2)}) copy-start(bf16[8,1,4]{0,2,1:T(4,128)(2,1)S(1)} %copy.158) | copy-start | bytes 196
  100.1 30.2 %copy-start.19 = (bf16[14,128,128]{2,1,0:T(8,128)(2,1)}, bf16[14,128,128]{2,1,0:T(8,128)(2,1)S(1)}, u32[]{:S(2)}) copy-start(bf16[14,128,128]{2,1,0:T(8,128)(2,1)S(1)} %collective-permute-done.8.refs_11_) | copy-start | bytes 1376260
  100.1 30.1 %collective-permute-start.17 = (bf16[14,128,128]{2,1,0:T(8,128)(2,1)}, bf16[14,128,128]{2,1,0:T(8,128)(2,1)}, u32[]{:S(2)}, u32[]{:S(2)}) collective-permute-start(bf16[14,128,128]{2,1,0:T(8,128)(2,1)} %collective-permute-done.9.refs_12_), channel_id=1, source_target_pairs={{0,8},{8,0},{16,24},{24,16},{1,9},{9,1},{17,25},{25,17},{2,10},{10... | collective-permute-start | bytes 1376264 | tf_op jit(solution)/shard_map/ppermute | solution.py:26
  100.1 30.1 %collective-permute-start.16 = (bf16[14,128,128]{2,1,0:T(8,128)(2,1)S(1)}, bf16[14,128,128]{2,1,0:T(8,128)(2,1)}, u32[]{:S(2)}, u32[]{:S(2)}) collective-permute-start(bf16[14,128,128]{2,1,0:T(8,128)(2,1)S(1)} %collective-permute-done.8.refs_11_), channel_id=1, source_target_pairs={{0,8},{8,0},{16,24},{24,16},{1,9},{9,1},{17,25},{25,17},{2,10},{10... | collective-permute-start | bytes 1376264 | tf_op jit(solution)/shard_map/ppermute | solution.py:26
  100.6 29.6 %collective-permute-start.19 = (bf16[14,128,128]{2,1,0:T(8,128)(2,1)S(1)}, bf16[14,128,128]{2,1,0:T(8,128)(2,1)}, u32[]{:S(2)}, u32[]{:S(2)}) collective-permute-start(bf16[14,128,128]{2,1,0:T(8,128)(2,1)S(1)} %collective-permute-done.11.refs_14_), channel_id=1, source_target_pairs={{0,8},{8,0},{16,24},{24,16},{1,9},{9,1},{17,25},{25,17},{2,10},{10... | collective-permute-start | bytes 1376264 | tf_op jit(solution)/shard_map/ppermute | solution.py:26
  110.1 20.2 %collective-permute-start.18 = (bf16[14,128,128]{2,1,0:T(8,128)(2,1)}, bf16[14,128,128]{2,1,0:T(8,128)(2,1)}, u32[]{:S(2)}, u32[]{:S(2)}) collective-permute-start(bf16[14,128,128]{2,1,0:T(8,128)(2,1)} %collective-permute-done.10.refs_13_), channel_id=1, source_target_pairs={{0,8},{8,0},{16,24},{24,16},{1,9},{9,1},{17,25},{25,17},{2,10},{10... | collective-permute-start | bytes 1376264 | tf_op jit(solution)/shard_map/ppermute | solution.py:26
  118.8 11.4 %collective-permute-start.20 = (bf16[14,128,128]{2,1,0:T(8,128)(2,1)}, bf16[14,128,128]{2,1,0:T(8,128)(2,1)}, u32[]{:S(2)}, u32[]{:S(2)}) collective-permute-start(bf16[14,128,128]{2,1,0:T(8,128)(2,1)} %collective-permute-done.12.refs_15_), channel_id=1, source_target_pairs={{0,8},{8,0},{16,24},{24,16},{1,9},{9,1},{17,25},{25,17},{2,10},{10... | collective-permute-start | bytes 1376264 | tf_op jit(solution)/shard_map/ppermute | solution.py:26
  142.0 23.4 %collective-permute-start.21 = (bf16[3584,128]{1,0:T(8,128)(2,1)}, bf16[3584,128]{1,0:T(8,128)(2,1)S(1)}, u32[]{:S(2)}, u32[]{:S(2)}) collective-permute-start(bf16[3584,128]{1,0:T(8,128)(2,1)} %shard_map.128.refs_1_), channel_id=1, source_target_pairs={{0,16},{8,24},{16,0},{24,8},{1,17},{9,25},{17,1},{25,9},{2,18},{10... | collective-permute-start | bytes 2752520 | tf_op jit(solution)/shard_map/ppermute | solution.py:22
  142.6 26.4 %collective-permute-start.22 = (bf16[3584,128]{1,0:T(8,128)(2,1)}, bf16[3584,128]{1,0:T(8,128)(2,1)S(1)}, u32[]{:S(2)}, u32[]{:S(2)}) collective-permute-start(bf16[3584,128]{1,0:T(8,128)(2,1)} %shard_map.128.refs_1_), channel_id=1, source_target_pairs={{0,8},{8,0},{16,24},{24,16},{1,9},{9,1},{17,25},{25,17},{2,10},{10... | collective-permute-start | bytes 2752520 | tf_op jit(solution)/shard_map/ppermute | solution.py:26
  165.4 3.6 %copy-start.5 = (bf16[3584,128]{1,0:T(8,128)(2,1)}, bf16[3584,128]{1,0:T(8,128)(2,1)S(1)}, u32[]{:S(2)}) copy-start(bf16[3584,128]{1,0:T(8,128)(2,1)S(1)} %collective-permute-done.21.refs_2_) | copy-start | bytes 2752516
  165.4 4.6 %collective-permute-start.23 = (bf16[3584,128]{1,0:T(8,128)(2,1)S(1)}, bf16[3584,128]{1,0:T(8,128)(2,1)}, u32[]{:S(2)}, u32[]{:S(2)}) collective-permute-start(bf16[3584,128]{1,0:T(8,128)(2,1)S(1)} %collective-permute-done.21.refs_2_), channel_id=1, source_target_pairs={{0,8},{8,0},{16,24},{24,16},{1,9},{9,1},{17,25},{25,17},{2,10},{10... | collective-permute-start | bytes 2752520 | tf_op jit(solution)/shard_map/ppermute | solution.py:26
  165.6 4.4 %copy-start = (bf16[3584,128]{1,0:T(8,128)(2,1)S(1)}, bf16[3584,128]{1,0:T(8,128)(2,1)}, u32[]{:S(2)}) copy-start(bf16[3584,128]{1,0:T(8,128)(2,1)} %shard_map.128.refs_1_) | copy-start | bytes 2752516
  165.6 4.4 %copy-start.9 = (bf16[256,256]{1,0:T(8,128)(2,1)S(1)}, bf16[256,256]{1,0:T(8,128)(2,1)}, u32[]{:S(2)}) copy-start(bf16[256,256]{1,0:T(8,128)(2,1)} %refs_6_.1) | copy-start | bytes 393220
  182.5 43.5 %copy-start.14 = (bf16[1792,128]{1,0:T(8,128)(2,1)}, bf16[1792,128]{1,0:T(8,128)(2,1)S(1)}, u32[]{:S(2)}) copy-start(bf16[1792,128]{1,0:T(8,128)(2,1)S(1)} %dynamic_slice.38) | copy-start | bytes 1376260
  182.5 14.6 %collective-permute-start.25 = (bf16[14,128,128]{2,1,0:T(8,128)(2,1)S(1)}, bf16[14,128,128]{2,1,0:T(8,128)(2,1)}, u32[]{:S(2)}, u32[]{:S(2)}) collective-permute-start(bf16[14,128,128]{2,1,0:T(8,128)(2,1)S(1)} %bitcast.65), channel_id=1, source_target_pairs={{0,2},{1,3},{2,4},{3,5},{4,6},{5,7},{6,0},{7,1},{8,10},{9,11},{10,... | collective-permute-start | bytes 1376264 | tf_op jit(solution)/shard_map/ppermute | solution.py:34
  197.1 14.0 %collective-permute-start.27 = (bf16[14,128,128]{2,1,0:T(8,128)(2,1)}, bf16[14,128,128]{2,1,0:T(8,128)(2,1)}, u32[]{:S(2)}, u32[]{:S(2)}) collective-permute-start(bf16[14,128,128]{2,1,0:T(8,128)(2,1)} %collective-permute-done.25.refs_10_), channel_id=1, source_target_pairs={{0,2},{1,3},{2,4},{3,5},{4,6},{5,7},{6,0},{7,1},{8,10},{9,11},{10,... | collective-permute-start | bytes 1376264 | tf_op jit(solution)/shard_map/ppermute | solution.py:34
  197.1 15.4 %collective-permute-start.24 = (bf16[14,128,128]{2,1,0:T(8,128)(2,1)S(1)}, bf16[14,128,128]{2,1,0:T(8,128)(2,1)}, u32[]{:S(2)}, u32[]{:S(2)}) collective-permute-start(bf16[14,128,128]{2,1,0:T(8,128)(2,1)S(1)} %bitcast.66), channel_id=1, source_target_pairs={{0,1},{1,0},{2,3},{3,2},{4,5},{5,4},{6,7},{7,6},{8,9},{9,8},{10,11... | collective-permute-start | bytes 1376264 | tf_op jit(solution)/shard_map/ppermute | solution.py:40
  198.5 14.5 %collective-permute-start.31 = (bf16[14,128,128]{2,1,0:T(8,128)(2,1)S(1)}, bf16[14,128,128]{2,1,0:T(8,128)(2,1)S(1)}, u32[]{:S(2)}, u32[]{:S(2)}) collective-permute-start(bf16[14,128,128]{2,1,0:T(8,128)(2,1)S(1)} %bitcast.67), channel_id=1, source_target_pairs={{0,8},{8,0},{16,24},{24,16},{1,9},{9,1},{17,25},{25,17},{2,10},{10... | collective-permute-start | bytes 1376264 | tf_op jit(solution)/shard_map/ppermute | solution.py:26
  211.1 13.0 %collective-permute-start.29 = (bf16[14,128,128]{2,1,0:T(8,128)(2,1)}, bf16[14,128,128]{2,1,0:T(8,128)(2,1)}, u32[]{:S(2)}, u32[]{:S(2)}) collective-permute-start(bf16[14,128,128]{2,1,0:T(8,128)(2,1)} %collective-permute-done.27.refs_12_), channel_id=1, source_target_pairs={{0,2},{1,3},{2,4},{3,5},{4,6},{5,7},{6,0},{7,1},{8,10},{9,11},{10,... | collective-permute-start | bytes 1376264 | tf_op jit(solution)/shard_map/ppermute | solution.py:34
  211.1 14.5 %collective-permute-start.26 = (bf16[14,128,128]{2,1,0:T(8,128)(2,1)}, bf16[14,128,128]{2,1,0:T(8,128)(2,1)}, u32[]{:S(2)}, u32[]{:S(2)}) collective-permute-start(bf16[14,128,128]{2,1,0:T(8,128)(2,1)} %collective-permute-done.25.refs_10_), channel_id=1, source_target_pairs={{0,1},{1,0},{2,3},{3,2},{4,5},{5,4},{6,7},{7,6},{8,9},{9,8},{10,11... | collective-permute-start | bytes 1376264 | tf_op jit(solution)/shard_map/ppermute | solution.py:40
  212.5 13.5 %collective-permute-start.32 = (bf16[14,128,128]{2,1,0:T(8,128)(2,1)}, bf16[14,128,128]{2,1,0:T(8,128)(2,1)}, u32[]{:S(2)}, u32[]{:S(2)}) collective-permute-start(bf16[14,128,128]{2,1,0:T(8,128)(2,1)} %collective-permute-done.24.refs_9_), channel_id=1, source_target_pairs={{0,8},{8,0},{16,24},{24,16},{1,9},{9,1},{17,25},{25,17},{2,10},{10... | collective-permute-start | bytes 1376264 | tf_op jit(solution)/shard_map/ppermute | solution.py:26
  212.5 14.1 %collective-permute-start.33 = (bf16[14,128,128]{2,1,0:T(8,128)(2,1)}, bf16[14,128,128]{2,1,0:T(8,128)(2,1)}, u32[]{:S(2)}, u32[]{:S(2)}) collective-permute-start(bf16[14,128,128]{2,1,0:T(8,128)(2,1)} %collective-permute-done.25.refs_10_), channel_id=1, source_target_pairs={{0,8},{8,0},{16,24},{24,16},{1,9},{9,1},{17,25},{25,17},{2,10},{10... | collective-permute-start | bytes 1376264 | tf_op jit(solution)/shard_map/ppermute | solution.py:26
  213.8 20.9 %collective-permute-start.28 = (bf16[14,128,128]{2,1,0:T(8,128)(2,1)}, bf16[14,128,128]{2,1,0:T(8,128)(2,1)}, u32[]{:S(2)}, u32[]{:S(2)}) collective-permute-start(bf16[14,128,128]{2,1,0:T(8,128)(2,1)} %collective-permute-done.27.refs_12_), channel_id=1, source_target_pairs={{0,1},{1,0},{2,3},{3,2},{4,5},{5,4},{6,7},{7,6},{8,9},{9,8},{10,11... | collective-permute-start | bytes 1376264 | tf_op jit(solution)/shard_map/ppermute | solution.py:40
  224.1 17.9 %collective-permute-start.30 = (bf16[14,128,128]{2,1,0:T(8,128)(2,1)}, bf16[14,128,128]{2,1,0:T(8,128)(2,1)}, u32[]{:S(2)}, u32[]{:S(2)}) collective-permute-start(bf16[14,128,128]{2,1,0:T(8,128)(2,1)} %collective-permute-done.29.refs_14_), channel_id=1, source_target_pairs={{0,1},{1,0},{2,3},{3,2},{4,5},{5,4},{6,7},{7,6},{8,9},{9,8},{10,11... | collective-permute-start | bytes 1376264 | tf_op jit(solution)/shard_map/ppermute | solution.py:40
  225.5 16.5 %copy-start.2 = (bf16[3584,256]{1,0:T(8,128)(2,1)S(1)}, bf16[3584,256]{1,0:T(8,128)(2,1)}, u32[]{:S(2)}) copy-start(bf16[3584,256]{1,0:T(8,128)(2,1)} %refs_0_.1) | copy-start | bytes 5505028
  225.5 17.2 %collective-permute-start.34 = (bf16[14,128,128]{2,1,0:T(8,128)(2,1)}, bf16[14,128,128]{2,1,0:T(8,128)(2,1)S(1)}, u32[]{:S(2)}, u32[]{:S(2)}) collective-permute-start(bf16[14,128,128]{2,1,0:T(8,128)(2,1)} %collective-permute-done.26.refs_11_), channel_id=1, source_target_pairs={{0,8},{8,0},{16,24},{24,16},{1,9},{9,1},{17,25},{25,17},{2,10},{10... | collective-permute-start | bytes 1376264 | tf_op jit(solution)/shard_map/ppermute | solution.py:26
  226.0 18.2 %collective-permute-start.35 = (bf16[14,128,128]{2,1,0:T(8,128)(2,1)}, bf16[14,128,128]{2,1,0:T(8,128)(2,1)S(1)}, u32[]{:S(2)}, u32[]{:S(2)}) collective-permute-start(bf16[14,128,128]{2,1,0:T(8,128)(2,1)} %collective-permute-done.27.refs_12_), channel_id=1, source_target_pairs={{0,8},{8,0},{16,24},{24,16},{1,9},{9,1},{17,25},{25,17},{2,10},{10... | collective-permute-start | bytes 1376264 | tf_op jit(solution)/shard_map/ppermute | solution.py:26
  226.6 17.7 %collective-permute-start.37 = (bf16[14,128,128]{2,1,0:T(8,128)(2,1)}, bf16[14,128,128]{2,1,0:T(8,128)(2,1)S(1)}, u32[]{:S(2)}, u32[]{:S(2)}) collective-permute-start(bf16[14,128,128]{2,1,0:T(8,128)(2,1)} %collective-permute-done.29.refs_14_), channel_id=1, source_target_pairs={{0,8},{8,0},{16,24},{24,16},{1,9},{9,1},{17,25},{25,17},{2,10},{10... | collective-permute-start | bytes 1376264 | tf_op jit(solution)/shard_map/ppermute | solution.py:26
  234.7 9.6 %collective-permute-start.36 = (bf16[14,128,128]{2,1,0:T(8,128)(2,1)}, bf16[14,128,128]{2,1,0:T(8,128)(2,1)S(1)}, u32[]{:S(2)}, u32[]{:S(2)}) collective-permute-start(bf16[14,128,128]{2,1,0:T(8,128)(2,1)} %collective-permute-done.28.refs_13_), channel_id=1, source_target_pairs={{0,8},{8,0},{16,24},{24,16},{1,9},{9,1},{17,25},{25,17},{2,10},{10... | collective-permute-start | bytes 1376264 | tf_op jit(solution)/shard_map/ppermute | solution.py:26
  242.0 2.3 collective-permute-start.38
  242.7 15.7 %collective-permute-start.42 = (f32[192,256]{1,0:T(8,128)S(1)}, f32[192,256]{1,0:T(8,128)S(1)}, u32[]{:S(2)}, u32[]{:S(2)}) collective-permute-start(f32[192,256]{1,0:T(8,128)S(1)} %pad_maximum_fusion.4), channel_id=1, source_target_pairs={{0,1},{1,0},{2,3},{3,2},{4,5},{5,4},{6,7},{7,6},{8,9},{9,8},{10,11... | collective-permute-start | bytes 589832 | tf_op jit(solution)/shard_map/ppermute | solution.py:290
  257.8 28.8 %collective-permute-start.39 = (bf16[3584,128]{1,0:T(8,128)(2,1)}, bf16[3584,128]{1,0:T(8,128)(2,1)}, u32[]{:S(2)}, u32[]{:S(2)}) collective-permute-start(bf16[3584,128]{1,0:T(8,128)(2,1)} %shard_map.130.refs_1_), channel_id=1, source_target_pairs={{0,16},{8,24},{16,0},{24,8},{1,17},{9,25},{17,1},{25,9},{2,18},{10... | collective-permute-start | bytes 2752520 | tf_op jit(solution)/shard_map/ppermute | solution.py:22
  258.5 27.7 %copy-start.3 = (bf16[3584,128]{1,0:T(8,128)(2,1)S(1)}, bf16[3584,128]{1,0:T(8,128)(2,1)}, u32[]{:S(2)}) copy-start(bf16[3584,128]{1,0:T(8,128)(2,1)} %shard_map.130.refs_1_) | copy-start | bytes 2752516
  258.5 7.3 %collective-permute-start.43 = (f32[192,256]{1,0:T(8,128)S(1)}, f32[192,256]{1,0:T(8,128)S(1)}, u32[]{:S(2)}, u32[]{:S(2)}) collective-permute-start(f32[192,256]{1,0:T(8,128)S(1)} %fusion.24), channel_id=1, source_target_pairs={{0,2},{1,3},{2,0},{3,1},{4,6},{5,7},{6,4},{7,5},{8,10},{9,11},{10,... | collective-permute-start | bytes 589832 | tf_op jit(solution)/shard_map/ppermute | solution.py:290
  265.8 11.8 %collective-permute-start.44 = (f32[192,256]{1,0:T(8,128)S(1)}, f32[192,256]{1,0:T(8,128)S(1)}, u32[]{:S(2)}, u32[]{:S(2)}) collective-permute-start(f32[192,256]{1,0:T(8,128)S(1)} %add.122), channel_id=1, source_target_pairs={{0,4},{1,5},{2,6},{3,7},{4,0},{5,1},{6,2},{7,3},{8,12},{9,13},{10,... | collective-permute-start | bytes 589832 | tf_op jit(solution)/shard_map/ppermute | solution.py:290
  277.6 7.7 %collective-permute-start.45 = (f32[192,256]{1,0:T(8,128)S(1)}, f32[192,256]{1,0:T(8,128)S(1)}, u32[]{:S(2)}, u32[]{:S(2)}) collective-permute-start(f32[192,256]{1,0:T(8,128)S(1)} %add.123), channel_id=1, source_target_pairs={{0,16},{8,24},{16,0},{24,8},{1,17},{9,25},{17,1},{25,9},{2,18},{10... | collective-permute-start | bytes 589832 | tf_op jit(solution)/shard_map/ppermute | solution.py:22
  286.1 2.6 collective-permute-start.46
  286.1 10.7 %collective-permute-start.40 = (bf16[3584,128]{1,0:T(8,128)(2,1)S(1)}, bf16[3584,128]{1,0:T(8,128)(2,1)}, u32[]{:S(2)}, u32[]{:S(2)}) collective-permute-start(bf16[3584,128]{1,0:T(8,128)(2,1)S(1)} %copy-done.3), channel_id=1, source_target_pairs={{0,8},{8,0},{16,24},{24,16},{1,9},{9,1},{17,25},{25,17},{2,10},{10... | collective-permute-start | bytes 2752520 | tf_op jit(solution)/shard_map/ppermute | solution.py:26
  286.6 10.2 %collective-permute-start.41 = (bf16[3584,128]{1,0:T(8,128)(2,1)}, bf16[3584,128]{1,0:T(8,128)(2,1)}, u32[]{:S(2)}, u32[]{:S(2)}) collective-permute-start(bf16[3584,128]{1,0:T(8,128)(2,1)} %collective-permute-done.39.refs_2_), channel_id=1, source_target_pairs={{0,8},{8,0},{16,24},{24,16},{1,9},{9,1},{17,25},{25,17},{2,10},{10... | collective-permute-start | bytes 2752520 | tf_op jit(solution)/shard_map/ppermute | solution.py:26
  (14 other events, 16.1 us)

commit v2 on v1

v2 whole, which is shorter than its diff:
```python
import functools

import jax
import jax.numpy as jnp
from jax import lax
from jax.experimental import pallas as pl
from jax.experimental.pallas import tpu as pltpu
from jax.sharding import PartitionSpec as P

BF = jnp.bfloat16
F32 = jnp.float32
META = 16
CORES = 2


def dims(wide, narrow):
    z = 4 if narrow % 4 == 0 else 1
    return wide // CORES, z, narrow // z


def x_shift(a, k, wide):
    return lax.ppermute(a, "wide", [(i, (i + CORES * k) % wide) for i in range(wide)])


def core_swap(a, wide):
    return lax.ppermute(a, "wide", [(i, i ^ 1) for i in range(wide)])


def to_core(a, source, target, k, wide):
    return lax.ppermute(
        a,
        "wide",
        [(i, ((i // CORES + k) * CORES + target) % wide) for i in range(source, wide, CORES)],
    )


def z_shift(a, k, zs, ys):
    return lax.ppermute(
        a, "narrow", [(z * ys + y, (z + k) % zs * ys + y) for z in range(zs) for y in range(ys)]
    )


def y_shift(a, k, zs, ys):
    return lax.ppermute(
        a, "narrow", [(z * ys + y, z * ys + (y + k) % ys) for z in range(zs) for y in range(ys)]
    )


def after(a, *others):
    return lax.optimization_barrier((a,) + others)[0]


def aggregate_kernel(wide, cap, side, blocks, qs, layout, last, scal, *refs):
    half = blocks // CORES
    refs = list(refs)
    row_sets = [refs.pop(0) for _ in range(wide)]
    col_sets = [[refs.pop(0) for _ in part] for part in layout["cols"]]
    mine = [[refs.pop(0) for _ in range(layout["split"][q])] for q in qs]
    other = [[refs.pop(0) for _ in range(layout["split"][q])] for q in qs]
    acc_in = refs.pop(0) if layout["carry"] else None
    out_ref, tiles, feats, acc, facts_v, facts_s, tile_sem, feat_sem, sem = refs
    narrow = layout["narrow"]

    if acc_in is not None:
        carried = pltpu.make_async_copy(acc_in, acc, sem.at[0])
        carried.start()

    def row_copy(n, w):
        return pltpu.make_async_copy(
            row_sets[w].at[scal[1 + qs[n]]], tiles.at[n * wide + w], tile_sem.at[n * wide + w]
        )

    def col_copy(n, w):
        part, start = layout["where"][qs[n]]
        return pltpu.make_async_copy(
            col_sets[w][part].at[qs[n] - start],
            tiles.at[n * wide + w],
            tile_sem.at[n * wide + w],
        )

    @pl.when(scal[0] == 0)
    def _():
        for n in range(len(qs)):
            for w in range(wide):
                row_copy(n, w).start()

    @pl.when(scal[0] != 0)
    def _():
        for n in range(len(qs)):
            for w in range(wide):
                col_copy(n, w).start()

    copies = []
    for n in range(len(qs)):
        here = []
        for h, group in enumerate((mine[n], other[n])):
            size = half // len(group)
            for e, source in enumerate(group):
                copy = pltpu.make_async_copy(
                    source,
                    feats.at[pl.ds(n * blocks + h * half + e * size, size)],
                    feat_sem.at[(n * CORES + h) * 2 + e],
                )
                copy.start()
                here.append(copy)
        copies.append(here)
    if acc_in is None:
        acc[...] = jnp.zeros_like(acc)
    for n in range(len(qs)):
        for w in range(wide):
            row_copy(n, w).wait()
    core = scal[0]
    facts = tiles[:, cap * side : cap * side + META, :].astype(F32)
    row = facts[:, 0, :].astype(jnp.int32)
    source = facts[:, 1, :].astype(jnp.int32)
    alive = facts[:, 2, :] > 0.5
    to_block = jnp.where(core == 0, row, source)
    from_block = jnp.where(core == 0, source, row)
    upper = (from_block >= half).astype(jnp.int32)
    facts_v[0] = jnp.where(alive, to_block, blocks)
    facts_v[1] = from_block - upper * half + jnp.where(upper == core, 0, half)
    scalars = pltpu.make_async_copy(facts_v, facts_s, sem.at[1])
    scalars.start()
    scalars.wait()
    if acc_in is not None:
        carried.wait()
    for n in range(len(qs)):
        for copy in copies[n]:
            copy.wait()
        for w in range(wide):
            t = n * wide + w
            terms = []
            for i in range(cap):
                terms.append(
                    jnp.dot(
                        tiles[t, i * side : (i + 1) * side, :],
                        feats[n * blocks + facts_s[1, t, i]],
                        preferred_element_type=F32,
                    )
                )
            for i in range(cap):
                to = facts_s[0, t, i]
                acc[to] = acc[to] + terms[i]
    if last:
        for b in range(blocks):
            out_ref[b * side : (b + 1) * side, :] = acc[b].astype(BF)
    else:
        out_ref[...] = acc[...]


def aggregate(scal, row_sets, col_sets, where, mine, other, qs, carry, last, blocks, side, cap):
    wide = len(row_sets)
    width = mine[qs[0]][0].shape[-1]
    narrow = row_sets[0].shape[0]
    layout = dict(
        cols=[[0] * len(c) for c in col_sets],
        where=where,
        split={q: len(mine[q]) for q in qs},
        carry=carry is not None,
        narrow=narrow,
    )
    operands = list(row_sets) + [a for c in col_sets for a in c]
    operands += [a for q in qs for a in mine[q]] + [a for q in qs for a in other[q]]
    if carry is not None:
        operands.append(carry)
    count = len(qs) * wide
    if last:
        shape = jax.ShapeDtypeStruct((blocks * side, width), BF)
    else:
        shape = jax.ShapeDtypeStruct((blocks + 1, side, width), F32)
    flops = 2 * count * cap * side * side * width
    return pl.pallas_call(
        functools.partial(aggregate_kernel, wide, cap, side, blocks, qs, layout, last),
        out_shape=shape,
        in_specs=[pl.BlockSpec(memory_space=pltpu.SMEM)]
        + [pl.BlockSpec(memory_space=pl.ANY)] * len(operands),
        out_specs=pl.BlockSpec(memory_space=pltpu.VMEM),
        scratch_shapes=[
            pltpu.VMEM((count,) + row_sets[0].shape[1:], BF),
            pltpu.VMEM((len(qs) * blocks, side, width), BF),
            pltpu.VMEM((blocks + 1, side, width), F32),
            pltpu.VMEM((2, count, side), jnp.int32),
            pltpu.SMEM((2, count, side), jnp.int32),
            pltpu.SemaphoreType.DMA((count,)),
            pltpu.SemaphoreType.DMA((len(qs) * CORES * 2,)),
            pltpu.SemaphoreType.DMA((2,)),
        ],
        compiler_params=pltpu.CompilerParams(vmem_limit_bytes=58 << 20),
        cost_estimate=pl.CostEstimate(
            flops=flops, bytes_accessed=count * cap * side * side * 6, transcendentals=0
        ),
    )(scal, *operands)


def joined_dot(parts, weight):
    return jnp.dot(
        jnp.concatenate([r[...] for r in parts], axis=1), weight[...], preferred_element_type=F32
    )


def layer_kernel(parts, *refs):
    ins = refs[:parts]
    cotangent, weight, hidden_ref, grad_ref = refs[parts:]
    pre = joined_dot(ins, weight)
    sigma = 1.0 / (1.0 + jnp.exp(-pre))
    hidden_ref[...] = (pre * sigma).astype(BF)
    grad_ref[...] = (cotangent[...].astype(F32) * sigma * (1.0 + pre * (1.0 - sigma))).astype(BF)


def final_kernel(parts, *refs):
    ins = refs[:parts]
    weight, out_ref = refs[parts:]
    out_ref[...] = joined_dot(ins, weight).astype(BF)


def row_specs(arrays, step):
    return [pl.BlockSpec((step, a.shape[1]), lambda i: (i, 0)) for a in arrays]


def layer(ins, cotangent, weight, step):
    rows, width = cotangent.shape
    shape = jax.ShapeDtypeStruct((rows, width), BF)
    return pl.pallas_call(
        functools.partial(layer_kernel, len(ins)),
        grid=(rows // step,),
        out_shape=(shape, shape),
        in_specs=row_specs(list(ins) + [cotangent], step)
        + [pl.BlockSpec(weight.shape, lambda i: (0, 0))],
        out_specs=tuple(row_specs([cotangent, cotangent], step)),
        compiler_params=pltpu.CompilerParams(vmem_limit_bytes=58 << 20),
    )(*ins, cotangent, weight)


def final(ins, weight, step):
    rows, width = ins[0].shape[0], weight.shape[1]
    return pl.pallas_call(
        functools.partial(final_kernel, len(ins)),
        grid=(rows // step,),
        out_shape=jax.ShapeDtypeStruct((rows, width), BF),
        in_specs=row_specs(ins, step) + [pl.BlockSpec(weight.shape, lambda i: (0, 0))],
        out_specs=pl.BlockSpec((step, width), lambda i: (i, 0)),
        compiler_params=pltpu.CompilerParams(vmem_limit_bytes=58 << 20),
    )(*ins, weight)


def body(node_feats, grad_out, tile_weight, tile_row, src_block, tile_count, w_self, w_out, w_in):
    wide, narrow = lax.axis_size("wide"), lax.axis_size("narrow")
    xs, zs, ys = dims(wide, narrow)
    slots = tile_row.shape[-1]
    cap = slots // narrow
    nodes, width = node_feats.shape
    side = tile_weight.shape[-1]
    blocks = nodes // side
    half = blocks // CORES
    cols = width // xs
    step = nodes // 7
    w_id, n_id = lax.axis_index("wide"), lax.axis_index("narrow")
    core, x_id = w_id % CORES, w_id // CORES
    z_id, y_id = n_id // ys, n_id % ys
    first = core == 0
    every = [(k, j) for k in range(zs) for j in range(ys)]

    def own_piece(a):
        piece = lax.dynamic_slice(a, (core * half * side, x_id * cols), (half * side, cols))
        return piece.reshape(half, side, cols)

    tiles = tile_weight.reshape(narrow, cap, side, side)
    live = jnp.arange(cap, dtype=jnp.int32)[None, :] < tile_count.reshape(narrow, 1)
    facts = jnp.stack(
        [
            tile_row.reshape(narrow, cap).astype(BF),
            src_block.reshape(narrow, cap).astype(BF),
            live.astype(BF),
        ],
        axis=1,
    )
    facts = jnp.pad(facts, ((0, 0), (0, META - 3), (0, side - cap)))

    def packed(t):
        return jnp.concatenate([t.reshape(narrow, cap * side, side), facts], axis=1)

    row_own = packed(tiles)
    col_by_owner = packed(tiles.swapaxes(2, 3)).reshape(zs, ys, cap * side + META, side)
    q = jnp.arange(narrow, dtype=jnp.int32)
    order = (z_id - q // ys) % zs * ys + (y_id - q % ys) % ys
    scal = jnp.concatenate([core.reshape(1), order]).astype(jnp.int32)

    feats = {(0, 0): own_piece(node_feats)}
    toward = [
        lax.dynamic_index_in_dim(col_by_owner, (y_id + j) % ys, 1, keepdims=False)
        for j in range(ys)
    ]
    moved = [toward[0]] + [y_shift(toward[j], j, zs, ys) for j in range(1, ys)]
    row_sets = [row_own, to_core(row_own, 1, 0, 0, wide)]
    for k in range(1, xs):
        row_sets += [to_core(row_own, c, 0, k, wide) for c in range(CORES)]
    feats[1, 0] = z_shift(feats[0, 0], 1, zs, ys)
    feats[0, 1] = y_shift(after(feats[0, 0], *moved[1:]), 1, zs, ys)
    col_by_z = jnp.stack(moved, axis=1)

    def col_shift(k, *ahead):
        part = lax.dynamic_index_in_dim(col_by_z, (z_id + k) % zs, 0, keepdims=False)
        return z_shift(after(part, *ahead), k, zs, ys) if k else part

    col_parts = [col_shift(0), col_shift(1)]
    feats[2, 0] = z_shift(after(feats[1, 0]), 1, zs, ys)
    feats[1, 1] = y_shift(after(feats[1, 0], feats[0, 1]), 1, zs, ys)
    col_parts.append(col_shift(2, feats[2, 0]))
    feats[3, 0] = z_shift(after(feats[2, 0], col_parts[1]), 1, zs, ys)
    feats[2, 1] = y_shift(after(feats[2, 0], feats[1, 1]), 1, zs, ys)
    col_parts.append(col_shift(3, col_parts[2]))
    feats[3, 1] = y_shift(after(feats[3, 0], feats[2, 1]), 1, zs, ys)
    for k in range(zs):
        for j in range(2, ys):
            feats[k, j] = y_shift(feats[k, j - 1], 1, zs, ys)
    early_cols = jnp.concatenate(col_parts[:3], axis=0)
    late_cols = col_parts[3]

    def col_sources(a):
        sets = [a, to_core(a, 0, 1, 0, wide)]
        for k in range(1, xs):
            sets += [to_core(a, c, 1, k, wide) for c in range(CORES)]
        return sets

    col_sets = [list(pair) for pair in zip(col_sources(early_cols), col_sources(late_cols))]
    cut = 3 * ys
    where = {i: (0, 0) if i < cut else (1, cut) for i in range(narrow)}

    def spread(pieces):
        mine = [pieces[kj] if isinstance(pieces[kj], list) else [pieces[kj]] for kj in every]
        other = [[core_swap(p, wide) for p in group] for group in mine]
        late = [i for i, kj in enumerate(every) if kj[0] == 3 or kj[0] == 2 and kj[1] > 0]
        soon = [i for i in range(narrow) if i not in late]
        args = (mine, other)
        carry = aggregate(
            scal, row_sets, [c[:1] for c in col_sets], where, *args, soon, None, False,
            blocks, side, cap,
        )
        own = aggregate(
            scal, row_sets, col_sets, where, *args, late, carry, True, blocks, side, cap
        )
        here = [own] + [x_shift(own, k, wide) for k in range(1, xs)]
        return own, here + [core_swap(p, wide) for p in here]

    def stacked(self_w, first_w, second_w):
        own_w = jnp.where(first, first_w, second_w)
        oth_w = jnp.where(first, second_w, first_w)
        at = [(x_id - k) % xs * cols for k in range(xs)]
        return jnp.concatenate(
            [self_w]
            + [lax.dynamic_slice(w, (a, 0), (cols, width)) for w in (own_w, oth_w) for a in at],
            axis=0,
        )

    own, aggs = spread(feats)
    hidden, grad_pre = layer(
        [node_feats] + aggs, grad_out, stacked(w_self, w_out, w_in), step
    )

    grads = {(0, 0): own_piece(grad_pre)}
    grads[1, 0] = z_shift(grads[0, 0], 1, zs, ys)
    grads[0, 1] = y_shift(grads[0, 0], 1, zs, ys)
    over_rows = (((0,), (0,)), ((), ()))
    share = width // wide
    feat_part = lax.dynamic_slice(node_feats, (0, w_id * share), (nodes, share))
    grad_part = lax.dot_general(
        jnp.concatenate([own, feat_part], axis=1), grad_pre, over_rows, preferred_element_type=F32
    )
    grads[2, 0] = z_shift(after(grads[1, 0], grads[0, 1]), 1, zs, ys)
    grads[1, 1] = y_shift(after(grads[1, 0], grads[0, 1]), 1, zs, ys)
    grads[3, 0] = z_shift(after(grads[2, 0], grads[1, 1]), 1, zs, ys)
    grads[2, 1] = y_shift(after(grads[2, 0], grads[1, 1]), 1, zs, ys)
    for k in range(zs):
        for j in range(1, ys):
            if (k, j) not in grads and (k < 3 or j > 1):
                if k == 3 and ys > 2:
                    continue
                grads[k, j] = y_shift(grads[k, j - 1], 1, zs, ys)
    quarter = half // 2
    for j in range(1, ys):
        before = grads[3, j - 1]
        before = jnp.concatenate(before, axis=0) if isinstance(before, list) else before
        ready = grads[2, 1]
        grads[3, j] = [
            y_shift(after(before[:quarter], ready), 1, zs, ys),
            z_shift(grads[2, j][quarter:], 1, zs, ys),
        ]
    _, backs = spread(grads)

    for pairs in narrow_swaps(narrow):
        grad_part = grad_part + lax.ppermute(grad_part, "narrow", pairs)
    x_parts = [grad_part] + [x_shift(grad_part, k, wide) for k in range(1, xs)]
    stack = jnp.stack(x_parts)
    stack = jnp.stack([stack, core_swap(stack, wide)])
    stack = jnp.where(first, stack, stack[::-1])
    if xs == 2:
        stack = jnp.where(x_id == 0, stack, stack[:, ::-1])
    else:
        stack = stack[:, (x_id - jnp.arange(xs)) % xs]
    agg_grads = stack[:, :, :cols].reshape(CORES, width, width)
    grad_ws = stack[:, :, cols:].swapaxes(0, 1).reshape(width, width)

    grad_feats = final([grad_pre] + backs, stacked(w_self.T, w_in.T, w_out.T), step)
    return (hidden, grad_feats, grad_ws, agg_grads[0], agg_grads[1])


def narrow_swaps(narrow):
    bit = 1
    while bit < narrow:
        yield [(i, i ^ bit) for i in range(narrow)]
        bit *= 2


def solution(mesh):
    return jax.shard_map(
        body,
        mesh=mesh,
        in_specs=(
            P("narrow", None),
            P("narrow", None),
            P("wide", "narrow", None, None, None),
            P("wide", "narrow", None),
            P("wide", "narrow", None),
            P("wide", "narrow", None),
            P(),
            P(),
            P(),
        ),
        out_specs=(P("narrow", None), P("narrow", None), P(), P(), P()),
        check_vma=False,
    )
```

time: 306 us -> 270 us (0.88)
  local copies, waits for them, and re-layouts: 49.3 us -> 12.1 us
  other arithmetic: 11.5 us -> 3.49 us
  starting transfers between devices: 40.5 us -> 45.3 us
  Pallas kernels: 37.6 us -> 41.2 us
    all_to_all x1 -> x0, waiting for transfers between devices: 25 us -> none  [body(): lax.all_to_all(packed(tiles.swapaxes(2, 3)), 'narrow', split_axis=0, conc...]
    slice x29 -> x2, local copies, waits for them, and re-layouts: 21.2 us -> 0.03 us  [the longest x1 0.02 us: body(): before[:quarter]]
    ppermute x18 -> x28, starting transfers between devices: 19.6 us -> 32 us  [the longest x9 18.1 us: to_core(): lax.ppermute(a, 'wide', [(i, ((i // CORES + k) * CORES + target) % wide)...]
    ppermute x3, waiting for transfers between devices: 16.6 us -> 26.6 us  [body(): grad_part = grad_part + lax.ppermute(grad_part, 'narrow', pairs)]
    ppermute x5 -> x3, waiting for transfers between devices: 28.2 us -> 38 us  [x_shift(): lax.ppermute(a, 'wide', [(i, (i + CORES * k) % wide) for i in range(wide)])]
    all_to_all x1 -> x0, starting transfers between devices: 7.42 us -> none  [body(): lax.all_to_all(packed(tiles.swapaxes(2, 3)), 'narrow', split_axis=0, conc...]
    unnamed x63 -> x105, local copies, waits for them, and re-layouts: 11.9 us -> 5.62 us
    ppermute x21 -> x22, waiting for transfers between devices: 0.93 us -> 5.69 us  [core_swap(): return lax.ppermute(a, 'wide', [(i, i ^ 1) for i in range(wide)])]
  transfers between devices with their start and end apart: 48 -> 56, of which waited for: 18 -> 20; matrix products, arithmetic and copies ran while one was open for 16% -> 2% of each run, Pallas kernels for 4% -> 7%
where the time goes in v2:
time: 270 us; the launch traced here: 269 us
  waiting for transfers between devices  164 us (61%)
  starting transfers between devices  45.3 us (17%)
  Pallas kernels  41.2 us (15%)
  local copies, waits for them, and re-layouts  12.1 us (4%)
  other arithmetic  3.49 us (1%)
    ppermute x10, waiting for transfers between devices, z_shift(): lax.ppermute(a, 'narrow', [(z * ys + y, (z + k) % zs * ys + y) for z in r...  56.2 us
    ppermute x3, waiting for transfers between devices, x_shift(): lax.ppermute(a, 'wide', [(i, (i + CORES * k) % wide) for i in range(wide)])  38 us
    ppermute x9, waiting for transfers between devices, y_shift(): lax.ppermute(a, 'narrow', [(z * ys + y, z * ys + (y + k) % ys) for z in r...  37.9 us
    ppermute x3, waiting for transfers between devices, body(): grad_part = grad_part + lax.ppermute(grad_part, 'narrow', pairs)  26.6 us
    pallas_call x4, Pallas kernels, aggregate(): pl.pallas_call(functools.partial(aggregate_kernel, wide, cap, side, block...  25 us
    ppermute x9, starting transfers between devices, to_core(): lax.ppermute(a, 'wide', [(i, ((i // CORES + k) * CORES + target) % wide)...  18.1 us
    pallas_call x1, Pallas kernels, layer(): pl.pallas_call(functools.partial(layer_kernel, len(ins)), grid=(rows // s...  8.83 us
    ppermute x9, starting transfers between devices, y_shift(): lax.ppermute(a, 'narrow', [(z * ys + y, z * ys + (y + k) % ys) for z in r...  8.28 us
  transfers between devices with their start and end apart: 56, of which 20 were waited for; matrix products, arithmetic and copies ran while one was open for 2% of the time, Pallas kernels for 7%

profile of v2, /device:TPU:0, one launch (start us, length us, event | category | flops | bytes accessed | tf_op | source)
XLA Modules:
  0.0 268.8 jit_solution(4132849458945571086)
XLA Ops:
  0.7 0.7 convert_reduce_fusion
  1.5 0.7 compare_convert_fusion
  2.3 1.6 copy.55
  4.0 3.0 %collective-permute-start.3 = (bf16[4,528,128]{2,1,0:T(8,128)(2,1)S(1)}, bf16[4,528,128]{2,1,0:T(8,128)(2,1)S(1)}, u32[]{:S(2)}, u32[]{:S(2)}) collective-permute-start(bf16[4,528,128]{2,1,0:T(8,128)(2,1)S(1)} %get-tuple-element.33), channel_id=1, source_target_pairs={{0,1},{1,0},{2,3},{3,2},{4,5},{5,4},{6,7},{7,6},{8,9},{9,8},{10,11... | collective-permute-start | bytes 1622024 | tf_op jit(solution)/shard_map/ppermute | solution.py:44
  7.1 1.0 dynamic_slice.58
  8.1 1.6 collective-permute-start.5
  9.8 12.4 %collective-permute-done.5.refs_10_ = bf16[14,128,128]{2,1,0:T(8,128)(2,1)} collective-permute-done((bf16[14,128,128]{2,1,0:T(8,128)(2,1)S(1)}, bf16[14,128,128]{2,1,0:T(8,128)(2,1)}, u32[]{:S(2)}, u32[]{:S(2)}) %collective-permute-start.5) | collective-permute-done | bytes 458784 | tf_op jit(solution)/shard_map/ppermute | solution.py:38
  22.3 1.3 collective-permute-start.4
  24.2 1.3 collective-permute-start
  25.5 3.4 %collective-permute-start.1 = (bf16[8,528,128]{2,1,0:T(8,128)(2,1)S(1)}, bf16[8,528,128]{2,1,0:T(8,128)(2,1)S(1)}, u32[]{:S(2)}, u32[]{:S(2)}) collective-permute-start(bf16[8,528,128]{2,1,0:T(8,128)(2,1)S(1)} %pad_maximum_fusion.refs_0_), channel_id=1, source_target_pairs={{0,16},{16,0},{1,17},{17,1},{2,18},{18,2},{3,19},{19,3},{4,20},{20... | collective-permute-start | bytes 3244040 | tf_op jit(solution)/shard_map/ppermute | solution.py:30
  28.9 12.2 %collective-permute-done.4 = bf16[2,528,128]{2,1,0:T(8,128)(2,1)S(1)} collective-permute-done((bf16[2,528,128]{2,1,0:T(8,128)(2,1)S(1)}, bf16[2,528,128]{2,1,0:T(8,128)(2,1)S(1)}, u32[]{:S(2)}, u32[]{:S(2)}) %collective-permute-start.4) | collective-permute-done | bytes 270368 | tf_op jit(solution)/shard_map/ppermute | solution.py:38
  41.1 1.3 collective-permute-start.2
  42.4 2.4 collective-permute-start.25
  45.2 1.1 collective-permute-done.25.refs_15_
  46.4 11.1 %collective-permute-done.16.refs_11_ = bf16[14,128,128]{2,1,0:T(8,128)(2,1)S(1)} collective-permute-done((bf16[14,128,128]{2,1,0:T(8,128)(2,1)}, bf16[14,128,128]{2,1,0:T(8,128)(2,1)S(1)}, u32[]{:S(2)}, u32[]{:S(2)}) %collective-permute-start.16) | collective-permute-done | bytes 458784 | tf_op jit(solution)/shard_map/ppermute | solution.py:44
  57.6 2.2 collective-permute-done.7
  60.3 2.5 collective-permute-start.8
  62.9 2.6 collective-permute-start.11
  65.5 12.6 %collective-permute-done.8.refs_5_ = bf16[2,528,128]{2,1,0:T(8,128)(2,1)S(1)} collective-permute-done((bf16[2,528,128]{2,1,0:T(8,128)(2,1)S(1)}, bf16[2,528,128]{2,1,0:T(8,128)(2,1)S(1)}, u32[]{:S(2)}, u32[]{:S(2)}) %collective-permute-start.8) | collective-permute-done | bytes 270368 | tf_op jit(solution)/shard_map/ppermute | solution.py:38
  78.1 1.9 collective-permute-start.10
  80.1 0.7 collective-permute-start.13
  80.8 2.8 %collective-permute-start.9 = (bf16[6,528,128]{2,1,0:T(8,128)(2,1)S(1)}, bf16[6,528,128]{2,1,0:T(8,128)(2,1)S(1)}, u32[]{:S(2)}, u32[]{:S(2)}) collective-permute-start(bf16[6,528,128]{2,1,0:T(8,128)(2,1)S(1)} %pad_maximum_fusion.1.refs_4_), channel_id=1, source_target_pairs={{0,8},{16,24},{1,9},{17,25},{2,10},{18,26},{3,11},{19,27},{4,12},{... | collective-permute-start | bytes 2433032 | tf_op jit(solution)/shard_map/ppermute | solution.py:30
  83.7 0.8 collective-permute-start.19
  84.5 1.6 collective-permute-done.26.refs_16_
  86.6 10.3 %collective-permute-done.19.refs_14_ = bf16[14,128,128]{2,1,0:T(8,128)(2,1)} collective-permute-done((bf16[14,128,128]{2,1,0:T(8,128)(2,1)}, bf16[14,128,128]{2,1,0:T(8,128)(2,1)}, u32[]{:S(2)}, u32[]{:S(2)}) %collective-permute-start.19) | collective-permute-done | bytes 458784 | tf_op jit(solution)/shard_map/ppermute | solution.py:44
  96.9 3.5 %collective-permute-start.12 = (bf16[2,528,128]{2,1,0:T(8,128)(2,1)S(1)}, bf16[2,528,128]{2,1,0:T(8,128)(2,1)S(1)}, u32[]{:S(2)}, u32[]{:S(2)}) collective-permute-start(bf16[2,528,128]{2,1,0:T(8,128)(2,1)S(1)} %collective-permute-done.8.refs_5_), channel_id=1, source_target_pairs={{0,24},{16,8},{1,25},{17,9},{2,26},{18,10},{3,27},{19,11},{4,28},{... | collective-permute-start | bytes 811016 | tf_op jit(solution)/shard_map/ppermute | solution.py:30
  100.5 0.9 copy-done.7
  101.4 0.7 collective-permute-start.14
  102.7 6.7 %shard_map.128.refs_18_ = f32[29,128,128]{2,1,0:T(8,128)} custom-call(s32[9]{0:T(128)} %pad_add_fusion.scal, bf16[8,528,128]{2,1,0:T(8,128)(2,1)} %copy-done, bf16[8,528,128]{2,1,0:T(8,128)(2,1)} %copy-done.2, bf16[8,528,128]{2,1,0:T(8,128)(2,1)} %copy-done.3, bf16[8,528,128]{2,1,0:T(8,128)(2,1)} %copy-done.4, bf16[6,528,128]{2,1,0:T(8,128)(2,1)} %copy-done.1, ...), custom_call_target="tpu_custom_call" | custom-call | flops 335544320 | bytes 7864320 | tf_op jit(solution)/shard_map/pallas_call | solution.py:172
  109.5 0.6 copy-done.17
  110.3 5.8 %shard_map.129.refs_1_ = bf16[3584,128]{1,0:T(8,128)(2,1)} custom-call(s32[9]{0:T(128)} %pad_add_fusion.scal, bf16[8,528,128]{2,1,0:T(8,128)(2,1)} %copy-done, bf16[8,528,128]{2,1,0:T(8,128)(2,1)} %copy-done.2, bf16[8,528,128]{2,1,0:T(8,128)(2,1)} %copy-done.3, bf16[8,528,128]{2,1,0:T(8,128)(2,1)} %copy-done.4, bf16[6,528,128]{2,1,0:T(8,128)(2,1)} %copy-done.1, ...), custom_call_target="tpu_custom_call" | custom-call | flops 201326592 | bytes 4718592 | tf_op jit(solution)/shard_map/pallas_call | solution.py:172
  116.1 0.6 collective-permute-start.28
  116.9 1.6 collective-permute-start.29
  118.6 20.1 %collective-permute-done.28.refs_2_ = bf16[3584,128]{1,0:T(8,128)(2,1)S(1)} collective-permute-done((bf16[3584,128]{1,0:T(8,128)(2,1)}, bf16[3584,128]{1,0:T(8,128)(2,1)S(1)}, u32[]{:S(2)}, u32[]{:S(2)}) %collective-permute-start.28) | collective-permute-done | bytes 917536 | tf_op jit(solution)/shard_map/ppermute | solution.py:22
  138.7 0.7 collective-permute-start.30
  140.1 1.4 collective-permute-done.30.refs_4_
  141.5 0.9 copy-done.24
  142.4 8.8 %shard_map.130 = (bf16[3584,256]{1,0:T(8,128)(2,1)}, bf16[3584,256]{1,0:T(8,128)(2,1)}) custom-call(bf16[3584,256]{1,0:T(8,128)(2,1)} %refs_0_.1, bf16[3584,128]{1,0:T(8,128)(2,1)} %shard_map.129.refs_1_, bf16[3584,128]{1,0:T(8,128)(2,1)} %copy-done.21, bf16[3584,128]{1,0:T(8,128)(2,1)} %copy-done.23, bf16[3584,128]{1,0:T(8,128)(2,1)} %copy-done.24, ...), custom_call_target="tpu_custom_call" | custom-call | tf_op jit(solution)/shard_map/pallas_call | solution.py:223
  151.3 1.2 dynamic_slice.64
  153.6 13.5 %collective-permute-done.31.refs_10_ = bf16[14,128,128]{2,1,0:T(8,128)(2,1)S(1)} collective-permute-done((bf16[14,128,128]{2,1,0:T(8,128)(2,1)S(1)}, bf16[14,128,128]{2,1,0:T(8,128)(2,1)S(1)}, u32[]{:S(2)}, u32[]{:S(2)}) %collective-permute-start.31) | collective-permute-done | bytes 458784 | tf_op jit(solution)/shard_map/ppermute | solution.py:38
  167.7 0.7 fusion
  168.4 1.5 collective-permute-start.51
  170.0 10.7 %collective-permute-done.34.refs_11_ = bf16[14,128,128]{2,1,0:T(8,128)(2,1)S(1)} collective-permute-done((bf16[14,128,128]{2,1,0:T(8,128)(2,1)S(1)}, bf16[14,128,128]{2,1,0:T(8,128)(2,1)S(1)}, u32[]{:S(2)}, u32[]{:S(2)}) %collective-permute-start.34) | collective-permute-done | bytes 458784 | tf_op jit(solution)/shard_map/ppermute | solution.py:44
  180.6 0.7 collective-permute-done.33.refs_12_
  181.3 2.0 collective-permute-done.51
  184.1 14.2 %collective-permute-done.52 = f32[192,256]{1,0:T(8,128)S(1)} collective-permute-done((f32[192,256]{1,0:T(8,128)S(1)}, f32[192,256]{1,0:T(8,128)S(1)}, u32[]{:S(2)}, u32[]{:S(2)}) %collective-permute-start.52) | collective-permute-done | bytes 196640 | tf_op jit(solution)/shard_map/ppermute | solution.py:391
  198.9 0.6 collective-permute-start.53
  199.6 10.4 %collective-permute-done.53 = f32[192,256]{1,0:T(8,128)S(1)} collective-permute-done((f32[192,256]{1,0:T(8,128)S(1)}, f32[192,256]{1,0:T(8,128)S(1)}, u32[]{:S(2)}, u32[]{:S(2)}) %collective-permute-start.53) | collective-permute-done | bytes 196640 | tf_op jit(solution)/shard_map/ppermute | solution.py:391
  209.9 1.1 collective-permute-start.37
  211.6 5.9 %collective-permute-done.37.refs_14_ = bf16[7,128,128]{2,1,0:T(8,128)(2,1)S(1)} collective-permute-done((bf16[7,128,128]{2,1,0:T(8,128)(2,1)S(1)}, bf16[7,128,128]{2,1,0:T(8,128)(2,1)S(1)}, u32[]{:S(2)}, u32[]{:S(2)}) %collective-permute-start.37) | collective-permute-done | bytes 229408 | tf_op jit(solution)/shard_map/ppermute | solution.py:44
  217.5 2.7 %collective-permute-done.38.refs_15_ = bf16[7,128,128]{2,1,0:T(8,128)(2,1)} collective-permute-done((bf16[7,128,128]{2,1,0:T(8,128)(2,1)S(1)}, bf16[7,128,128]{2,1,0:T(8,128)(2,1)}, u32[]{:S(2)}, u32[]{:S(2)}) %collective-permute-start.38) | collective-permute-done | bytes 229408 | tf_op jit(solution)/shard_map/ppermute | solution.py:38
  220.4 0.9 collective-permute-start.54
  221.3 6.6 %shard_map.131.refs_20_ = f32[29,128,128]{2,1,0:T(8,128)} custom-call(s32[9]{0:T(128)} %pad_add_fusion.scal, bf16[8,528,128]{2,1,0:T(8,128)(2,1)} %copy-done, bf16[8,528,128]{2,1,0:T(8,128)(2,1)} %copy-done.2, bf16[8,528,128]{2,1,0:T(8,128)(2,1)} %copy-done.3, bf16[8,528,128]{2,1,0:T(8,128)(2,1)} %copy-done.4, bf16[6,528,128]{2,1,0:T(8,128)(2,1)} %copy-done.1, ...), custom_call_target="tpu_custom_call" | custom-call | flops 335544320 | bytes 7864320 | tf_op jit(solution)/shard_map/pallas_call | solution.py:172
  228.0 5.9 %shard_map.132.refs_1_ = bf16[3584,128]{1,0:T(8,128)(2,1)} custom-call(s32[9]{0:T(128)} %pad_add_fusion.scal, bf16[8,528,128]{2,1,0:T(8,128)(2,1)} %copy-done, bf16[8,528,128]{2,1,0:T(8,128)(2,1)} %copy-done.2, bf16[8,528,128]{2,1,0:T(8,128)(2,1)} %copy-done.3, bf16[8,528,128]{2,1,0:T(8,128)(2,1)} %copy-done.4, bf16[6,528,128]{2,1,0:T(8,128)(2,1)} %copy-done.1, ...), custom_call_target="tpu_custom_call" | custom-call | flops 201326592 | bytes 4718592 | tf_op jit(solution)/shard_map/pallas_call | solution.py:172
  233.9 1.3 collective-permute-start.48
  235.2 0.8 fusion.31
  236.1 1.1 collective-permute-start.55
  237.2 1.5 collective-permute-done.55
  239.2 17.9 %collective-permute-done.48.refs_2_ = bf16[3584,128]{1,0:T(8,128)(2,1)S(1)} collective-permute-done((bf16[3584,128]{1,0:T(8,128)(2,1)}, bf16[3584,128]{1,0:T(8,128)(2,1)S(1)}, u32[]{:S(2)}, u32[]{:S(2)}) %collective-permute-start.48) | collective-permute-done | bytes 917536 | tf_op jit(solution)/shard_map/ppermute | solution.py:22
  258.0 0.7 copy.65
  258.7 0.8 fusion.32
  259.6 0.9 copy-done.25
  260.5 1.0 copy-done.26
  261.5 7.3 %shard_map.133 = bf16[3584,256]{1,0:T(8,128)(2,1)} custom-call(bf16[3584,256]{1,0:T(8,128)(2,1)} %get-tuple-element.25.refs_0_, bf16[3584,128]{1,0:T(8,128)(2,1)} %shard_map.132.refs_1_, bf16[3584,128]{1,0:T(8,128)(2,1)} %copy-done.22, bf16[3584,128]{1,0:T(8,128)(2,1)} %copy-done.25, bf16[3584,128]{1,0:T(8,128)(2,1)} %copy-done.26, bf16[768,256]{1,0:T(8,128)(2,1)} %copy-done.27), custom_call_target="tpu_custom_call" | custom-call | tf_op jit(solution)/shard_map/pallas_call | solution.py:236
  (195 shorter events, 9.7 us)
Async XLA Ops:
  4.0 18.1 %collective-permute-start.3 = (bf16[4,528,128]{2,1,0:T(8,128)(2,1)S(1)}, bf16[4,528,128]{2,1,0:T(8,128)(2,1)S(1)}, u32[]{:S(2)}, u32[]{:S(2)}) collective-permute-start(bf16[4,528,128]{2,1,0:T(8,128)(2,1)S(1)} %get-tuple-element.33), channel_id=1, source_target_pairs={{0,1},{1,0},{2,3},{3,2},{4,5},{5,4},{6,7},{7,6},{8,9},{9,8},{10,11... | collective-permute-start | bytes 1622024 | tf_op jit(solution)/shard_map/ppermute | solution.py:44
  8.1 14.0 %collective-permute-start.5 = (bf16[14,128,128]{2,1,0:T(8,128)(2,1)S(1)}, bf16[14,128,128]{2,1,0:T(8,128)(2,1)}, u32[]{:S(2)}, u32[]{:S(2)}) collective-permute-start(bf16[14,128,128]{2,1,0:T(8,128)(2,1)S(1)} %bitcast.45), channel_id=1, source_target_pairs={{0,2},{1,3},{2,4},{3,5},{4,6},{5,7},{6,0},{7,1},{8,10},{9,11},{10,... | collective-permute-start | bytes 1376264 | tf_op jit(solution)/shard_map/ppermute | solution.py:38
  9.8 15.7 %collective-permute-start.23 = (bf16[14,128,128]{2,1,0:T(8,128)(2,1)S(1)}, bf16[14,128,128]{2,1,0:T(8,128)(2,1)}, u32[]{:S(2)}, u32[]{:S(2)}) collective-permute-start(bf16[14,128,128]{2,1,0:T(8,128)(2,1)S(1)} %bitcast.46), channel_id=1, source_target_pairs={{0,8},{8,0},{16,24},{24,16},{1,9},{9,1},{17,25},{25,17},{2,10},{10... | collective-permute-start | bytes 1376264 | tf_op jit(solution)/shard_map/ppermute | solution.py:26
  22.1 22.6 %collective-permute-start.6 = (bf16[14,128,128]{2,1,0:T(8,128)(2,1)}, bf16[14,128,128]{2,1,0:T(8,128)(2,1)S(1)}, u32[]{:S(2)}, u32[]{:S(2)}) collective-permute-start(bf16[14,128,128]{2,1,0:T(8,128)(2,1)} %collective-permute-done.5.refs_10_), channel_id=1, source_target_pairs={{0,2},{1,3},{2,4},{3,5},{4,6},{5,7},{6,0},{7,1},{8,10},{9,11},{10,... | collective-permute-start | bytes 1376264 | tf_op jit(solution)/shard_map/ppermute | solution.py:38
  22.3 18.8 %collective-permute-start.4 = (bf16[2,528,128]{2,1,0:T(8,128)(2,1)S(1)}, bf16[2,528,128]{2,1,0:T(8,128)(2,1)S(1)}, u32[]{:S(2)}, u32[]{:S(2)}) collective-permute-start(bf16[2,528,128]{2,1,0:T(8,128)(2,1)S(1)} %get-tuple-element.31), channel_id=1, source_target_pairs={{0,2},{1,3},{2,4},{3,5},{4,6},{5,7},{6,0},{7,1},{8,10},{9,11},{10,... | collective-permute-start | bytes 811016 | tf_op jit(solution)/shard_map/ppermute | solution.py:38
  23.6 18.8 %collective-permute-start.15 = (bf16[14,128,128]{2,1,0:T(8,128)(2,1)S(1)}, bf16[14,128,128]{2,1,0:T(8,128)(2,1)S(1)}, u32[]{:S(2)}, u32[]{:S(2)}) collective-permute-start(bf16[14,128,128]{2,1,0:T(8,128)(2,1)S(1)} %bitcast.47), channel_id=1, source_target_pairs={{0,1},{1,0},{2,3},{3,2},{4,5},{5,4},{6,7},{7,6},{8,9},{9,8},{10,11... | collective-permute-start | bytes 1376264 | tf_op jit(solution)/shard_map/ppermute | solution.py:44
  24.2 78.5 %copy-start = (bf16[8,528,128]{2,1,0:T(8,128)(2,1)}, bf16[8,528,128]{2,1,0:T(8,128)(2,1)S(1)}, u32[]{:S(2)}) copy-start(bf16[8,528,128]{2,1,0:T(8,128)(2,1)S(1)} %pad_maximum_fusion.refs_0_) | copy-start | bytes 3244036
  24.2 33.3 %collective-permute-start = (bf16[8,528,128]{2,1,0:T(8,128)(2,1)S(1)}, bf16[8,528,128]{2,1,0:T(8,128)(2,1)S(1)}, u32[]{:S(2)}, u32[]{:S(2)}) collective-permute-start(bf16[8,528,128]{2,1,0:T(8,128)(2,1)S(1)} %pad_maximum_fusion.refs_0_), channel_id=1, source_target_pairs={{8,0},{24,16},{9,1},{25,17},{10,2},{26,18},{11,3},{27,19},{12,4},{... | collective-permute-start | bytes 3244040 | tf_op jit(solution)/shard_map/ppermute | solution.py:30
  25.5 34.8 %collective-permute-start.1 = (bf16[8,528,128]{2,1,0:T(8,128)(2,1)S(1)}, bf16[8,528,128]{2,1,0:T(8,128)(2,1)S(1)}, u32[]{:S(2)}, u32[]{:S(2)}) collective-permute-start(bf16[8,528,128]{2,1,0:T(8,128)(2,1)S(1)} %pad_maximum_fusion.refs_0_), channel_id=1, source_target_pairs={{0,16},{16,0},{1,17},{17,1},{2,18},{18,2},{3,19},{19,3},{4,20},{20... | collective-permute-start | bytes 3244040 | tf_op jit(solution)/shard_map/ppermute | solution.py:30
  41.1 21.7 %collective-permute-start.2 = (bf16[8,528,128]{2,1,0:T(8,128)(2,1)S(1)}, bf16[8,528,128]{2,1,0:T(8,128)(2,1)S(1)}, u32[]{:S(2)}, u32[]{:S(2)}) collective-permute-start(bf16[8,528,128]{2,1,0:T(8,128)(2,1)S(1)} %pad_maximum_fusion.refs_0_), channel_id=1, source_target_pairs={{8,16},{24,0},{9,17},{25,1},{10,18},{26,2},{11,19},{27,3},{12,20},... | collective-permute-start | bytes 3244040 | tf_op jit(solution)/shard_map/ppermute | solution.py:30
  42.4 59.7 %copy-start.31 = (bf16[14,128,128]{2,1,0:T(8,128)(2,1)}, bf16[14,128,128]{2,1,0:T(8,128)(2,1)S(1)}, u32[]{:S(2)}) copy-start(bf16[14,128,128]{2,1,0:T(8,128)(2,1)S(1)} %collective-permute-done.15.refs_9_) | copy-start | bytes 1376260
  42.4 4.0 %collective-permute-start.25 = (bf16[14,128,128]{2,1,0:T(8,128)(2,1)}, bf16[14,128,128]{2,1,0:T(8,128)(2,1)S(1)}, u32[]{:S(2)}, u32[]{:S(2)}) collective-permute-start(bf16[14,128,128]{2,1,0:T(8,128)(2,1)} %collective-permute-done.5.refs_10_), channel_id=1, source_target_pairs={{0,8},{8,0},{16,24},{24,16},{1,9},{9,1},{17,25},{25,17},{2,10},{10... | collective-permute-start | bytes 1376264 | tf_op jit(solution)/shard_map/ppermute | solution.py:26
  44.7 57.3 %copy-start.30 = (bf16[14,128,128]{2,1,0:T(8,128)(2,1)}, bf16[14,128,128]{2,1,0:T(8,128)(2,1)S(1)}, u32[]{:S(2)}) copy-start(bf16[14,128,128]{2,1,0:T(8,128)(2,1)S(1)} %collective-permute-done.6.refs_12_) | copy-start | bytes 1376260
  44.7 12.7 %collective-permute-start.16 = (bf16[14,128,128]{2,1,0:T(8,128)(2,1)}, bf16[14,128,128]{2,1,0:T(8,128)(2,1)S(1)}, u32[]{:S(2)}, u32[]{:S(2)}) collective-permute-start(bf16[14,128,128]{2,1,0:T(8,128)(2,1)} %collective-permute-done.5.refs_10_), channel_id=1, source_target_pairs={{0,1},{1,0},{2,3},{3,2},{4,5},{5,4},{6,7},{7,6},{8,9},{9,8},{10,11... | collective-permute-start | bytes 1376264 | tf_op jit(solution)/shard_map/ppermute | solution.py:44
  46.4 13.4 %collective-permute-start.7 = (bf16[2,528,128]{2,1,0:T(8,128)(2,1)S(1)}, bf16[2,528,128]{2,1,0:T(8,128)(2,1)S(1)}, u32[]{:S(2)}, u32[]{:S(2)}) collective-permute-start(bf16[2,528,128]{2,1,0:T(8,128)(2,1)S(1)} %get-tuple-element.17), channel_id=1, source_target_pairs={{0,4},{1,5},{2,6},{3,7},{4,0},{5,1},{6,2},{7,3},{8,12},{9,13},{10,... | collective-permute-start | bytes 811016 | tf_op jit(solution)/shard_map/ppermute | solution.py:38
  57.5 5.4 %collective-permute-start.27 = (bf16[14,128,128]{2,1,0:T(8,128)(2,1)S(1)}, bf16[14,128,128]{2,1,0:T(8,128)(2,1)S(1)}, u32[]{:S(2)}, u32[]{:S(2)}) collective-permute-start(bf16[14,128,128]{2,1,0:T(8,128)(2,1)S(1)} %collective-permute-done.6.refs_12_), channel_id=1, source_target_pairs={{0,8},{8,0},{16,24},{24,16},{1,9},{9,1},{17,25},{25,17},{2,10},{10... | collective-permute-start | bytes 1376264 | tf_op jit(solution)/shard_map/ppermute | solution.py:26
  57.5 45.2 %copy-start.2 = (bf16[8,528,128]{2,1,0:T(8,128)(2,1)}, bf16[8,528,128]{2,1,0:T(8,128)(2,1)S(1)}, u32[]{:S(2)}) copy-start(bf16[8,528,128]{2,1,0:T(8,128)(2,1)S(1)} %collective-permute-done.refs_1_) | copy-start | bytes 3244036
  57.5 22.6 %collective-permute-start.18 = (bf16[14,128,128]{2,1,0:T(8,128)(2,1)S(1)}, bf16[14,128,128]{2,1,0:T(8,128)(2,1)}, u32[]{:S(2)}, u32[]{:S(2)}) collective-permute-start(bf16[14,128,128]{2,1,0:T(8,128)(2,1)S(1)} %collective-permute-done.6.refs_12_), channel_id=1, source_target_pairs={{0,2},{1,3},{2,4},{3,5},{4,6},{5,7},{6,0},{7,1},{8,10},{9,11},{10,... | collective-permute-start | bytes 1376264 | tf_op jit(solution)/shard_map/ppermute | solution.py:38
  59.8 21.0 %collective-permute-start.17 = (bf16[14,128,128]{2,1,0:T(8,128)(2,1)S(1)}, bf16[14,128,128]{2,1,0:T(8,128)(2,1)}, u32[]{:S(2)}, u32[]{:S(2)}) collective-permute-start(bf16[14,128,128]{2,1,0:T(8,128)(2,1)S(1)} %collective-permute-done.6.refs_12_), channel_id=1, source_target_pairs={{0,1},{1,0},{2,3},{3,2},{4,5},{5,4},{6,7},{7,6},{8,9},{9,8},{10,11... | collective-permute-start | bytes 1376264 | tf_op jit(solution)/shard_map/ppermute | solution.py:44
  60.3 42.5 %copy-start.3 = (bf16[8,528,128]{2,1,0:T(8,128)(2,1)}, bf16[8,528,128]{2,1,0:T(8,128)(2,1)S(1)}, u32[]{:S(2)}) copy-start(bf16[8,528,128]{2,1,0:T(8,128)(2,1)S(1)} %collective-permute-done.1.refs_2_) | copy-start | bytes 3244036
  60.3 17.8 %collective-permute-start.8 = (bf16[2,528,128]{2,1,0:T(8,128)(2,1)S(1)}, bf16[2,528,128]{2,1,0:T(8,128)(2,1)S(1)}, u32[]{:S(2)}, u32[]{:S(2)}) collective-permute-start(bf16[2,528,128]{2,1,0:T(8,128)(2,1)S(1)} %get-tuple-element.18), channel_id=1, source_target_pairs={{0,6},{1,7},{2,0},{3,1},{4,2},{5,3},{6,4},{7,5},{8,14},{9,15},{10,... | collective-permute-start | bytes 811016 | tf_op jit(solution)/shard_map/ppermute | solution.py:38
  62.8 39.9 %copy-start.4 = (bf16[8,528,128]{2,1,0:T(8,128)(2,1)}, bf16[8,528,128]{2,1,0:T(8,128)(2,1)S(1)}, u32[]{:S(2)}) copy-start(bf16[8,528,128]{2,1,0:T(8,128)(2,1)S(1)} %collective-permute-done.2.refs_3_) | copy-start | bytes 3244036
  62.8 20.8 %collective-permute-start.24 = (bf16[14,128,128]{2,1,0:T(8,128)(2,1)S(1)}, bf16[14,128,128]{2,1,0:T(8,128)(2,1)S(1)}, u32[]{:S(2)}, u32[]{:S(2)}) collective-permute-start(bf16[14,128,128]{2,1,0:T(8,128)(2,1)S(1)} %collective-permute-done.15.refs_9_), channel_id=1, source_target_pairs={{0,8},{8,0},{16,24},{24,16},{1,9},{9,1},{17,25},{25,17},{2,10},{10... | collective-permute-start | bytes 1376264 | tf_op jit(solution)/shard_map/ppermute | solution.py:26
  62.9 39.8 %copy-start.1 = (bf16[6,528,128]{2,1,0:T(8,128)(2,1)}, bf16[6,528,128]{2,1,0:T(8,128)(2,1)S(1)}, u32[]{:S(2)}) copy-start(bf16[6,528,128]{2,1,0:T(8,128)(2,1)S(1)} %pad_maximum_fusion.1.refs_4_) | copy-start | bytes 2433028
  62.9 23.5 %collective-permute-start.11 = (bf16[6,528,128]{2,1,0:T(8,128)(2,1)S(1)}, bf16[6,528,128]{2,1,0:T(8,128)(2,1)S(1)}, u32[]{:S(2)}, u32[]{:S(2)}) collective-permute-start(bf16[6,528,128]{2,1,0:T(8,128)(2,1)S(1)} %pad_maximum_fusion.1.refs_4_), channel_id=1, source_target_pairs={{0,24},{16,8},{1,25},{17,9},{2,26},{18,10},{3,27},{19,11},{4,28},{... | collective-permute-start | bytes 2433032 | tf_op jit(solution)/shard_map/ppermute | solution.py:30
  78.1 5.6 %collective-permute-start.10 = (bf16[2,528,128]{2,1,0:T(8,128)(2,1)S(1)}, bf16[2,528,128]{2,1,0:T(8,128)(2,1)S(1)}, u32[]{:S(2)}, u32[]{:S(2)}) collective-permute-start(bf16[2,528,128]{2,1,0:T(8,128)(2,1)S(1)} %collective-permute-done.8.refs_5_), channel_id=1, source_target_pairs={{0,8},{16,24},{1,9},{17,25},{2,10},{18,26},{3,11},{19,27},{4,12},{... | collective-permute-start | bytes 811016 | tf_op jit(solution)/shard_map/ppermute | solution.py:30
  80.1 16.9 %collective-permute-start.13 = (bf16[6,528,128]{2,1,0:T(8,128)(2,1)S(1)}, bf16[6,528,128]{2,1,0:T(8,128)(2,1)S(1)}, u32[]{:S(2)}, u32[]{:S(2)}) collective-permute-start(bf16[6,528,128]{2,1,0:T(8,128)(2,1)S(1)} %pad_maximum_fusion.1.refs_4_), channel_id=1, source_target_pairs={{8,24},{24,8},{9,25},{25,9},{10,26},{26,10},{11,27},{27,11},{12,28... | collective-permute-start | bytes 2433032 | tf_op jit(solution)/shard_map/ppermute | solution.py:30
  80.8 19.7 %collective-permute-start.9 = (bf16[6,528,128]{2,1,0:T(8,128)(2,1)S(1)}, bf16[6,528,128]{2,1,0:T(8,128)(2,1)S(1)}, u32[]{:S(2)}, u32[]{:S(2)}) collective-permute-start(bf16[6,528,128]{2,1,0:T(8,128)(2,1)S(1)} %pad_maximum_fusion.1.refs_4_), channel_id=1, source_target_pairs={{0,8},{16,24},{1,9},{17,25},{2,10},{18,26},{3,11},{19,27},{4,12},{... | collective-permute-start | bytes 2433032 | tf_op jit(solution)/shard_map/ppermute | solution.py:30
  83.6 2.5 collective-permute-start.26
  83.7 13.2 %collective-permute-start.19 = (bf16[14,128,128]{2,1,0:T(8,128)(2,1)}, bf16[14,128,128]{2,1,0:T(8,128)(2,1)}, u32[]{:S(2)}, u32[]{:S(2)}) collective-permute-start(bf16[14,128,128]{2,1,0:T(8,128)(2,1)} %collective-permute-done.18.refs_13_), channel_id=1, source_target_pairs={{0,1},{1,0},{2,3},{3,2},{4,5},{5,4},{6,7},{7,6},{8,9},{9,8},{10,11... | collective-permute-start | bytes 1376264 | tf_op jit(solution)/shard_map/ppermute | solution.py:44
  86.1 23.4 %collective-permute-start.21 = (bf16[14,128,128]{2,1,0:T(8,128)(2,1)}, bf16[14,128,128]{2,1,0:T(8,128)(2,1)}, u32[]{:S(2)}, u32[]{:S(2)}) collective-permute-start(bf16[14,128,128]{2,1,0:T(8,128)(2,1)} %collective-permute-done.18.refs_13_), channel_id=1, source_target_pairs={{0,8},{8,0},{16,24},{24,16},{1,9},{9,1},{17,25},{25,17},{2,10},{10... | collective-permute-start | bytes 1376264 | tf_op jit(solution)/shard_map/ppermute | solution.py:26
  86.5 23.0 %collective-permute-start.20 = (bf16[14,128,128]{2,1,0:T(8,128)(2,1)}, bf16[14,128,128]{2,1,0:T(8,128)(2,1)}, u32[]{:S(2)}, u32[]{:S(2)}) collective-permute-start(bf16[14,128,128]{2,1,0:T(8,128)(2,1)} %collective-permute-done.17.refs_12_), channel_id=1, source_target_pairs={{0,8},{8,0},{16,24},{24,16},{1,9},{9,1},{17,25},{25,17},{2,10},{10... | collective-permute-start | bytes 1376264 | tf_op jit(solution)/shard_map/ppermute | solution.py:26
  96.9 12.6 %collective-permute-start.22 = (bf16[14,128,128]{2,1,0:T(8,128)(2,1)}, bf16[14,128,128]{2,1,0:T(8,128)(2,1)}, u32[]{:S(2)}, u32[]{:S(2)}) collective-permute-start(bf16[14,128,128]{2,1,0:T(8,128)(2,1)} %collective-permute-done.19.refs_14_), channel_id=1, source_target_pairs={{0,8},{8,0},{16,24},{24,16},{1,9},{9,1},{17,25},{25,17},{2,10},{10... | collective-permute-start | bytes 1376264 | tf_op jit(solution)/shard_map/ppermute | solution.py:26
  96.9 12.5 %collective-permute-start.12 = (bf16[2,528,128]{2,1,0:T(8,128)(2,1)S(1)}, bf16[2,528,128]{2,1,0:T(8,128)(2,1)S(1)}, u32[]{:S(2)}, u32[]{:S(2)}) collective-permute-start(bf16[2,528,128]{2,1,0:T(8,128)(2,1)S(1)} %collective-permute-done.8.refs_5_), channel_id=1, source_target_pairs={{0,24},{16,8},{1,25},{17,9},{2,26},{18,10},{3,27},{19,11},{4,28},{... | collective-permute-start | bytes 811016 | tf_op jit(solution)/shard_map/ppermute | solution.py:30
  101.4 8.1 %collective-permute-start.14 = (bf16[2,528,128]{2,1,0:T(8,128)(2,1)S(1)}, bf16[2,528,128]{2,1,0:T(8,128)(2,1)S(1)}, u32[]{:S(2)}, u32[]{:S(2)}) collective-permute-start(bf16[2,528,128]{2,1,0:T(8,128)(2,1)S(1)} %collective-permute-done.8.refs_5_), channel_id=1, source_target_pairs={{8,24},{24,8},{9,25},{25,9},{10,26},{26,10},{11,27},{27,11},{12,28... | collective-permute-start | bytes 811016 | tf_op jit(solution)/shard_map/ppermute | solution.py:30
  116.1 22.6 %collective-permute-start.28 = (bf16[3584,128]{1,0:T(8,128)(2,1)}, bf16[3584,128]{1,0:T(8,128)(2,1)S(1)}, u32[]{:S(2)}, u32[]{:S(2)}) collective-permute-start(bf16[3584,128]{1,0:T(8,128)(2,1)} %shard_map.129.refs_1_), channel_id=1, source_target_pairs={{0,16},{8,24},{16,0},{24,8},{1,17},{9,25},{17,1},{25,9},{2,18},{10... | collective-permute-start | bytes 2752520 | tf_op jit(solution)/shard_map/ppermute | solution.py:22
  116.9 23.1 %collective-permute-start.29 = (bf16[3584,128]{1,0:T(8,128)(2,1)}, bf16[3584,128]{1,0:T(8,128)(2,1)S(1)}, u32[]{:S(2)}, u32[]{:S(2)}) collective-permute-start(bf16[3584,128]{1,0:T(8,128)(2,1)} %shard_map.129.refs_1_), channel_id=1, source_target_pairs={{0,8},{8,0},{16,24},{24,16},{1,9},{9,1},{17,25},{25,17},{2,10},{10... | collective-permute-start | bytes 2752520 | tf_op jit(solution)/shard_map/ppermute | solution.py:26
  138.7 2.8 %collective-permute-start.30 = (bf16[3584,128]{1,0:T(8,128)(2,1)S(1)}, bf16[3584,128]{1,0:T(8,128)(2,1)S(1)}, u32[]{:S(2)}, u32[]{:S(2)}) collective-permute-start(bf16[3584,128]{1,0:T(8,128)(2,1)S(1)} %collective-permute-done.28.refs_2_), channel_id=1, source_target_pairs={{0,8},{8,0},{16,24},{24,16},{1,9},{9,1},{17,25},{25,17},{2,10},{10... | collective-permute-start | bytes 2752520 | tf_op jit(solution)/shard_map/ppermute | solution.py:26
  152.5 14.6 %collective-permute-start.31 = (bf16[14,128,128]{2,1,0:T(8,128)(2,1)S(1)}, bf16[14,128,128]{2,1,0:T(8,128)(2,1)S(1)}, u32[]{:S(2)}, u32[]{:S(2)}) collective-permute-start(bf16[14,128,128]{2,1,0:T(8,128)(2,1)S(1)} %bitcast.49), channel_id=1, source_target_pairs={{0,2},{1,3},{2,4},{3,5},{4,6},{5,7},{6,0},{7,1},{8,10},{9,11},{10,... | collective-permute-start | bytes 1376264 | tf_op jit(solution)/shard_map/ppermute | solution.py:38
  152.5 14.6 %collective-permute-start.32 = (bf16[14,128,128]{2,1,0:T(8,128)(2,1)S(1)}, bf16[14,128,128]{2,1,0:T(8,128)(2,1)S(1)}, u32[]{:S(2)}, u32[]{:S(2)}) collective-permute-start(bf16[14,128,128]{2,1,0:T(8,128)(2,1)S(1)} %bitcast.50), channel_id=1, source_target_pairs={{0,1},{1,0},{2,3},{3,2},{4,5},{5,4},{6,7},{7,6},{8,9},{9,8},{10,11... | collective-permute-start | bytes 1376264 | tf_op jit(solution)/shard_map/ppermute | solution.py:44
  153.5 44.9 %collective-permute-start.43 = (bf16[14,128,128]{2,1,0:T(8,128)(2,1)S(1)}, bf16[14,128,128]{2,1,0:T(8,128)(2,1)S(1)}, u32[]{:S(2)}, u32[]{:S(2)}) collective-permute-start(bf16[14,128,128]{2,1,0:T(8,128)(2,1)S(1)} %bitcast.51), channel_id=1, source_target_pairs={{0,8},{8,0},{16,24},{24,16},{1,9},{9,1},{17,25},{25,17},{2,10},{10... | collective-permute-start | bytes 1376264 | tf_op jit(solution)/shard_map/ppermute | solution.py:26
  167.1 13.5 %collective-permute-start.34 = (bf16[14,128,128]{2,1,0:T(8,128)(2,1)S(1)}, bf16[14,128,128]{2,1,0:T(8,128)(2,1)S(1)}, u32[]{:S(2)}, u32[]{:S(2)}) collective-permute-start(bf16[14,128,128]{2,1,0:T(8,128)(2,1)S(1)} %collective-permute-done.31.refs_10_), channel_id=1, source_target_pairs={{0,1},{1,0},{2,3},{3,2},{4,5},{5,4},{6,7},{7,6},{8,9},{9,8},{10,11... | collective-permute-start | bytes 1376264 | tf_op jit(solution)/shard_map/ppermute | solution.py:44
  167.7 13.6 %collective-permute-start.33 = (bf16[14,128,128]{2,1,0:T(8,128)(2,1)S(1)}, bf16[14,128,128]{2,1,0:T(8,128)(2,1)}, u32[]{:S(2)}, u32[]{:S(2)}) collective-permute-start(bf16[14,128,128]{2,1,0:T(8,128)(2,1)S(1)} %collective-permute-done.31.refs_10_), channel_id=1, source_target_pairs={{0,2},{1,3},{2,4},{3,5},{4,6},{5,7},{6,0},{7,1},{8,10},{9,11},{10,... | collective-permute-start | bytes 1376264 | tf_op jit(solution)/shard_map/ppermute | solution.py:38
  168.4 15.0 %collective-permute-start.51 = (f32[192,256]{1,0:T(8,128)S(1)}, f32[192,256]{1,0:T(8,128)S(1)}, u32[]{:S(2)}, u32[]{:S(2)}) collective-permute-start(f32[192,256]{1,0:T(8,128)S(1)} %fusion), channel_id=1, source_target_pairs={{0,1},{1,0},{2,3},{3,2},{4,5},{5,4},{6,7},{7,6},{8,9},{9,8},{10,11... | collective-permute-start | bytes 589832 | tf_op jit(solution)/shard_map/ppermute | solution.py:391
  180.6 39.6 %copy-start.37 = (bf16[14,128,128]{2,1,0:T(8,128)(2,1)}, bf16[14,128,128]{2,1,0:T(8,128)(2,1)S(1)}, u32[]{:S(2)}) copy-start(bf16[14,128,128]{2,1,0:T(8,128)(2,1)S(1)} %collective-permute-done.34.refs_11_) | copy-start | bytes 1376260
  181.3 17.6 %collective-permute-start.36 = (bf16[14,128,128]{2,1,0:T(8,128)(2,1)}, bf16[14,128,128]{2,1,0:T(8,128)(2,1)S(1)}, u32[]{:S(2)}, u32[]{:S(2)}) collective-permute-start(bf16[14,128,128]{2,1,0:T(8,128)(2,1)} %collective-permute-done.33.refs_12_), channel_id=1, source_target_pairs={{0,2},{1,3},{2,4},{3,5},{4,6},{5,7},{6,0},{7,1},{8,10},{9,11},{10,... | collective-permute-start | bytes 1376264 | tf_op jit(solution)/shard_map/ppermute | solution.py:38
  183.4 14.9 %collective-permute-start.52 = (f32[192,256]{1,0:T(8,128)S(1)}, f32[192,256]{1,0:T(8,128)S(1)}, u32[]{:S(2)}, u32[]{:S(2)}) collective-permute-start(f32[192,256]{1,0:T(8,128)S(1)} %add.149), channel_id=1, source_target_pairs={{0,2},{1,3},{2,0},{3,1},{4,6},{5,7},{6,4},{7,5},{8,10},{9,11},{10,... | collective-permute-start | bytes 589832 | tf_op jit(solution)/shard_map/ppermute | solution.py:391
  183.5 16.0 %collective-permute-start.35 = (bf16[14,128,128]{2,1,0:T(8,128)(2,1)}, bf16[14,128,128]{2,1,0:T(8,128)(2,1)S(1)}, u32[]{:S(2)}, u32[]{:S(2)}) collective-permute-start(bf16[14,128,128]{2,1,0:T(8,128)(2,1)} %collective-permute-done.33.refs_12_), channel_id=1, source_target_pairs={{0,1},{1,0},{2,3},{3,2},{4,5},{5,4},{6,7},{7,6},{8,9},{9,8},{10,11... | collective-permute-start | bytes 1376264 | tf_op jit(solution)/shard_map/ppermute | solution.py:44
  184.1 26.9 %collective-permute-start.44 = (bf16[14,128,128]{2,1,0:T(8,128)(2,1)S(1)}, bf16[14,128,128]{2,1,0:T(8,128)(2,1)S(1)}, u32[]{:S(2)}, u32[]{:S(2)}) collective-permute-start(bf16[14,128,128]{2,1,0:T(8,128)(2,1)S(1)} %collective-permute-done.32.refs_9_), channel_id=1, source_target_pairs={{0,8},{8,0},{16,24},{24,16},{1,9},{9,1},{17,25},{25,17},{2,10},{10... | collective-permute-start | bytes 1376264 | tf_op jit(solution)/shard_map/ppermute | solution.py:26
  198.3 12.7 %collective-permute-start.45 = (bf16[14,128,128]{2,1,0:T(8,128)(2,1)S(1)}, bf16[14,128,128]{2,1,0:T(8,128)(2,1)S(1)}, u32[]{:S(2)}, u32[]{:S(2)}) collective-permute-start(bf16[14,128,128]{2,1,0:T(8,128)(2,1)S(1)} %collective-permute-done.31.refs_10_), channel_id=1, source_target_pairs={{0,8},{8,0},{16,24},{24,16},{1,9},{9,1},{17,25},{25,17},{2,10},{10... | collective-permute-start | bytes 1376264 | tf_op jit(solution)/shard_map/ppermute | solution.py:26
  198.4 12.8 %collective-permute-start.46 = (bf16[14,128,128]{2,1,0:T(8,128)(2,1)S(1)}, bf16[14,128,128]{2,1,0:T(8,128)(2,1)S(1)}, u32[]{:S(2)}, u32[]{:S(2)}) collective-permute-start(bf16[14,128,128]{2,1,0:T(8,128)(2,1)S(1)} %collective-permute-done.34.refs_11_), channel_id=1, source_target_pairs={{0,8},{8,0},{16,24},{24,16},{1,9},{9,1},{17,25},{25,17},{2,10},{10... | collective-permute-start | bytes 1376264 | tf_op jit(solution)/shard_map/ppermute | solution.py:26
  198.9 11.0 %collective-permute-start.53 = (f32[192,256]{1,0:T(8,128)S(1)}, f32[192,256]{1,0:T(8,128)S(1)}, u32[]{:S(2)}, u32[]{:S(2)}) collective-permute-start(f32[192,256]{1,0:T(8,128)S(1)} %add.150), channel_id=1, source_target_pairs={{0,4},{1,5},{2,6},{3,7},{4,0},{5,1},{6,2},{7,3},{8,12},{9,13},{10,... | collective-permute-start | bytes 589832 | tf_op jit(solution)/shard_map/ppermute | solution.py:391
  199.5 20.9 %collective-permute-start.47 = (bf16[14,128,128]{2,1,0:T(8,128)(2,1)}, bf16[14,128,128]{2,1,0:T(8,128)(2,1)}, u32[]{:S(2)}, u32[]{:S(2)}) collective-permute-start(bf16[14,128,128]{2,1,0:T(8,128)(2,1)} %collective-permute-done.33.refs_12_), channel_id=1, source_target_pairs={{0,8},{8,0},{16,24},{24,16},{1,9},{9,1},{17,25},{25,17},{2,10},{10... | collective-permute-start | bytes 1376264 | tf_op jit(solution)/shard_map/ppermute | solution.py:26
  209.9 7.5 %collective-permute-start.37 = (bf16[7,128,128]{2,1,0:T(8,128)(2,1)S(1)}, bf16[7,128,128]{2,1,0:T(8,128)(2,1)S(1)}, u32[]{:S(2)}, u32[]{:S(2)}) collective-permute-start(bf16[7,128,128]{2,1,0:T(8,128)(2,1)S(1)} %slice.25), channel_id=1, source_target_pairs={{0,1},{1,0},{2,3},{3,2},{4,5},{5,4},{6,7},{7,6},{8,9},{9,8},{10,11... | collective-permute-start | bytes 688136 | tf_op jit(solution)/shard_map/ppermute | solution.py:44
  211.0 9.2 %collective-permute-start.38 = (bf16[7,128,128]{2,1,0:T(8,128)(2,1)S(1)}, bf16[7,128,128]{2,1,0:T(8,128)(2,1)}, u32[]{:S(2)}, u32[]{:S(2)}) collective-permute-start(bf16[7,128,128]{2,1,0:T(8,128)(2,1)S(1)} %slice.26), channel_id=1, source_target_pairs={{0,2},{1,3},{2,4},{3,5},{4,6},{5,7},{6,0},{7,1},{8,10},{9,11},{10,... | collective-permute-start | bytes 688136 | tf_op jit(solution)/shard_map/ppermute | solution.py:38
  211.1 16.9 %collective-permute-start.39 = (bf16[14,128,128]{2,1,0:T(8,128)(2,1)S(1)}, bf16[14,128,128]{2,1,0:T(8,128)(2,1)}, u32[]{:S(2)}, u32[]{:S(2)}) collective-permute-start(bf16[14,128,128]{2,1,0:T(8,128)(2,1)S(1)} %collective-permute-done.35.refs_12_), channel_id=1, source_target_pairs={{0,8},{8,0},{16,24},{24,16},{1,9},{9,1},{17,25},{25,17},{2,10},{10... | collective-permute-start | bytes 1376264 | tf_op jit(solution)/shard_map/ppermute | solution.py:26
  211.2 16.9 %collective-permute-start.40 = (bf16[14,128,128]{2,1,0:T(8,128)(2,1)S(1)}, bf16[14,128,128]{2,1,0:T(8,128)(2,1)}, u32[]{:S(2)}, u32[]{:S(2)}) collective-permute-start(bf16[14,128,128]{2,1,0:T(8,128)(2,1)S(1)} %collective-permute-done.36.refs_13_), channel_id=1, source_target_pairs={{0,8},{8,0},{16,24},{24,16},{1,9},{9,1},{17,25},{25,17},{2,10},{10... | collective-permute-start | bytes 1376264 | tf_op jit(solution)/shard_map/ppermute | solution.py:26
  217.5 10.5 %collective-permute-start.41 = (bf16[7,128,128]{2,1,0:T(8,128)(2,1)S(1)}, bf16[7,128,128]{2,1,0:T(8,128)(2,1)}, u32[]{:S(2)}, u32[]{:S(2)}) collective-permute-start(bf16[7,128,128]{2,1,0:T(8,128)(2,1)S(1)} %collective-permute-done.37.refs_14_), channel_id=1, source_target_pairs={{0,8},{8,0},{16,24},{24,16},{1,9},{9,1},{17,25},{25,17},{2,10},{10... | collective-permute-start | bytes 688136 | tf_op jit(solution)/shard_map/ppermute | solution.py:26
  220.2 7.8 %collective-permute-start.42 = (bf16[7,128,128]{2,1,0:T(8,128)(2,1)}, bf16[7,128,128]{2,1,0:T(8,128)(2,1)}, u32[]{:S(2)}, u32[]{:S(2)}) collective-permute-start(bf16[7,128,128]{2,1,0:T(8,128)(2,1)} %collective-permute-done.38.refs_15_), channel_id=1, source_target_pairs={{0,8},{8,0},{16,24},{24,16},{1,9},{9,1},{17,25},{25,17},{2,10},{10... | collective-permute-start | bytes 688136 | tf_op jit(solution)/shard_map/ppermute | solution.py:26
  220.4 14.8 %collective-permute-start.54 = (f32[192,256]{1,0:T(8,128)S(1)}, f32[192,256]{1,0:T(8,128)S(1)}, u32[]{:S(2)}, u32[]{:S(2)}) collective-permute-start(f32[192,256]{1,0:T(8,128)S(1)} %add.151), channel_id=1, source_target_pairs={{0,16},{8,24},{16,0},{24,8},{1,17},{9,25},{17,1},{25,9},{2,18},{10... | collective-permute-start | bytes 589832 | tf_op jit(solution)/shard_map/ppermute | solution.py:22
  233.9 23.2 %collective-permute-start.48 = (bf16[3584,128]{1,0:T(8,128)(2,1)}, bf16[3584,128]{1,0:T(8,128)(2,1)S(1)}, u32[]{:S(2)}, u32[]{:S(2)}) collective-permute-start(bf16[3584,128]{1,0:T(8,128)(2,1)} %shard_map.132.refs_1_), channel_id=1, source_target_pairs={{0,16},{8,24},{16,0},{24,8},{1,17},{9,25},{17,1},{25,9},{2,18},{10... | collective-permute-start | bytes 2752520 | tf_op jit(solution)/shard_map/ppermute | solution.py:22
  236.1 2.6 collective-permute-start.55
  238.8 20.8 %collective-permute-start.49 = (bf16[3584,128]{1,0:T(8,128)(2,1)S(1)}, bf16[3584,128]{1,0:T(8,128)(2,1)S(1)}, u32[]{:S(2)}, u32[]{:S(2)}) collective-permute-start(bf16[3584,128]{1,0:T(8,128)(2,1)S(1)} %copy-done.11), channel_id=1, source_target_pairs={{0,8},{8,0},{16,24},{24,16},{1,9},{9,1},{17,25},{25,17},{2,10},{10... | collective-permute-start | bytes 2752520 | tf_op jit(solution)/shard_map/ppermute | solution.py:26
  257.1 2.5 collective-permute-start.50
  (39 other events, 518.7 us)

commit v3 on v2

v3 whole, which is shorter than its diff:
```python
import functools

import jax
import jax.numpy as jnp
from jax import lax
from jax.experimental import pallas as pl
from jax.experimental.pallas import tpu as pltpu
from jax.sharding import PartitionSpec as P

BF = jnp.bfloat16
F32 = jnp.float32
META = 16
CORES = 2


def dims(wide, narrow):
    z = 4 if narrow % 4 == 0 else 1
    return wide // CORES, z, narrow // z


def x_shift(a, k, wide):
    return lax.ppermute(a, "wide", [(i, (i + CORES * k) % wide) for i in range(wide)])


def core_swap(a, wide):
    return lax.ppermute(a, "wide", [(i, i ^ 1) for i in range(wide)])


def z_shift(a, k, zs, ys):
    return lax.ppermute(
        a, "narrow", [(z * ys + y, (z + k) % zs * ys + y) for z in range(zs) for y in range(ys)]
    )


def y_shift(a, k, zs, ys):
    return lax.ppermute(
        a, "narrow", [(z * ys + y, z * ys + (y + k) % ys) for z in range(zs) for y in range(ys)]
    )


def after(a, *others):
    return lax.optimization_barrier((a,) + others)[0]


def aggregate_kernel(wide, cap, side, blocks, layout, scal, *refs):
    qs = range(layout["narrow"])
    half = blocks // CORES
    refs = list(refs)
    arrays = [refs.pop(0) for _ in range(layout["arrays"])]
    row_sets, col_sets = layout["rows"], layout["cols"]
    out_ref, tiles, feats, acc, facts_v, facts_s, tile_sem, feat_sem, sem = refs

    def take(place):
        at, index = place
        return arrays[at] if index is None else arrays[at].at[index]

    def col_copy(n, w):
        part, start = layout["where"][n]
        return pltpu.make_async_copy(
            take(col_sets[w][part]).at[start],
            tiles.at[n * wide + w],
            tile_sem.at[n * wide + w],
        )

    @pl.when(scal[0] == 0)
    def _():
        for n in range(len(qs)):
            owner = scal[2 + n]
            for w in range(wide):
                low, high = (take(r) for r in row_sets[w])
                into, done = tiles.at[n * wide + w], tile_sem.at[n * wide + w]
                if row_sets[w][0] == row_sets[w][1]:
                    pltpu.make_async_copy(low.at[owner], into, done).start()
                else:
                    split = len(qs) // 2

                    @pl.when(owner < split)
                    def _():
                        pltpu.make_async_copy(low.at[owner], into, done).start()

                    @pl.when(owner >= split)
                    def _():
                        pltpu.make_async_copy(high.at[owner - split], into, done).start()

    @pl.when(scal[0] != 0)
    def _():
        for n in range(len(qs)):
            for w in range(wide):
                col_copy(n, w).start()

    copies = []
    for n in range(len(qs)):
        here = []
        for h, group in enumerate(layout["feats"][n]):
            size = half // len(group)
            for e, place in enumerate(group):
                source = take(place)
                copy = pltpu.make_async_copy(
                    source,
                    feats.at[pl.ds(n * blocks + h * half + e * size, size)],
                    feat_sem.at[(n * CORES + h) * 2 + e],
                )
                copy.start()
                here.append(copy)
        copies.append(here)
    acc[...] = jnp.zeros_like(acc)
    for n in range(len(qs)):
        for w in range(wide):
            col_copy(n, w).wait()
    core = scal[0]
    facts = tiles[:, cap * side : cap * side + META, :].astype(F32)
    row = facts[:, 0, :].astype(jnp.int32)
    source = facts[:, 1, :].astype(jnp.int32)
    alive = facts[:, 2, :] > 0.5
    to_block = jnp.where(core == 0, row, source)
    from_block = jnp.where(core == 0, source, row)
    upper = (from_block >= half).astype(jnp.int32)
    facts_v[0] = jnp.where(alive, to_block, blocks)
    facts_v[1] = from_block - upper * half + jnp.where(upper == core, 0, half)
    scalars = pltpu.make_async_copy(facts_v, facts_s, sem.at[0])
    scalars.start()
    scalars.wait()
    for n in range(len(qs)):
        for copy in copies[n]:
            copy.wait()
        for w in range(wide):
            t = n * wide + w
            terms = []
            for i in range(cap):
                terms.append(
                    jnp.dot(
                        tiles[t, i * side : (i + 1) * side, :],
                        feats[n * blocks + facts_s[1, t, i]],
                        preferred_element_type=F32,
                    )
                )
            for i in range(cap):
                to = facts_s[0, t, i]
                acc[to] = acc[to] + terms[i]
    for b in range(blocks):
        out_ref[b * side : (b + 1) * side, :] = acc[b].astype(BF)


def aggregate(scal, row_sets, col_sets, where, mine, other, blocks, side, cap):
    wide, narrow = len(row_sets), len(mine)
    qs = range(narrow)
    width = mine[0][0][0].shape[-1]
    arrays = []

    def place(array, index):
        for at, known in enumerate(arrays):
            if known is array:
                return at, index
        arrays.append(array)
        return len(arrays) - 1, index

    layout = dict(
        rows=[[place(a, None) for a in r] for r in row_sets],
        cols=[[place(a, None) for a in c] for c in col_sets],
        where=where,
        feats=[[[place(*p) for p in group] for group in (mine[q], other[q])] for q in qs],
        narrow=narrow,
    )
    layout["arrays"] = len(arrays)
    operands = list(arrays)
    count = len(qs) * wide
    shape = jax.ShapeDtypeStruct((blocks * side, width), BF)
    flops = 2 * count * cap * side * side * width
    return pl.pallas_call(
        functools.partial(aggregate_kernel, wide, cap, side, blocks, layout),
        out_shape=shape,
        in_specs=[pl.BlockSpec(memory_space=pltpu.SMEM)]
        + [pl.BlockSpec(memory_space=pl.ANY)] * len(operands),
        out_specs=pl.BlockSpec(memory_space=pltpu.VMEM),
        scratch_shapes=[
            pltpu.VMEM((count,) + row_sets[0][0].shape[-2:], BF),
            pltpu.VMEM((len(qs) * blocks, side, width), BF),
            pltpu.VMEM((blocks + 1, side, width), F32),
            pltpu.VMEM((2, count, side), jnp.int32),
            pltpu.SMEM((2, count, side), jnp.int32),
            pltpu.SemaphoreType.DMA((count,)),
            pltpu.SemaphoreType.DMA((len(qs) * CORES * 2,)),
            pltpu.SemaphoreType.DMA((1,)),
        ],
        compiler_params=pltpu.CompilerParams(vmem_limit_bytes=58 << 20),
        cost_estimate=pl.CostEstimate(
            flops=flops, bytes_accessed=count * cap * side * side * 6, transcendentals=0
        ),
    )(scal, *operands)


def fill_weights(scal, refs, scratch, cols, across):
    self_ref, out_ref, in_ref = refs
    width = self_ref.shape[0]
    xs = width // cols
    core, chip = scal[0], scal[1]

    def put(at, value):
        if across:
            scratch[:, at : at + value.shape[1]] = value
        else:
            scratch[at : at + value.shape[0], :] = value

    put(0, self_ref[...])
    for d in range(CORES):
        for k in range(xs):
            rank = lax.rem(chip - k + xs, xs)
            out_w, in_w = out_ref[0], in_ref[0]
            for e in range(1, xs):
                out_w = jnp.where(rank == e, out_ref[e], out_w)
                in_w = jnp.where(rank == e, in_ref[e], in_w)
            use_out = (core == 0) == (d == 0)
            put(width + (d * xs + k) * cols, jnp.where(use_out, out_w, in_w))


def dense_kernel(parts, outs, cols, chunks, across, scal, *refs):
    refs = list(refs)
    count = parts + outs - 1
    ins = [refs.pop(0) for _ in range(count)]
    weights = [refs.pop(0) for _ in range(3)]
    results = [refs.pop(0) for _ in range(outs)]
    here = [refs.pop(0) for _ in range(count)]
    made = [refs.pop(0) for _ in range(outs)]
    scratch, in_sem, out_sem = refs
    step = here[0].shape[0] // chunks

    def rows(c):
        return pl.ds(c * step, step)

    def load(c, i):
        return pltpu.make_async_copy(
            ins[i].at[rows(c)], here[i].at[rows(c)], in_sem.at[c * count + i]
        )

    def save(c, i):
        return pltpu.make_async_copy(
            made[i].at[rows(c)], results[i].at[rows(c)], out_sem.at[c * outs + i]
        )

    for c in range(chunks):
        for i in range(count):
            load(c, i).start()
    fill_weights(scal, weights, scratch, cols, across)
    dims_ = (((1,), (1 if across else 0,)), ((), ()))
    for c in range(chunks):
        for i in range(count):
            load(c, i).wait()
        both = jnp.concatenate([h[rows(c), :] for h in here[:parts]], axis=1)
        pre = lax.dot_general(both, scratch[...], dims_, preferred_element_type=F32)
        if outs == 1:
            made[0][rows(c), :] = pre.astype(BF)
        else:
            sigma = 1.0 / (1.0 + jnp.exp(-pre))
            made[0][rows(c), :] = (pre * sigma).astype(BF)
            slope = here[parts][rows(c), :].astype(F32) * sigma * (1.0 + pre * (1.0 - sigma))
            made[1][rows(c), :] = slope.astype(BF)
        for i in range(outs):
            save(c, i).start()
    for c in range(chunks):
        for i in range(outs):
            save(c, i).wait()


def whole(a):
    return pl.BlockSpec(a.shape, lambda: (0,) * a.ndim)


def dense(scal, ins, weights, cols, chunks, outs, across):
    rows, width = ins[0].shape
    xs = width // cols
    if across:
        split = [w.reshape(width, xs, cols).swapaxes(0, 1) for w in weights[1:]]
        scratch = (width, width * (1 + CORES))
    else:
        split = [w.reshape(xs, cols, width) for w in weights[1:]]
        scratch = (width * (1 + CORES), width)
    weights = [weights[0]] + split
    shape = jax.ShapeDtypeStruct((rows, width), BF)
    any_spec = pl.BlockSpec(memory_space=pl.ANY)
    result = pl.pallas_call(
        functools.partial(dense_kernel, 1 + CORES * xs, outs, cols, chunks, across),
        out_shape=(shape,) * outs,
        in_specs=[pl.BlockSpec(memory_space=pltpu.SMEM)]
        + [any_spec] * len(ins)
        + [whole(w) for w in weights],
        out_specs=(any_spec,) * outs,
        scratch_shapes=[pltpu.VMEM(a.shape, BF) for a in ins]
        + [pltpu.VMEM((rows, width), BF)] * outs
        + [
            pltpu.VMEM(scratch, BF),
            pltpu.SemaphoreType.DMA((chunks * len(ins),)),
            pltpu.SemaphoreType.DMA((chunks * outs,)),
        ],
        compiler_params=pltpu.CompilerParams(vmem_limit_bytes=58 << 20),
    )(scal, *ins, *weights)
    return result if outs > 1 else result[0]


def body(node_feats, grad_out, tile_weight, tile_row, src_block, tile_count, w_self, w_out, w_in):
    wide, narrow = lax.axis_size("wide"), lax.axis_size("narrow")
    xs, zs, ys = dims(wide, narrow)
    slots = tile_row.shape[-1]
    cap = slots // narrow
    nodes, width = node_feats.shape
    side = tile_weight.shape[-1]
    blocks = nodes // side
    half = blocks // CORES
    cols = width // xs
    w_id, n_id = lax.axis_index("wide"), lax.axis_index("narrow")
    core, x_id = w_id % CORES, w_id // CORES
    z_id, y_id = n_id // ys, n_id % ys
    first = core == 0
    every = [(k, j) for k in range(zs) for j in range(ys)]

    def own_piece(a):
        piece = lax.dynamic_slice(a, (core * half * side, x_id * cols), (half * side, cols))
        return piece.reshape(half, side, cols)

    tiles = tile_weight.reshape(narrow, cap, side, side)
    live = jnp.arange(cap, dtype=jnp.int32)[None, :] < tile_count.reshape(narrow, 1)
    facts = jnp.stack(
        [
            tile_row.reshape(narrow, cap).astype(BF),
            src_block.reshape(narrow, cap).astype(BF),
            live.astype(BF),
        ],
        axis=1,
    )
    facts = jnp.pad(facts, ((0, 0), (0, META - 3), (0, side - cap)))

    def packed(t):
        return jnp.concatenate([t.reshape(narrow, cap * side, side), facts], axis=1)

    q = jnp.arange(narrow, dtype=jnp.int32)
    order = (z_id - q // ys) % zs * ys + (y_id - q % ys) % ys
    scal = jnp.concatenate([core.reshape(1), x_id.reshape(1), order]).astype(jnp.int32)

    def here(arrays):
        return [(a, None) for a in arrays]

    def swap(a, *ahead):
        return core_swap(after(a, *ahead), wide)

    def meet(a, bit):
        return lax.ppermute(a, "narrow", [(i, i ^ bit) for i in range(narrow)])

    def along_x(a, *ahead):
        return [x_shift(after(a, *ahead), k, wide) for k in range(1, xs)]

    own = own_piece(node_feats)
    z1 = z_shift(own, 1, zs, ys)
    row_own = packed(after(tiles, own))
    row_x0 = along_x(row_own[: narrow // 2], own)
    col_by_owner = packed(after(tiles, row_own).swapaxes(2, 3))
    col_by_owner = col_by_owner.reshape(zs, ys, cap * side + META, side)
    toward = [
        lax.dynamic_index_in_dim(col_by_owner, (y_id + j) % ys, 1, keepdims=False)
        for j in range(ys)
    ]
    moved = [y_shift(toward[j], j, zs, ys) for j in range(1, ys)]
    one = [z1] + moved + row_x0
    col_by_z = jnp.stack([toward[0]] + [after(m, *one) for m in moved], axis=1)

    def col_part(k, *ahead):
        part = lax.dynamic_index_in_dim(col_by_z, (z_id + k) % zs, 0, keepdims=False)
        return after(part, *ahead)

    s1 = z_shift(col_part(1, *one), 1, zs, ys)
    s3 = z_shift(col_part(3, *one), 3, zs, ys)
    y0 = y_shift(after(own, *one), 1, zs, ys)
    row_x1 = along_x(row_own[narrow // 2 :], *one)
    row_swap = swap(row_own, *one)
    two = [s1, s3, y0, row_swap] + row_x1
    z2 = z_shift(after(z1, *two), 1, zs, ys)
    y1 = y_shift(after(z1, *two), 1, zs, ys)
    near = jnp.concatenate([col_part(0, *one), s1], axis=0)
    near_x = along_x(near, *two)
    own_swap, z1_swap = swap(own, *two), swap(z1, *two)
    three = [z2, y1, own_swap, z1_swap] + near_x
    z3 = z_shift(after(z2, *three), 1, zs, ys)
    y2 = y_shift(after(z2, *three), 1, zs, ys)
    s3_x = along_x(s3, *three)
    y0_swap = swap(y0, *three)
    row_x0_swap = [swap(a, *three) for a in row_x0]
    four = [z3, y2, y0_swap] + s3_x + row_x0_swap
    y3 = y_shift(after(z3, *four), 1, zs, ys)
    s2 = z_shift(col_part(2, *four), 2, zs, ys)
    z2_swap, y1_swap = swap(z2, *four), swap(y1, *four)
    row_x1_swap = [swap(a, *four) for a in row_x1]
    five = [y3, s2, z2_swap, y1_swap] + row_x1_swap
    s2_x = along_x(s2, *five)
    z3_swap, y2_swap = swap(z3, *five), swap(y2, *five)
    near_swap = [swap(a, *five) for a in [near] + near_x]
    six = [z3_swap, y2_swap] + s2_x + near_swap
    y3_swap = swap(y3, *six)
    s3_swap = [swap(a, *six) for a in [s3] + s3_x]
    s2_swap = [swap(a, *six) for a in [s2] + s2_x]

    row_sets = [[row_own, row_own]] + [list(p) for p in zip(row_x0, row_x1)]
    row_sets += [[row_swap, row_swap]] + [list(p) for p in zip(row_x0_swap, row_x1_swap)]
    col_sets = [list(p) for p in zip([near] + near_x, [s3] + s3_x, [s2] + s2_x)]
    col_sets += [list(p) for p in zip(near_swap, s3_swap, s2_swap)]
    where = {}
    for i, (k, j) in enumerate(every):
        where[i] = {0: (0, i), 1: (0, i), 2: (2, j), 3: (1, j)}[k]

    def spread(pieces, swaps):
        for kj in every:
            if kj not in pieces:
                pieces[kj] = y_shift(pieces[kj[0], kj[1] - 1], 1, zs, ys)
            if kj not in swaps:
                swaps[kj] = core_swap(pieces[kj], wide)
        own = aggregate(
            scal, row_sets, col_sets, where, [here([pieces[kj]]) for kj in every],
            [here([swaps[kj]]) for kj in every], blocks, side, cap,
        )
        all_own = [own] + along_x(own)
        return own, all_own + [core_swap(p, wide) for p in all_own]

    names = [(0, 0), (1, 0), (2, 0), (3, 0), (0, 1), (1, 1), (2, 1), (3, 1)]
    agg, aggs = spread(
        dict(zip(names, [own, z1, z2, z3, y0, y1, y2, y3])),
        dict(zip(names, [own_swap, z1_swap, z2_swap, z3_swap, y0_swap, y1_swap, y2_swap, y3_swap])),
    )
    hidden, grad_pre = dense(
        scal, [node_feats] + aggs + [grad_out], [w_self, w_out, w_in], cols, 4, 2, False
    )

    own = own_piece(grad_pre)
    z1 = z_shift(own, 1, zs, ys)
    y0 = y_shift(own, 1, zs, ys)
    share = width // wide
    feat_part = lax.dynamic_slice(node_feats, (0, w_id * share), (nodes, share))
    grad_part = lax.dot_general(
        jnp.concatenate([agg, feat_part], axis=1),
        after(grad_pre, own),
        (((0,), (0,)), ((), ())),
        preferred_element_type=F32,
    )
    one = [z1, y0]
    z2 = z_shift(after(z1, *one), 1, zs, ys)
    y1 = y_shift(after(z1, *one), 1, zs, ys)
    upper = n_id % 2
    halves = after(grad_part, *one).reshape(2, -1, width)
    sent = lax.dynamic_index_in_dim(halves, 1 - upper, 0, keepdims=False)
    kept = lax.dynamic_index_in_dim(halves, upper, 0, keepdims=False)
    grad_half = kept + meet(sent, 1)
    own_swap, z1_swap = swap(own, *one), swap(z1, *one)
    two = [z2, y1, own_swap, z1_swap, grad_half]
    z3 = z_shift(after(z2, *two), 1, zs, ys)
    y2 = y_shift(after(z2, *two), 1, zs, ys)
    y0_swap, z2_swap = swap(y0, *two), swap(z2, *two)
    for bit in (2, 8):
        if bit < narrow:
            grad_half = grad_half + meet(after(grad_half, *two), bit)
    three = [z3, y2, y0_swap, z2_swap, grad_half]
    quarter = half // 2
    y3 = y_shift(after(z3, *three)[:quarter], 1, zs, ys)
    y3_rest = z_shift(after(y2, *three)[quarter:], 1, zs, ys)
    grad_half = grad_half + meet(after(grad_half, *three), 4)
    y1_swap, z3_swap = swap(y1, *three), swap(z3, *three)
    four = [y3, y3_rest, y1_swap, z3_swap, grad_half]
    y3 = jnp.concatenate([y3, y3_rest], axis=0)
    y2_swap, y3_swap = swap(y2, *four), swap(y3, *four)
    stack = jnp.stack([grad_half] + along_x(grad_half, *four))
    _, backs = spread(
        dict(zip(names, [own, z1, z2, z3, y0, y1, y2, y3])),
        dict(zip(names, [own_swap, z1_swap, z2_swap, z3_swap, y0_swap, y1_swap, y2_swap, y3_swap])),
    )
    there = meet(stack, 1)
    stack = jnp.concatenate(
        [jnp.where(upper == 1, there, stack), jnp.where(upper == 1, stack, there)], axis=1
    )
    stack = jnp.stack([stack, core_swap(stack, wide)])
    stack = jnp.where(first, stack, stack[::-1])
    if xs == 2:
        stack = jnp.where(x_id == 0, stack, stack[:, ::-1])
    else:
        stack = stack[:, (x_id - jnp.arange(xs)) % xs]
    agg_grads = stack[:, :, :cols].reshape(CORES, width, width)
    grad_ws = stack[:, :, cols:].swapaxes(0, 1).reshape(width, width)

    grad_feats = dense(scal, [grad_pre] + backs, [w_self, w_in, w_out], cols, 4, 1, True)
    return (hidden, grad_feats, grad_ws, agg_grads[0], agg_grads[1])


def solution(mesh):
    return jax.shard_map(
        body,
        mesh=mesh,
        in_specs=(
            P("narrow", None),
            P("narrow", None),
            P("wide", "narrow", None, None, None),
            P("wide", "narrow", None),
            P("wide", "narrow", None),
            P("wide", "narrow", None),
            P(),
            P(),
            P(),
        ),
        out_specs=(P("narrow", None), P("narrow", None), P(), P(), P()),
        check_vma=False,
    )
```

time: 270 us -> 258 us (0.956)
  Pallas kernels: 41.2 us -> 31.5 us
  starting transfers between devices: 45.3 us -> 41.4 us
  local copies, waits for them, and re-layouts: 12.1 us -> 14.9 us
    ppermute x9, waiting for transfers between devices: 37.9 us -> 0.39 us  [y_shift(): lax.ppermute(a, 'narrow', [(z * ys + y, z * ys + (y + k) % ys) for z in r...]
    ppermute x3 -> x8, waiting for transfers between devices: 38 us -> 59.7 us  [x_shift(): lax.ppermute(a, 'wide', [(i, (i + CORES * k) % wide) for i in range(wide)])]
    ppermute x12 -> x4, starting transfers between devices: 20.4 us -> 6.47 us  [meet(): return lax.ppermute(a, 'narrow', [(i, i ^ bit) for i in range(narrow)])]
    ppermute x10, waiting for transfers between devices: 56.2 us -> 64.7 us  [z_shift(): lax.ppermute(a, 'narrow', [(z * ys + y, (z + k) % zs * ys + y) for z in r...]
    pallas_call x4 -> x2, Pallas kernels: 25 us -> 16.6 us  [aggregate(): pl.pallas_call(functools.partial(aggregate_kernel, wide, cap, side, block...]
    ppermute x12 -> x4, waiting for transfers between devices: 26.7 us -> 33.4 us  [meet(): return lax.ppermute(a, 'narrow', [(i, i ^ bit) for i in range(narrow)])]
    ppermute x3 -> x8, starting transfers between devices: 2.81 us -> 8.25 us  [x_shift(): lax.ppermute(a, 'wide', [(i, (i + CORES * k) % wide) for i in range(wide)])]
    unnamed x105 -> x122, local copies, waits for them, and re-layouts: 5.62 us -> 7.56 us
  transfers between devices with their start and end apart: 56 -> 61, of which waited for: 20 -> 21; matrix products, arithmetic and copies ran while one was open for 2% -> 3% of each run, Pallas kernels for 7% -> 3%
where the time goes in v3:
time: 258 us
  waiting for transfers between devices  162 us (63%)
  starting transfers between devices  41.4 us (16%)
  Pallas kernels  31.5 us (12%)
  local copies, waits for them, and re-layouts  14.9 us (6%)
  other arithmetic  5.66 us (2%)
    ppermute x10, waiting for transfers between devices, z_shift(): lax.ppermute(a, 'narrow', [(z * ys + y, (z + k) % zs * ys + y) for z in r...  64.7 us
    ppermute x8, waiting for transfers between devices, x_shift(): lax.ppermute(a, 'wide', [(i, (i + CORES * k) % wide) for i in range(wide)])  59.7 us
    ppermute x4, waiting for transfers between devices, meet(): return lax.ppermute(a, 'narrow', [(i, i ^ bit) for i in range(narrow)])  33.4 us
    pallas_call x2, Pallas kernels, aggregate(): pl.pallas_call(functools.partial(aggregate_kernel, wide, cap, side, block...  16.6 us
    pallas_call x2, Pallas kernels, dense(): pl.pallas_call(functools.partial(dense_kernel, 1 + CORES * xs, outs, cols...  14.9 us
    ppermute x30, starting transfers between devices, core_swap(): return lax.ppermute(a, 'wide', [(i, i ^ 1) for i in range(wide)])  9.24 us
    ppermute x9, starting transfers between devices, y_shift(): lax.ppermute(a, 'narrow', [(z * ys + y, z * ys + (y + k) % ys) for z in r...  9.21 us
    ppermute x8, starting transfers between devices, x_shift(): lax.ppermute(a, 'wide', [(i, (i + CORES * k) % wide) for i in range(wide)])  8.25 us
  transfers between devices with their start and end apart: 61, of which 21 were waited for; matrix products, arithmetic and copies ran while one was open for 3% of the time, Pallas kernels for 3%

profile of v3, /device:TPU:0, one launch (start us, length us, event | category | flops | bytes accessed | tf_op | source)
XLA Modules:
  0.0 258.0 jit_solution(10154358315556172089)
XLA Ops:
  0.7 0.8 compare_convert_fusion
  1.5 0.7 convert_reduce_fusion
  2.3 1.8 dynamic_slice.36
  4.2 1.1 fusion.5
  5.3 2.9 %collective-permute-start = (bf16[4,528,128]{2,1,0:T(8,128)(2,1)}, bf16[4,528,128]{2,1,0:T(8,128)(2,1)}, u32[]{:S(2)}, u32[]{:S(2)}) collective-permute-start(bf16[4,528,128]{2,1,0:T(8,128)(2,1)} %get-tuple-element.54), channel_id=1, source_target_pairs={{0,16},{8,24},{16,0},{24,8},{1,17},{9,25},{17,1},{25,9},{2,18},{10... | collective-permute-start | bytes 1622024 | tf_op jit(solution)/shard_map/ppermute | solution.py:22
  8.3 0.7 copy.37
  9.0 0.9 fusion.6
  9.9 1.5 collective-permute-start.2
  11.4 1.6 collective-permute-start.1
  13.0 12.0 %collective-permute-done.1.refs_22_ = bf16[14,128,128]{2,1,0:T(8,128)(2,1)S(1)} collective-permute-done((bf16[14,128,128]{2,1,0:T(8,128)(2,1)S(1)}, bf16[14,128,128]{2,1,0:T(8,128)(2,1)S(1)}, u32[]{:S(2)}, u32[]{:S(2)}) %collective-permute-start.1) | collective-permute-done | bytes 458784 | tf_op jit(solution)/shard_map/ppermute | solution.py:30
  25.1 0.7 copy-done.36
  26.8 1.2 fusion.10
  28.1 0.6 collective-permute-start.5
  28.6 3.3 %collective-permute-start.6 = (bf16[2,528,128]{2,1,0:T(8,128)(2,1)S(1)}, bf16[2,528,128]{2,1,0:T(8,128)(2,1)S(1)}, u32[]{:S(2)}, u32[]{:S(2)}) collective-permute-start(bf16[2,528,128]{2,1,0:T(8,128)(2,1)S(1)} %get-tuple-element.60), channel_id=1, source_target_pairs={{0,6},{1,7},{2,0},{3,1},{4,2},{5,3},{6,4},{7,5},{8,14},{9,15},{10,... | collective-permute-start | bytes 811016 | tf_op jit(solution)/shard_map/ppermute | solution.py:30
  32.0 7.4 %collective-permute-done.5 = bf16[2,528,128]{2,1,0:T(8,128)(2,1)S(1)} collective-permute-done((bf16[2,528,128]{2,1,0:T(8,128)(2,1)S(1)}, bf16[2,528,128]{2,1,0:T(8,128)(2,1)S(1)}, u32[]{:S(2)}, u32[]{:S(2)}) %collective-permute-start.5) | collective-permute-done | bytes 270368 | tf_op jit(solution)/shard_map/ppermute | solution.py:30
  39.4 3.0 %collective-permute-done.6.refs_7_ = bf16[2,528,128]{2,1,0:T(8,128)(2,1)S(1)} collective-permute-done((bf16[2,528,128]{2,1,0:T(8,128)(2,1)S(1)}, bf16[2,528,128]{2,1,0:T(8,128)(2,1)S(1)}, u32[]{:S(2)}, u32[]{:S(2)}) %collective-permute-start.6) | collective-permute-done | bytes 270368 | tf_op jit(solution)/shard_map/ppermute | solution.py:30
  42.5 1.6 collective-permute-start.12
  44.0 1.5 collective-permute-start.8
  45.5 0.6 collective-permute-start.9
  46.6 10.4 %collective-permute-done.8.refs_26_ = bf16[14,128,128]{2,1,0:T(8,128)(2,1)S(1)} collective-permute-done((bf16[14,128,128]{2,1,0:T(8,128)(2,1)S(1)}, bf16[14,128,128]{2,1,0:T(8,128)(2,1)S(1)}, u32[]{:S(2)}, u32[]{:S(2)}) %collective-permute-start.8) | collective-permute-done | bytes 458784 | tf_op jit(solution)/shard_map/ppermute | solution.py:30
  57.4 0.9 copy-done.43
  59.0 1.0 collective-permute-start.17
  59.9 7.9 %collective-permute-done.17.refs_10_ = bf16[2,528,128]{2,1,0:T(8,128)(2,1)S(1)} collective-permute-done((bf16[2,528,128]{2,1,0:T(8,128)(2,1)S(1)}, bf16[2,528,128]{2,1,0:T(8,128)(2,1)S(1)}, u32[]{:S(2)}, u32[]{:S(2)}) %collective-permute-start.17) | collective-permute-done | bytes 270368 | tf_op jit(solution)/shard_map/ppermute | solution.py:22
  67.8 5.2 %collective-permute-done.14.refs_30_ = bf16[14,128,128]{2,1,0:T(8,128)(2,1)S(1)} collective-permute-done((bf16[14,128,128]{2,1,0:T(8,128)(2,1)S(1)}, bf16[14,128,128]{2,1,0:T(8,128)(2,1)S(1)}, u32[]{:S(2)}, u32[]{:S(2)}) %collective-permute-start.14) | collective-permute-done | bytes 458784 | tf_op jit(solution)/shard_map/ppermute | solution.py:30
  74.1 14.2 %collective-permute-done.19.refs_8_ = bf16[2,528,128]{2,1,0:T(8,128)(2,1)S(1)} collective-permute-done((bf16[2,528,128]{2,1,0:T(8,128)(2,1)S(1)}, bf16[2,528,128]{2,1,0:T(8,128)(2,1)S(1)}, u32[]{:S(2)}, u32[]{:S(2)}) %collective-permute-start.19) | collective-permute-done | bytes 270368 | tf_op jit(solution)/shard_map/ppermute | solution.py:30
  90.1 7.9 %collective-permute-done.23.refs_11_ = bf16[2,528,128]{2,1,0:T(8,128)(2,1)S(1)} collective-permute-done((bf16[2,528,128]{2,1,0:T(8,128)(2,1)S(1)}, bf16[2,528,128]{2,1,0:T(8,128)(2,1)S(1)}, u32[]{:S(2)}, u32[]{:S(2)}) %collective-permute-start.23) | collective-permute-done | bytes 270368 | tf_op jit(solution)/shard_map/ppermute | solution.py:22
  101.8 0.7 copy-done.24
  102.6 8.3 %shard_map.128.refs_1_ = bf16[3584,128]{1,0:T(8,128)(2,1)} custom-call(s32[10]{0:T(128)} %pad_add_fusion.scal, bf16[8,528,128]{2,1,0:T(8,128)(2,1)} %copy-done, bf16[4,528,128]{2,1,0:T(8,128)(2,1)} %collective-permute-done.refs_1_, bf16[4,528,128]{2,1,0:T(8,128)(2,1)} %copy-done.8, bf16[8,528,128]{2,1,0:T(8,128)(2,1)} %copy-done.3, ...), custom_call_target="tpu_custom_call" | custom-call | flops 536870912 | bytes 12582912 | tf_op jit(solution)/shard_map/pallas_call | solution.py:169
  111.0 0.6 collective-permute-start.33
  111.6 1.8 collective-permute-start.34
  113.4 20.0 %collective-permute-done.33.refs_2_ = bf16[3584,128]{1,0:T(8,128)(2,1)S(1)} collective-permute-done((bf16[3584,128]{1,0:T(8,128)(2,1)}, bf16[3584,128]{1,0:T(8,128)(2,1)S(1)}, u32[]{:S(2)}, u32[]{:S(2)}) %collective-permute-start.33) | collective-permute-done | bytes 917536 | tf_op jit(solution)/shard_map/ppermute | solution.py:22
  133.4 0.9 collective-permute-start.35
  134.3 2.1 collective-permute-done.35.refs_4_
  136.4 1.0 copy-done.32
  137.4 8.0 %shard_map.129 = (bf16[3584,256]{1,0:T(8,128)(2,1)}, bf16[3584,256]{1,0:T(8,128)(2,1)}) custom-call(s32[10]{0:T(128)} %pad_add_fusion.scal, bf16[3584,256]{1,0:T(8,128)(2,1)} %refs_0_.1, bf16[3584,128]{1,0:T(8,128)(2,1)} %shard_map.128.refs_1_, bf16[3584,128]{1,0:T(8,128)(2,1)} %copy-done.30, bf16[3584,128]{1,0:T(8,128)(2,1)} %copy-done.31, ...), custom_call_target="tpu_custom_call" | custom-call | tf_op jit(solution)/shard_map/pallas_call | solution.py:280
  145.4 1.2 dynamic_slice.43
  146.7 1.8 collective-permute-start.37
  148.8 12.4 %collective-permute-done.36.refs_22_ = bf16[14,128,128]{2,1,0:T(8,128)(2,1)S(1)} collective-permute-done((bf16[14,128,128]{2,1,0:T(8,128)(2,1)S(1)}, bf16[14,128,128]{2,1,0:T(8,128)(2,1)S(1)}, u32[]{:S(2)}, u32[]{:S(2)}) %collective-permute-start.36) | collective-permute-done | bytes 458784 | tf_op jit(solution)/shard_map/ppermute | solution.py:30
  161.3 1.8 collective-permute-start.40
  163.6 0.7 fusion
  164.7 10.8 %collective-permute-done.42 = f32[96,256]{1,0:T(8,128)S(1)} collective-permute-done((f32[96,256]{1,0:T(8,128)S(1)}, f32[96,256]{1,0:T(8,128)S(1)}, u32[]{:S(2)}, u32[]{:S(2)}) %collective-permute-start.42) | collective-permute-done | bytes 98336 | tf_op jit(solution)/shard_map/ppermute | solution.py:345
  175.6 0.7 collective-permute-start.44
  176.3 1.7 collective-permute-start.45
  178.0 1.7 collective-permute-start.47
  179.7 12.9 %collective-permute-done.47 = f32[96,256]{1,0:T(8,128)S(1)} collective-permute-done((f32[96,256]{1,0:T(8,128)S(1)}, f32[96,256]{1,0:T(8,128)S(1)}, u32[]{:S(2)}, u32[]{:S(2)}) %collective-permute-start.47) | collective-permute-done | bytes 98336 | tf_op jit(solution)/shard_map/ppermute | solution.py:345
  192.8 0.7 collective-permute-start.49
  194.1 3.3 %collective-permute-start.52 = (f32[96,256]{1,0:T(8,128)S(1)}, f32[96,256]{1,0:T(8,128)S(1)}, u32[]{:S(2)}, u32[]{:S(2)}) collective-permute-start(f32[96,256]{1,0:T(8,128)S(1)} %add.136), channel_id=1, source_target_pairs={{0,4},{1,5},{2,6},{3,7},{4,0},{5,1},{6,2},{7,3},{8,12},{9,13},{10,... | collective-permute-start | bytes 294920 | tf_op jit(solution)/shard_map/ppermute | solution.py:345
  197.4 9.7 %collective-permute-done.52 = f32[96,256]{1,0:T(8,128)S(1)} collective-permute-done((f32[96,256]{1,0:T(8,128)S(1)}, f32[96,256]{1,0:T(8,128)S(1)}, u32[]{:S(2)}, u32[]{:S(2)}) %collective-permute-start.52) | collective-permute-done | bytes 98336 | tf_op jit(solution)/shard_map/ppermute | solution.py:345
  208.3 4.3 %collective-permute-done.58 = f32[96,256]{1,0:T(8,128)S(1)} collective-permute-done((f32[96,256]{1,0:T(8,128)S(1)}, f32[96,256]{1,0:T(8,128)S(1)}, u32[]{:S(2)}, u32[]{:S(2)}) %collective-permute-start.58) | collective-permute-done | bytes 98336 | tf_op jit(solution)/shard_map/ppermute | solution.py:22
  212.6 1.1 collective-permute-start.59
  213.8 0.8 copy-done.57
  214.6 0.8 copy-done.58
  215.3 8.2 %shard_map.130.refs_1_ = bf16[3584,128]{1,0:T(8,128)(2,1)} custom-call(s32[10]{0:T(128)} %pad_add_fusion.scal, bf16[8,528,128]{2,1,0:T(8,128)(2,1)} %copy-done, bf16[4,528,128]{2,1,0:T(8,128)(2,1)} %collective-permute-done.refs_1_, bf16[4,528,128]{2,1,0:T(8,128)(2,1)} %copy-done.8, bf16[8,528,128]{2,1,0:T(8,128)(2,1)} %copy-done.3, ...), custom_call_target="tpu_custom_call" | custom-call | flops 536870912 | bytes 12582912 | tf_op jit(solution)/shard_map/pallas_call | solution.py:169
  223.6 0.6 collective-permute-start.55
  224.3 0.7 collective-permute-start.60
  225.3 0.8 copy.39
  226.1 0.7 copy.41
  226.8 0.6 collective-permute-start.56
  227.5 19.6 %collective-permute-done.55.refs_2_ = bf16[3584,128]{1,0:T(8,128)(2,1)S(1)} collective-permute-done((bf16[3584,128]{1,0:T(8,128)(2,1)}, bf16[3584,128]{1,0:T(8,128)(2,1)S(1)}, u32[]{:S(2)}, u32[]{:S(2)}) %collective-permute-start.55) | collective-permute-done | bytes 917536 | tf_op jit(solution)/shard_map/ppermute | solution.py:22
  247.3 0.7 copy-done.28
  248.0 0.7 copy.42
  248.8 0.8 fusion.34
  249.6 0.9 copy-done.29
  250.9 6.9 %shard_map.131 = bf16[3584,256]{1,0:T(8,128)(2,1)} custom-call(s32[10]{0:T(128)} %pad_add_fusion.scal, bf16[3584,256]{1,0:T(8,128)(2,1)} %get-tuple-element.89.refs_0_, bf16[3584,128]{1,0:T(8,128)(2,1)} %shard_map.130.refs_1_, bf16[3584,128]{1,0:T(8,128)(2,1)} %copy-done.28, bf16[3584,128]{1,0:T(8,128)(2,1)} %copy-done.29, bf16[3584,128]{1,0:T(8,128)(2,1)} %copy-done.33, ...), custom_call_target="tpu_custom_call" | custom-call | tf_op jit(solution)/shard_map/pallas_call | solution.py:280
  (219 shorter events, 13.7 us)
Async XLA Ops:
  5.3 19.7 %collective-permute-start = (bf16[4,528,128]{2,1,0:T(8,128)(2,1)}, bf16[4,528,128]{2,1,0:T(8,128)(2,1)}, u32[]{:S(2)}, u32[]{:S(2)}) collective-permute-start(bf16[4,528,128]{2,1,0:T(8,128)(2,1)} %get-tuple-element.54), channel_id=1, source_target_pairs={{0,16},{8,24},{16,0},{24,8},{1,17},{9,25},{17,1},{25,9},{2,18},{10... | collective-permute-start | bytes 1622024 | tf_op jit(solution)/shard_map/ppermute | solution.py:22
  9.9 15.1 %collective-permute-start.2 = (bf16[4,528,128]{2,1,0:T(8,128)(2,1)S(1)}, bf16[4,528,128]{2,1,0:T(8,128)(2,1)S(1)}, u32[]{:S(2)}, u32[]{:S(2)}) collective-permute-start(bf16[4,528,128]{2,1,0:T(8,128)(2,1)S(1)} %get-tuple-element.106), channel_id=1, source_target_pairs={{0,1},{1,0},{2,3},{3,2},{4,5},{5,4},{6,7},{7,6},{8,9},{9,8},{10,11... | collective-permute-start | bytes 1622024 | tf_op jit(solution)/shard_map/ppermute | solution.py:36
  11.4 13.6 %collective-permute-start.1 = (bf16[14,128,128]{2,1,0:T(8,128)(2,1)S(1)}, bf16[14,128,128]{2,1,0:T(8,128)(2,1)S(1)}, u32[]{:S(2)}, u32[]{:S(2)}) collective-permute-start(bf16[14,128,128]{2,1,0:T(8,128)(2,1)S(1)} %bitcast.49), channel_id=1, source_target_pairs={{0,2},{1,3},{2,4},{3,5},{4,6},{5,7},{6,0},{7,1},{8,10},{9,11},{10,... | collective-permute-start | bytes 1376264 | tf_op jit(solution)/shard_map/ppermute | solution.py:30
  25.0 17.4 %collective-permute-start.4 = (bf16[8,528,128]{2,1,0:T(8,128)(2,1)S(1)}, bf16[8,528,128]{2,1,0:T(8,128)(2,1)S(1)}, u32[]{:S(2)}, u32[]{:S(2)}) collective-permute-start(bf16[8,528,128]{2,1,0:T(8,128)(2,1)S(1)} %pad_maximum_fusion.refs_0_), channel_id=1, source_target_pairs={{0,8},{8,0},{16,24},{24,16},{1,9},{9,1},{17,25},{25,17},{2,10},{10... | collective-permute-start | bytes 3244040 | tf_op jit(solution)/shard_map/ppermute | solution.py:26
  25.8 16.7 %collective-permute-start.3 = (bf16[4,528,128]{2,1,0:T(8,128)(2,1)}, bf16[4,528,128]{2,1,0:T(8,128)(2,1)S(1)}, u32[]{:S(2)}, u32[]{:S(2)}) collective-permute-start(bf16[4,528,128]{2,1,0:T(8,128)(2,1)} %get-tuple-element.56), channel_id=1, source_target_pairs={{0,16},{8,24},{16,0},{24,8},{1,17},{9,25},{17,1},{25,9},{2,18},{10... | collective-permute-start | bytes 1622024 | tf_op jit(solution)/shard_map/ppermute | solution.py:22
  26.3 16.1 %collective-permute-start.7 = (bf16[14,128,128]{2,1,0:T(8,128)(2,1)}, bf16[14,128,128]{2,1,0:T(8,128)(2,1)S(1)}, u32[]{:S(2)}, u32[]{:S(2)}) collective-permute-start(bf16[14,128,128]{2,1,0:T(8,128)(2,1)} %bitcast.47), channel_id=1, source_target_pairs={{0,1},{1,0},{2,3},{3,2},{4,5},{5,4},{6,7},{7,6},{8,9},{9,8},{10,11... | collective-permute-start | bytes 1376264 | tf_op jit(solution)/shard_map/ppermute | solution.py:36
  28.1 11.3 %collective-permute-start.5 = (bf16[2,528,128]{2,1,0:T(8,128)(2,1)S(1)}, bf16[2,528,128]{2,1,0:T(8,128)(2,1)S(1)}, u32[]{:S(2)}, u32[]{:S(2)}) collective-permute-start(bf16[2,528,128]{2,1,0:T(8,128)(2,1)S(1)} %get-tuple-element.59), channel_id=1, source_target_pairs={{0,2},{1,3},{2,4},{3,5},{4,6},{5,7},{6,0},{7,1},{8,10},{9,11},{10,... | collective-permute-start | bytes 811016 | tf_op jit(solution)/shard_map/ppermute | solution.py:30
  28.6 13.8 %collective-permute-start.6 = (bf16[2,528,128]{2,1,0:T(8,128)(2,1)S(1)}, bf16[2,528,128]{2,1,0:T(8,128)(2,1)S(1)}, u32[]{:S(2)}, u32[]{:S(2)}) collective-permute-start(bf16[2,528,128]{2,1,0:T(8,128)(2,1)S(1)} %get-tuple-element.60), channel_id=1, source_target_pairs={{0,6},{1,7},{2,0},{3,1},{4,2},{5,3},{6,4},{7,5},{8,14},{9,15},{10,... | collective-permute-start | bytes 811016 | tf_op jit(solution)/shard_map/ppermute | solution.py:30
  39.4 63.1 %copy-start.6 = (bf16[4,528,128]{2,1,0:T(8,128)(2,1)}, bf16[4,528,128]{2,1,0:T(8,128)(2,1)S(1)}, u32[]{:S(2)}) copy-start(bf16[4,528,128]{2,1,0:T(8,128)(2,1)S(1)} %constant_dynamic-update-slice_fusion.refs_6_) | copy-start | bytes 1622020
  42.4 60.1 %copy-start.17 = (bf16[2,528,128]{2,1,0:T(8,128)(2,1)}, bf16[2,528,128]{2,1,0:T(8,128)(2,1)S(1)}, u32[]{:S(2)}) copy-start(bf16[2,528,128]{2,1,0:T(8,128)(2,1)S(1)} %collective-permute-done.6.refs_7_) | copy-start | bytes 811012
  42.4 60.1 %copy-start.8 = (bf16[4,528,128]{2,1,0:T(8,128)(2,1)}, bf16[4,528,128]{2,1,0:T(8,128)(2,1)S(1)}, u32[]{:S(2)}) copy-start(bf16[4,528,128]{2,1,0:T(8,128)(2,1)S(1)} %collective-permute-done.3.refs_2_) | copy-start | bytes 1622020
  42.5 15.8 %collective-permute-start.12 = (bf16[4,528,128]{2,1,0:T(8,128)(2,1)S(1)}, bf16[4,528,128]{2,1,0:T(8,128)(2,1)S(1)}, u32[]{:S(2)}, u32[]{:S(2)}) collective-permute-start(bf16[4,528,128]{2,1,0:T(8,128)(2,1)S(1)} %constant_dynamic-update-slice_fusion.refs_6_), channel_id=1, source_target_pairs={{0,16},{8,24},{16,0},{24,8},{1,17},{9,25},{17,1},{25,9},{2,18},{10... | collective-permute-start | bytes 1622024 | tf_op jit(solution)/shard_map/ppermute | solution.py:22
  44.0 13.0 %collective-permute-start.8 = (bf16[14,128,128]{2,1,0:T(8,128)(2,1)S(1)}, bf16[14,128,128]{2,1,0:T(8,128)(2,1)S(1)}, u32[]{:S(2)}, u32[]{:S(2)}) collective-permute-start(bf16[14,128,128]{2,1,0:T(8,128)(2,1)S(1)} %copy-done.37), channel_id=1, source_target_pairs={{0,2},{1,3},{2,4},{3,5},{4,6},{5,7},{6,0},{7,1},{8,10},{9,11},{10,... | collective-permute-start | bytes 1376264 | tf_op jit(solution)/shard_map/ppermute | solution.py:30
  45.5 11.9 %collective-permute-start.9 = (bf16[14,128,128]{2,1,0:T(8,128)(2,1)S(1)}, bf16[14,128,128]{2,1,0:T(8,128)(2,1)S(1)}, u32[]{:S(2)}, u32[]{:S(2)}) collective-permute-start(bf16[14,128,128]{2,1,0:T(8,128)(2,1)S(1)} %copy-done.37), channel_id=1, source_target_pairs={{0,1},{1,0},{2,3},{3,2},{4,5},{5,4},{6,7},{7,6},{8,9},{9,8},{10,11... | collective-permute-start | bytes 1376264 | tf_op jit(solution)/shard_map/ppermute | solution.py:36
  46.1 11.3 %collective-permute-start.10 = (bf16[14,128,128]{2,1,0:T(8,128)(2,1)S(1)}, bf16[14,128,128]{2,1,0:T(8,128)(2,1)S(1)}, u32[]{:S(2)}, u32[]{:S(2)}) collective-permute-start(bf16[14,128,128]{2,1,0:T(8,128)(2,1)S(1)} %bitcast.50), channel_id=1, source_target_pairs={{0,8},{8,0},{16,24},{24,16},{1,9},{9,1},{17,25},{25,17},{2,10},{10... | collective-permute-start | bytes 1376264 | tf_op jit(solution)/shard_map/ppermute | solution.py:26
  46.1 11.3 %collective-permute-start.11 = (bf16[14,128,128]{2,1,0:T(8,128)(2,1)S(1)}, bf16[14,128,128]{2,1,0:T(8,128)(2,1)S(1)}, u32[]{:S(2)}, u32[]{:S(2)}) collective-permute-start(bf16[14,128,128]{2,1,0:T(8,128)(2,1)S(1)} %copy-done.37), channel_id=1, source_target_pairs={{0,8},{8,0},{16,24},{24,16},{1,9},{9,1},{17,25},{25,17},{2,10},{10... | collective-permute-start | bytes 1376264 | tf_op jit(solution)/shard_map/ppermute | solution.py:26
  58.3 14.8 %collective-permute-start.13 = (bf16[4,528,128]{2,1,0:T(8,128)(2,1)}, bf16[4,528,128]{2,1,0:T(8,128)(2,1)S(1)}, u32[]{:S(2)}, u32[]{:S(2)}) collective-permute-start(bf16[4,528,128]{2,1,0:T(8,128)(2,1)} %collective-permute-done.refs_1_), channel_id=1, source_target_pairs={{0,8},{8,0},{16,24},{24,16},{1,9},{9,1},{17,25},{25,17},{2,10},{10... | collective-permute-start | bytes 1622024 | tf_op jit(solution)/shard_map/ppermute | solution.py:26
  58.3 14.7 %collective-permute-start.14 = (bf16[14,128,128]{2,1,0:T(8,128)(2,1)S(1)}, bf16[14,128,128]{2,1,0:T(8,128)(2,1)S(1)}, u32[]{:S(2)}, u32[]{:S(2)}) collective-permute-start(bf16[14,128,128]{2,1,0:T(8,128)(2,1)S(1)} %collective-permute-done.8.refs_26_), channel_id=1, source_target_pairs={{0,2},{1,3},{2,4},{3,5},{4,6},{5,7},{6,0},{7,1},{8,10},{9,11},{10,... | collective-permute-start | bytes 1376264 | tf_op jit(solution)/shard_map/ppermute | solution.py:30
  58.8 14.2 %collective-permute-start.15 = (bf16[14,128,128]{2,1,0:T(8,128)(2,1)S(1)}, bf16[14,128,128]{2,1,0:T(8,128)(2,1)S(1)}, u32[]{:S(2)}, u32[]{:S(2)}) collective-permute-start(bf16[14,128,128]{2,1,0:T(8,128)(2,1)S(1)} %collective-permute-done.8.refs_26_), channel_id=1, source_target_pairs={{0,1},{1,0},{2,3},{3,2},{4,5},{5,4},{6,7},{7,6},{8,9},{9,8},{10,11... | collective-permute-start | bytes 1376264 | tf_op jit(solution)/shard_map/ppermute | solution.py:36
  58.9 14.1 %collective-permute-start.16 = (bf16[14,128,128]{2,1,0:T(8,128)(2,1)S(1)}, bf16[14,128,128]{2,1,0:T(8,128)(2,1)S(1)}, u32[]{:S(2)}, u32[]{:S(2)}) collective-permute-start(bf16[14,128,128]{2,1,0:T(8,128)(2,1)S(1)} %collective-permute-done.7.refs_20_), channel_id=1, source_target_pairs={{0,8},{8,0},{16,24},{24,16},{1,9},{9,1},{17,25},{25,17},{2,10},{10... | collective-permute-start | bytes 1376264 | tf_op jit(solution)/shard_map/ppermute | solution.py:26
  59.0 8.9 %collective-permute-start.17 = (bf16[2,528,128]{2,1,0:T(8,128)(2,1)S(1)}, bf16[2,528,128]{2,1,0:T(8,128)(2,1)S(1)}, u32[]{:S(2)}, u32[]{:S(2)}) collective-permute-start(bf16[2,528,128]{2,1,0:T(8,128)(2,1)S(1)} %collective-permute-done.6.refs_7_), channel_id=1, source_target_pairs={{0,16},{8,24},{16,0},{24,8},{1,17},{9,25},{17,1},{25,9},{2,18},{10... | collective-permute-start | bytes 811016 | tf_op jit(solution)/shard_map/ppermute | solution.py:22
  73.1 15.3 %collective-permute-start.18 = (bf16[4,528,128]{2,1,0:T(8,128)(2,1)S(1)}, bf16[4,528,128]{2,1,0:T(8,128)(2,1)S(1)}, u32[]{:S(2)}, u32[]{:S(2)}) collective-permute-start(bf16[4,528,128]{2,1,0:T(8,128)(2,1)S(1)} %collective-permute-done.3.refs_2_), channel_id=1, source_target_pairs={{0,8},{8,0},{16,24},{24,16},{1,9},{9,1},{17,25},{25,17},{2,10},{10... | collective-permute-start | bytes 1622024 | tf_op jit(solution)/shard_map/ppermute | solution.py:26
  73.2 15.2 %collective-permute-start.20 = (bf16[14,128,128]{2,1,0:T(8,128)(2,1)S(1)}, bf16[14,128,128]{2,1,0:T(8,128)(2,1)S(1)}, u32[]{:S(2)}, u32[]{:S(2)}) collective-permute-start(bf16[14,128,128]{2,1,0:T(8,128)(2,1)S(1)} %collective-permute-done.14.refs_30_), channel_id=1, source_target_pairs={{0,1},{1,0},{2,3},{3,2},{4,5},{5,4},{6,7},{7,6},{8,9},{9,8},{10,11... | collective-permute-start | bytes 1376264 | tf_op jit(solution)/shard_map/ppermute | solution.py:36
  73.5 14.9 %collective-permute-start.21 = (bf16[14,128,128]{2,1,0:T(8,128)(2,1)S(1)}, bf16[14,128,128]{2,1,0:T(8,128)(2,1)S(1)}, u32[]{:S(2)}, u32[]{:S(2)}) collective-permute-start(bf16[14,128,128]{2,1,0:T(8,128)(2,1)S(1)} %collective-permute-done.8.refs_26_), channel_id=1, source_target_pairs={{0,8},{8,0},{16,24},{24,16},{1,9},{9,1},{17,25},{25,17},{2,10},{10... | collective-permute-start | bytes 1376264 | tf_op jit(solution)/shard_map/ppermute | solution.py:26
  73.7 14.7 %collective-permute-start.22 = (bf16[14,128,128]{2,1,0:T(8,128)(2,1)S(1)}, bf16[14,128,128]{2,1,0:T(8,128)(2,1)S(1)}, u32[]{:S(2)}, u32[]{:S(2)}) collective-permute-start(bf16[14,128,128]{2,1,0:T(8,128)(2,1)S(1)} %collective-permute-done.9.refs_24_), channel_id=1, source_target_pairs={{0,8},{8,0},{16,24},{24,16},{1,9},{9,1},{17,25},{25,17},{2,10},{10... | collective-permute-start | bytes 1376264 | tf_op jit(solution)/shard_map/ppermute | solution.py:26
  74.1 14.2 %collective-permute-start.19 = (bf16[2,528,128]{2,1,0:T(8,128)(2,1)S(1)}, bf16[2,528,128]{2,1,0:T(8,128)(2,1)S(1)}, u32[]{:S(2)}, u32[]{:S(2)}) collective-permute-start(bf16[2,528,128]{2,1,0:T(8,128)(2,1)S(1)} %get-tuple-element.71), channel_id=1, source_target_pairs={{0,4},{1,5},{2,6},{3,7},{4,0},{5,1},{6,2},{7,3},{8,12},{9,13},{10,... | collective-permute-start | bytes 811016 | tf_op jit(solution)/shard_map/ppermute | solution.py:30
  88.5 9.6 %collective-permute-start.24 = (bf16[4,528,128]{2,1,0:T(8,128)(2,1)S(1)}, bf16[4,528,128]{2,1,0:T(8,128)(2,1)S(1)}, u32[]{:S(2)}, u32[]{:S(2)}) collective-permute-start(bf16[4,528,128]{2,1,0:T(8,128)(2,1)S(1)} %constant_dynamic-update-slice_fusion.refs_6_), channel_id=1, source_target_pairs={{0,8},{8,0},{16,24},{24,16},{1,9},{9,1},{17,25},{25,17},{2,10},{10... | collective-permute-start | bytes 1622024 | tf_op jit(solution)/shard_map/ppermute | solution.py:26
  88.5 9.5 %collective-permute-start.27 = (bf16[4,528,128]{2,1,0:T(8,128)(2,1)S(1)}, bf16[4,528,128]{2,1,0:T(8,128)(2,1)S(1)}, u32[]{:S(2)}, u32[]{:S(2)}) collective-permute-start(bf16[4,528,128]{2,1,0:T(8,128)(2,1)S(1)} %collective-permute-done.12.refs_9_), channel_id=1, source_target_pairs={{0,8},{8,0},{16,24},{24,16},{1,9},{9,1},{17,25},{25,17},{2,10},{10... | collective-permute-start | bytes 1622024 | tf_op jit(solution)/shard_map/ppermute | solution.py:26
  89.0 9.0 %collective-permute-start.25 = (bf16[14,128,128]{2,1,0:T(8,128)(2,1)S(1)}, bf16[14,128,128]{2,1,0:T(8,128)(2,1)S(1)}, u32[]{:S(2)}, u32[]{:S(2)}) collective-permute-start(bf16[14,128,128]{2,1,0:T(8,128)(2,1)S(1)} %collective-permute-done.14.refs_30_), channel_id=1, source_target_pairs={{0,8},{8,0},{16,24},{24,16},{1,9},{9,1},{17,25},{25,17},{2,10},{10... | collective-permute-start | bytes 1376264 | tf_op jit(solution)/shard_map/ppermute | solution.py:26
  89.1 8.9 %collective-permute-start.26 = (bf16[14,128,128]{2,1,0:T(8,128)(2,1)S(1)}, bf16[14,128,128]{2,1,0:T(8,128)(2,1)S(1)}, u32[]{:S(2)}, u32[]{:S(2)}) collective-permute-start(bf16[14,128,128]{2,1,0:T(8,128)(2,1)S(1)} %collective-permute-done.15.refs_28_), channel_id=1, source_target_pairs={{0,8},{8,0},{16,24},{24,16},{1,9},{9,1},{17,25},{25,17},{2,10},{10... | collective-permute-start | bytes 1376264 | tf_op jit(solution)/shard_map/ppermute | solution.py:26
  89.5 8.5 %collective-permute-start.23 = (bf16[2,528,128]{2,1,0:T(8,128)(2,1)S(1)}, bf16[2,528,128]{2,1,0:T(8,128)(2,1)S(1)}, u32[]{:S(2)}, u32[]{:S(2)}) collective-permute-start(bf16[2,528,128]{2,1,0:T(8,128)(2,1)S(1)} %collective-permute-done.19.refs_8_), channel_id=1, source_target_pairs={{0,16},{8,24},{16,0},{24,8},{1,17},{9,25},{17,1},{25,9},{2,18},{10... | collective-permute-start | bytes 811016 | tf_op jit(solution)/shard_map/ppermute | solution.py:22
  98.1 4.5 %collective-permute-start.32 = (bf16[14,128,128]{2,1,0:T(8,128)(2,1)S(1)}, bf16[14,128,128]{2,1,0:T(8,128)(2,1)}, u32[]{:S(2)}, u32[]{:S(2)}) collective-permute-start(bf16[14,128,128]{2,1,0:T(8,128)(2,1)S(1)} %collective-permute-done.20.refs_32_), channel_id=1, source_target_pairs={{0,8},{8,0},{16,24},{24,16},{1,9},{9,1},{17,25},{25,17},{2,10},{10... | collective-permute-start | bytes 1376264 | tf_op jit(solution)/shard_map/ppermute | solution.py:26
  98.2 2.2 collective-permute-start.28
  98.7 2.1 collective-permute-start.29
  98.7 2.4 collective-permute-start.30
  99.2 2.3 collective-permute-start.31
  111.0 22.4 %collective-permute-start.33 = (bf16[3584,128]{1,0:T(8,128)(2,1)}, bf16[3584,128]{1,0:T(8,128)(2,1)S(1)}, u32[]{:S(2)}, u32[]{:S(2)}) collective-permute-start(bf16[3584,128]{1,0:T(8,128)(2,1)} %shard_map.128.refs_1_), channel_id=1, source_target_pairs={{0,16},{8,24},{16,0},{24,8},{1,17},{9,25},{17,1},{25,9},{2,18},{10... | collective-permute-start | bytes 2752520 | tf_op jit(solution)/shard_map/ppermute | solution.py:22
  111.6 22.7 %collective-permute-start.34 = (bf16[3584,128]{1,0:T(8,128)(2,1)}, bf16[3584,128]{1,0:T(8,128)(2,1)S(1)}, u32[]{:S(2)}, u32[]{:S(2)}) collective-permute-start(bf16[3584,128]{1,0:T(8,128)(2,1)} %shard_map.128.refs_1_), channel_id=1, source_target_pairs={{0,8},{8,0},{16,24},{24,16},{1,9},{9,1},{17,25},{25,17},{2,10},{10... | collective-permute-start | bytes 2752520 | tf_op jit(solution)/shard_map/ppermute | solution.py:26
  133.4 3.0 %collective-permute-start.35 = (bf16[3584,128]{1,0:T(8,128)(2,1)S(1)}, bf16[3584,128]{1,0:T(8,128)(2,1)S(1)}, u32[]{:S(2)}, u32[]{:S(2)}) collective-permute-start(bf16[3584,128]{1,0:T(8,128)(2,1)S(1)} %collective-permute-done.33.refs_2_), channel_id=1, source_target_pairs={{0,8},{8,0},{16,24},{24,16},{1,9},{9,1},{17,25},{25,17},{2,10},{10... | collective-permute-start | bytes 2752520 | tf_op jit(solution)/shard_map/ppermute | solution.py:26
  146.6 14.6 %collective-permute-start.36 = (bf16[14,128,128]{2,1,0:T(8,128)(2,1)S(1)}, bf16[14,128,128]{2,1,0:T(8,128)(2,1)S(1)}, u32[]{:S(2)}, u32[]{:S(2)}) collective-permute-start(bf16[14,128,128]{2,1,0:T(8,128)(2,1)S(1)} %bitcast.51), channel_id=1, source_target_pairs={{0,2},{1,3},{2,4},{3,5},{4,6},{5,7},{6,0},{7,1},{8,10},{9,11},{10,... | collective-permute-start | bytes 1376264 | tf_op jit(solution)/shard_map/ppermute | solution.py:30
  146.7 14.6 %collective-permute-start.37 = (bf16[14,128,128]{2,1,0:T(8,128)(2,1)S(1)}, bf16[14,128,128]{2,1,0:T(8,128)(2,1)S(1)}, u32[]{:S(2)}, u32[]{:S(2)}) collective-permute-start(bf16[14,128,128]{2,1,0:T(8,128)(2,1)S(1)} %bitcast.52), channel_id=1, source_target_pairs={{0,1},{1,0},{2,3},{3,2},{4,5},{5,4},{6,7},{7,6},{8,9},{9,8},{10,11... | collective-permute-start | bytes 1376264 | tf_op jit(solution)/shard_map/ppermute | solution.py:36
  161.2 14.2 %collective-permute-start.39 = (bf16[14,128,128]{2,1,0:T(8,128)(2,1)S(1)}, bf16[14,128,128]{2,1,0:T(8,128)(2,1)}, u32[]{:S(2)}, u32[]{:S(2)}) collective-permute-start(bf16[14,128,128]{2,1,0:T(8,128)(2,1)S(1)} %collective-permute-done.36.refs_22_), channel_id=1, source_target_pairs={{0,2},{1,3},{2,4},{3,5},{4,6},{5,7},{6,0},{7,1},{8,10},{9,11},{10,... | collective-permute-start | bytes 1376264 | tf_op jit(solution)/shard_map/ppermute | solution.py:30
  161.3 14.2 %collective-permute-start.40 = (bf16[14,128,128]{2,1,0:T(8,128)(2,1)S(1)}, bf16[14,128,128]{2,1,0:T(8,128)(2,1)}, u32[]{:S(2)}, u32[]{:S(2)}) collective-permute-start(bf16[14,128,128]{2,1,0:T(8,128)(2,1)S(1)} %collective-permute-done.36.refs_22_), channel_id=1, source_target_pairs={{0,1},{1,0},{2,3},{3,2},{4,5},{5,4},{6,7},{7,6},{8,9},{9,8},{10,11... | collective-permute-start | bytes 1376264 | tf_op jit(solution)/shard_map/ppermute | solution.py:36
  163.1 12.4 %collective-permute-start.41 = (bf16[14,128,128]{2,1,0:T(8,128)(2,1)S(1)}, bf16[14,128,128]{2,1,0:T(8,128)(2,1)}, u32[]{:S(2)}, u32[]{:S(2)}) collective-permute-start(bf16[14,128,128]{2,1,0:T(8,128)(2,1)S(1)} %collective-permute-done.36.refs_22_), channel_id=1, source_target_pairs={{0,8},{8,0},{16,24},{24,16},{1,9},{9,1},{17,25},{25,17},{2,10},{10... | collective-permute-start | bytes 1376264 | tf_op jit(solution)/shard_map/ppermute | solution.py:26
  163.1 12.4 %collective-permute-start.38 = (bf16[14,128,128]{2,1,0:T(8,128)(2,1)S(1)}, bf16[14,128,128]{2,1,0:T(8,128)(2,1)}, u32[]{:S(2)}, u32[]{:S(2)}) collective-permute-start(bf16[14,128,128]{2,1,0:T(8,128)(2,1)S(1)} %bitcast.53), channel_id=1, source_target_pairs={{0,8},{8,0},{16,24},{24,16},{1,9},{9,1},{17,25},{25,17},{2,10},{10... | collective-permute-start | bytes 1376264 | tf_op jit(solution)/shard_map/ppermute | solution.py:26
  164.3 11.1 %collective-permute-start.42 = (f32[96,256]{1,0:T(8,128)S(1)}, f32[96,256]{1,0:T(8,128)S(1)}, u32[]{:S(2)}, u32[]{:S(2)}) collective-permute-start(f32[96,256]{1,0:T(8,128)S(1)} %dynamic-slice_bitcast_fusion), channel_id=1, source_target_pairs={{0,1},{1,0},{2,3},{3,2},{4,5},{5,4},{6,7},{7,6},{8,9},{9,8},{10,11... | collective-permute-start | bytes 294920 | tf_op jit(solution)/shard_map/ppermute | solution.py:345
  175.5 17.1 %collective-permute-start.43 = (bf16[14,128,128]{2,1,0:T(8,128)(2,1)S(1)}, bf16[14,128,128]{2,1,0:T(8,128)(2,1)S(1)}, u32[]{:S(2)}, u32[]{:S(2)}) collective-permute-start(bf16[14,128,128]{2,1,0:T(8,128)(2,1)S(1)} %collective-permute-done.37.refs_20_), channel_id=1, source_target_pairs={{0,8},{8,0},{16,24},{24,16},{1,9},{9,1},{17,25},{25,17},{2,10},{10... | collective-permute-start | bytes 1376264 | tf_op jit(solution)/shard_map/ppermute | solution.py:26
  175.6 17.1 %collective-permute-start.44 = (bf16[14,128,128]{2,1,0:T(8,128)(2,1)}, bf16[14,128,128]{2,1,0:T(8,128)(2,1)S(1)}, u32[]{:S(2)}, u32[]{:S(2)}) collective-permute-start(bf16[14,128,128]{2,1,0:T(8,128)(2,1)} %collective-permute-done.39.refs_26_), channel_id=1, source_target_pairs={{0,2},{1,3},{2,4},{3,5},{4,6},{5,7},{6,0},{7,1},{8,10},{9,11},{10,... | collective-permute-start | bytes 1376264 | tf_op jit(solution)/shard_map/ppermute | solution.py:30
  176.3 16.4 %collective-permute-start.45 = (bf16[14,128,128]{2,1,0:T(8,128)(2,1)}, bf16[14,128,128]{2,1,0:T(8,128)(2,1)S(1)}, u32[]{:S(2)}, u32[]{:S(2)}) collective-permute-start(bf16[14,128,128]{2,1,0:T(8,128)(2,1)} %collective-permute-done.39.refs_26_), channel_id=1, source_target_pairs={{0,1},{1,0},{2,3},{3,2},{4,5},{5,4},{6,7},{7,6},{8,9},{9,8},{10,11... | collective-permute-start | bytes 1376264 | tf_op jit(solution)/shard_map/ppermute | solution.py:36
  178.0 14.7 %collective-permute-start.46 = (bf16[14,128,128]{2,1,0:T(8,128)(2,1)}, bf16[14,128,128]{2,1,0:T(8,128)(2,1)S(1)}, u32[]{:S(2)}, u32[]{:S(2)}) collective-permute-start(bf16[14,128,128]{2,1,0:T(8,128)(2,1)} %collective-permute-done.39.refs_26_), channel_id=1, source_target_pairs={{0,8},{8,0},{16,24},{24,16},{1,9},{9,1},{17,25},{25,17},{2,10},{10... | collective-permute-start | bytes 1376264 | tf_op jit(solution)/shard_map/ppermute | solution.py:26
  178.0 14.6 %collective-permute-start.47 = (f32[96,256]{1,0:T(8,128)S(1)}, f32[96,256]{1,0:T(8,128)S(1)}, u32[]{:S(2)}, u32[]{:S(2)}) collective-permute-start(f32[96,256]{1,0:T(8,128)S(1)} %bitcast_add_fusion), channel_id=1, source_target_pairs={{0,2},{1,3},{2,0},{3,1},{4,6},{5,7},{6,4},{7,5},{8,10},{9,11},{10,... | collective-permute-start | bytes 294920 | tf_op jit(solution)/shard_map/ppermute | solution.py:345
  192.8 14.3 %collective-permute-start.49 = (bf16[7,128,128]{2,1,0:T(8,128)(2,1)S(1)}, bf16[7,128,128]{2,1,0:T(8,128)(2,1)S(1)}, u32[]{:S(2)}, u32[]{:S(2)}) collective-permute-start(bf16[7,128,128]{2,1,0:T(8,128)(2,1)S(1)} %slice.28), channel_id=1, source_target_pairs={{0,1},{1,0},{2,3},{3,2},{4,5},{5,4},{6,7},{7,6},{8,9},{9,8},{10,11... | collective-permute-start | bytes 688136 | tf_op jit(solution)/shard_map/ppermute | solution.py:36
  193.5 13.7 %collective-permute-start.48 = (bf16[14,128,128]{2,1,0:T(8,128)(2,1)}, bf16[14,128,128]{2,1,0:T(8,128)(2,1)S(1)}, u32[]{:S(2)}, u32[]{:S(2)}) collective-permute-start(bf16[14,128,128]{2,1,0:T(8,128)(2,1)} %collective-permute-done.40.refs_24_), channel_id=1, source_target_pairs={{0,8},{8,0},{16,24},{24,16},{1,9},{9,1},{17,25},{25,17},{2,10},{10... | collective-permute-start | bytes 1376264 | tf_op jit(solution)/shard_map/ppermute | solution.py:26
  193.5 13.7 %collective-permute-start.51 = (bf16[14,128,128]{2,1,0:T(8,128)(2,1)S(1)}, bf16[14,128,128]{2,1,0:T(8,128)(2,1)S(1)}, u32[]{:S(2)}, u32[]{:S(2)}) collective-permute-start(bf16[14,128,128]{2,1,0:T(8,128)(2,1)S(1)} %collective-permute-done.44.refs_30_), channel_id=1, source_target_pairs={{0,8},{8,0},{16,24},{24,16},{1,9},{9,1},{17,25},{25,17},{2,10},{10... | collective-permute-start | bytes 1376264 | tf_op jit(solution)/shard_map/ppermute | solution.py:26
  194.0 13.1 %collective-permute-start.50 = (bf16[7,128,128]{2,1,0:T(8,128)(2,1)S(1)}, bf16[7,128,128]{2,1,0:T(8,128)(2,1)S(1)}, u32[]{:S(2)}, u32[]{:S(2)}) collective-permute-start(bf16[7,128,128]{2,1,0:T(8,128)(2,1)S(1)} %slice.29), channel_id=1, source_target_pairs={{0,2},{1,3},{2,4},{3,5},{4,6},{5,7},{6,0},{7,1},{8,10},{9,11},{10,... | collective-permute-start | bytes 688136 | tf_op jit(solution)/shard_map/ppermute | solution.py:30
  194.1 13.0 %collective-permute-start.52 = (f32[96,256]{1,0:T(8,128)S(1)}, f32[96,256]{1,0:T(8,128)S(1)}, u32[]{:S(2)}, u32[]{:S(2)}) collective-permute-start(f32[96,256]{1,0:T(8,128)S(1)} %add.136), channel_id=1, source_target_pairs={{0,4},{1,5},{2,6},{3,7},{4,0},{5,1},{6,2},{7,3},{8,12},{9,13},{10,... | collective-permute-start | bytes 294920 | tf_op jit(solution)/shard_map/ppermute | solution.py:345
  207.2 6.5 %collective-permute-start.53 = (bf16[14,128,128]{2,1,0:T(8,128)(2,1)S(1)}, bf16[14,128,128]{2,1,0:T(8,128)(2,1)S(1)}, u32[]{:S(2)}, u32[]{:S(2)}) collective-permute-start(bf16[14,128,128]{2,1,0:T(8,128)(2,1)S(1)} %collective-permute-done.45.refs_28_), channel_id=1, source_target_pairs={{0,8},{8,0},{16,24},{24,16},{1,9},{9,1},{17,25},{25,17},{2,10},{10... | collective-permute-start | bytes 1376264 | tf_op jit(solution)/shard_map/ppermute | solution.py:26
  207.3 6.5 %collective-permute-start.54 = (bf16[14,128,128]{2,1,0:T(8,128)(2,1)S(1)}, bf16[14,128,128]{2,1,0:T(8,128)(2,1)S(1)}, u32[]{:S(2)}, u32[]{:S(2)}) collective-permute-start(bf16[14,128,128]{2,1,0:T(8,128)(2,1)S(1)} %constant_dynamic-update-slice_fusion.2.refs_32_), channel_id=1, source_target_pairs={{0,8},{8,0},{16,24},{24,16},{1,9},{9,1},{17,25},{25,17},{2,10},{10... | collective-permute-start | bytes 1376264 | tf_op jit(solution)/shard_map/ppermute | solution.py:26
  207.8 4.8 %collective-permute-start.58 = (f32[96,256]{1,0:T(8,128)S(1)}, f32[96,256]{1,0:T(8,128)S(1)}, u32[]{:S(2)}, u32[]{:S(2)}) collective-permute-start(f32[96,256]{1,0:T(8,128)S(1)} %add.137), channel_id=1, source_target_pairs={{0,16},{8,24},{16,0},{24,8},{1,17},{9,25},{17,1},{25,9},{2,18},{10... | collective-permute-start | bytes 294920 | tf_op jit(solution)/shard_map/ppermute | solution.py:22
  212.6 11.6 %collective-permute-start.59 = (f32[2,96,256]{2,1,0:T(8,128)S(1)}, f32[2,96,256]{2,1,0:T(8,128)S(1)}, u32[]{:S(2)}, u32[]{:S(2)}) collective-permute-start(f32[2,96,256]{2,1,0:T(8,128)S(1)} %pad_maximum_fusion.3), channel_id=1, source_target_pairs={{0,1},{1,0},{2,3},{3,2},{4,5},{5,4},{6,7},{7,6},{8,9},{9,8},{10,11... | collective-permute-start | bytes 589832 | tf_op jit(solution)/shard_map/ppermute | solution.py:345
  223.6 23.5 %collective-permute-start.55 = (bf16[3584,128]{1,0:T(8,128)(2,1)}, bf16[3584,128]{1,0:T(8,128)(2,1)S(1)}, u32[]{:S(2)}, u32[]{:S(2)}) collective-permute-start(bf16[3584,128]{1,0:T(8,128)(2,1)} %shard_map.130.refs_1_), channel_id=1, source_target_pairs={{0,16},{8,24},{16,0},{24,8},{1,17},{9,25},{17,1},{25,9},{2,18},{10... | collective-permute-start | bytes 2752520 | tf_op jit(solution)/shard_map/ppermute | solution.py:22
  224.3 3.1 %collective-permute-start.60 = (f32[2,192,256]{2,1,0:T(8,128)S(1)}, f32[2,192,256]{2,1,0:T(8,128)S(1)}, u32[]{:S(2)}, u32[]{:S(2)}) collective-permute-start(f32[2,192,256]{2,1,0:T(8,128)S(1)} %get-tuple-element.112), channel_id=1, source_target_pairs={{0,8},{8,0},{16,24},{24,16},{1,9},{9,1},{17,25},{25,17},{2,10},{10... | collective-permute-start | bytes 1179656 | tf_op jit(solution)/shard_map/ppermute | solution.py:26
  226.8 22.8 %collective-permute-start.56 = (bf16[3584,128]{1,0:T(8,128)(2,1)S(1)}, bf16[3584,128]{1,0:T(8,128)(2,1)S(1)}, u32[]{:S(2)}, u32[]{:S(2)}) collective-permute-start(bf16[3584,128]{1,0:T(8,128)(2,1)S(1)} %copy-done.4), channel_id=1, source_target_pairs={{0,8},{8,0},{16,24},{24,16},{1,9},{9,1},{17,25},{25,17},{2,10},{10... | collective-permute-start | bytes 2752520 | tf_op jit(solution)/shard_map/ppermute | solution.py:26
  247.1 2.5 collective-permute-start.57
  (56 other events, 730.3 us)

commit v4 on v3

--- a/solution.py
+++ b/solution.py
@@ -184,9 +184,13 @@
         ],
         compiler_params=pltpu.CompilerParams(vmem_limit_bytes=58 << 20),
         cost_estimate=pl.CostEstimate(
-            flops=flops, bytes_accessed=count * cap * side * side * 6, transcendentals=0
+            flops=flops, bytes_accessed=count * cap * side * side * 15, transcendentals=0
         ),
     )(scal, *operands)
+
+
+def joined(refs):
+    return jnp.concatenate([r[...] for r in refs], axis=1)
 
 
 def fill_weights(scal, refs, scratch, cols, across):
@@ -213,59 +217,42 @@
             put(width + (d * xs + k) * cols, jnp.where(use_out, out_w, in_w))
 
 
-def dense_kernel(parts, outs, cols, chunks, across, scal, *refs):
-    refs = list(refs)
-    count = parts + outs - 1
-    ins = [refs.pop(0) for _ in range(count)]
-    weights = [refs.pop(0) for _ in range(3)]
-    results = [refs.pop(0) for _ in range(outs)]
-    here = [refs.pop(0) for _ in range(count)]
-    made = [refs.pop(0) for _ in range(outs)]
-    scratch, in_sem, out_sem = refs
-    step = here[0].shape[0] // chunks
-
-    def rows(c):
-        return pl.ds(c * step, step)
-
-    def load(c, i):
-        return pltpu.make_async_copy(
-            ins[i].at[rows(c)], here[i].at[rows(c)], in_sem.at[c * count + i]
-        )
-
-    def save(c, i):
-        return pltpu.make_async_copy(
-            made[i].at[rows(c)], results[i].at[rows(c)], out_sem.at[c * outs + i]
-        )
-
-    for c in range(chunks):
-        for i in range(count):
-            load(c, i).start()
-    fill_weights(scal, weights, scratch, cols, across)
-    dims_ = (((1,), (1 if across else 0,)), ((), ()))
-    for c in range(chunks):
-        for i in range(count):
-            load(c, i).wait()
-        both = jnp.concatenate([h[rows(c), :] for h in here[:parts]], axis=1)
-        pre = lax.dot_general(both, scratch[...], dims_, preferred_element_type=F32)
-        if outs == 1:
-            made[0][rows(c), :] = pre.astype(BF)
-        else:
-            sigma = 1.0 / (1.0 + jnp.exp(-pre))
-            made[0][rows(c), :] = (pre * sigma).astype(BF)
-            slope = here[parts][rows(c), :].astype(F32) * sigma * (1.0 + pre * (1.0 - sigma))
-            made[1][rows(c), :] = slope.astype(BF)
-        for i in range(outs):
-            save(c, i).start()
-    for c in range(chunks):
-        for i in range(outs):
-            save(c, i).wait()
+def layer_kernel(parts, cols, scal, *refs):
+    ins = refs[:parts]
+    cotangent, *weights, hidden_ref, grad_ref, scratch = refs[parts:]
+
+    @pl.when(pl.program_id(0) == 0)
+    def _():
+        fill_weights(scal, weights, scratch, cols, False)
+
+    pre = jnp.dot(joined(ins), scratch[...], preferred_element_type=F32)
+    sigma = 1.0 / (1.0 + jnp.exp(-pre))
+    hidden_ref[...] = (pre * sigma).astype(BF)
+    grad_ref[...] = (cotangent[...].astype(F32) * sigma * (1.0 + pre * (1.0 - sigma))).astype(BF)
+
+
+def final_kernel(parts, cols, scal, *refs):
+    ins = refs[:parts]
+    *weights, out_ref, scratch = refs[parts:]
+
+    @pl.when(pl.program_id(0) == 0)
+    def _():
+        fill_weights(scal, weights, scratch, cols, True)
+
+    out_ref[...] = lax.dot_general(
+        joined(ins), scratch[...], (((1,), (1,)), ((), ())), preferred_element_type=F32
+    ).astype(BF)
+
+
+def row_specs(arrays, step):
+    return [pl.BlockSpec((step, a.shape[1]), lambda i: (i, 0)) for a in arrays]
 
 
 def whole(a):
-    return pl.BlockSpec(a.shape, lambda: (0,) * a.ndim)
-
-
-def dense(scal, ins, weights, cols, chunks, outs, across):
+    return pl.BlockSpec(a.shape, lambda i: (0,) * a.ndim)
+
+
+def over_rows_call(kernel, scal, ins, weights, cols, step, outs, across):
     rows, width = ins[0].shape
     xs = width // cols
     if across:
@@ -276,21 +263,16 @@
         scratch = (width * (1 + CORES), width)
     weights = [weights[0]] + split
     shape = jax.ShapeDtypeStruct((rows, width), BF)
-    any_spec = pl.BlockSpec(memory_space=pl.ANY)
+    parts = 1 + CORES * xs
     result = pl.pallas_call(
-        functools.partial(dense_kernel, 1 + CORES * xs, outs, cols, chunks, across),
+        functools.partial(kernel, parts, cols),
+        grid=(rows // step,),
         out_shape=(shape,) * outs,
         in_specs=[pl.BlockSpec(memory_space=pltpu.SMEM)]
-        + [any_spec] * len(ins)
+        + row_specs(ins, step)
         + [whole(w) for w in weights],
-        out_specs=(any_spec,) * outs,
-        scratch_shapes=[pltpu.VMEM(a.shape, BF) for a in ins]
-        + [pltpu.VMEM((rows, width), BF)] * outs
-        + [
-            pltpu.VMEM(scratch, BF),
-            pltpu.SemaphoreType.DMA((chunks * len(ins),)),
-            pltpu.SemaphoreType.DMA((chunks * outs,)),
-        ],
+        out_specs=tuple(row_specs([shape] * outs, step)),
+        scratch_shapes=[pltpu.VMEM(scratch, BF)],
         compiler_params=pltpu.CompilerParams(vmem_limit_bytes=58 << 20),
     )(scal, *ins, *weights)
     return result if outs > 1 else result[0]
@@ -343,6 +325,18 @@
 
     def meet(a, bit):
         return lax.ppermute(a, "narrow", [(i, i ^ bit) for i in range(narrow)])
+
+    def halve(a, bit, *ahead):
+        upper = n_id // bit % 2
+        halves = after(a, *ahead).reshape(2, -1, width)
+        sent = lax.dynamic_index_in_dim(halves, 1 - upper, 0, keepdims=False)
+        kept = lax.dynamic_index_in_dim(halves, upper, 0, keepdims=False)
+        return kept + meet(sent, bit)
+
+    def in_order(parts, at):
+        count = len(parts)
+        ahead = [parts[-i % count] for i in range(count)]
+        return lax.dynamic_slice_in_dim(jnp.stack(ahead + ahead), count - at, count, 0)
 
     def along_x(a, *ahead):
         return [x_shift(after(a, *ahead), k, wide) for k in range(1, xs)]
@@ -404,26 +398,27 @@
     for i, (k, j) in enumerate(every):
         where[i] = {0: (0, i), 1: (0, i), 2: (2, j), 3: (1, j)}[k]
 
-    def spread(pieces, swaps):
+    def spread(pieces, swaps, *ahead):
         for kj in every:
             if kj not in pieces:
                 pieces[kj] = y_shift(pieces[kj[0], kj[1] - 1], 1, zs, ys)
             if kj not in swaps:
                 swaps[kj] = core_swap(pieces[kj], wide)
         own = aggregate(
-            scal, row_sets, col_sets, where, [here([pieces[kj]]) for kj in every],
+            after(scal, *ahead) if ahead else scal, row_sets, col_sets, where, [here([pieces[kj]]) for kj in every],
             [here([swaps[kj]]) for kj in every], blocks, side, cap,
         )
-        all_own = [own] + along_x(own)
-        return own, all_own + [core_swap(p, wide) for p in all_own]
+        return own, [own] + along_x(own), core_swap(own, wide)
 
     names = [(0, 0), (1, 0), (2, 0), (3, 0), (0, 1), (1, 1), (2, 1), (3, 1)]
-    agg, aggs = spread(
+    agg, aggs, agg_swap = spread(
         dict(zip(names, [own, z1, z2, z3, y0, y1, y2, y3])),
         dict(zip(names, [own_swap, z1_swap, z2_swap, z3_swap, y0_swap, y1_swap, y2_swap, y3_swap])),
     )
-    hidden, grad_pre = dense(
-        scal, [node_feats] + aggs + [grad_out], [w_self, w_out, w_in], cols, 4, 2, False
+    aggs += [agg_swap] + [swap(a) for a in aggs[1:]]
+    hidden, grad_pre = over_rows_call(
+        layer_kernel, scal, [node_feats] + aggs + [grad_out], [w_self, w_out, w_in], cols,
+        nodes // 2, 2, False,
     )
 
     own = own_piece(grad_pre)
@@ -440,47 +435,45 @@
     one = [z1, y0]
     z2 = z_shift(after(z1, *one), 1, zs, ys)
     y1 = y_shift(after(z1, *one), 1, zs, ys)
-    upper = n_id % 2
-    halves = after(grad_part, *one).reshape(2, -1, width)
-    sent = lax.dynamic_index_in_dim(halves, 1 - upper, 0, keepdims=False)
-    kept = lax.dynamic_index_in_dim(halves, upper, 0, keepdims=False)
-    grad_half = kept + meet(sent, 1)
+    grad_some = halve(grad_part, 1, *one)
     own_swap, z1_swap = swap(own, *one), swap(z1, *one)
-    two = [z2, y1, own_swap, z1_swap, grad_half]
+    two = [z2, y1, own_swap, z1_swap, grad_some]
     z3 = z_shift(after(z2, *two), 1, zs, ys)
     y2 = y_shift(after(z2, *two), 1, zs, ys)
     y0_swap, z2_swap = swap(y0, *two), swap(z2, *two)
-    for bit in (2, 8):
-        if bit < narrow:
-            grad_half = grad_half + meet(after(grad_half, *two), bit)
-    three = [z3, y2, y0_swap, z2_swap, grad_half]
+    for bit in range(2, ys, 2):
+        grad_some = halve(grad_some, bit, *two)
+    grad_some = halve(grad_some, 2 * ys, *two)
+    three = [z3, y2, y0_swap, z2_swap, grad_some]
     quarter = half // 2
     y3 = y_shift(after(z3, *three)[:quarter], 1, zs, ys)
     y3_rest = z_shift(after(y2, *three)[quarter:], 1, zs, ys)
-    grad_half = grad_half + meet(after(grad_half, *three), 4)
+    grad_some = halve(grad_some, ys, *three)
     y1_swap, z3_swap = swap(y1, *three), swap(z3, *three)
-    four = [y3, y3_rest, y1_swap, z3_swap, grad_half]
+    four = [y3, y3_rest, y1_swap, z3_swap, grad_some]
     y3 = jnp.concatenate([y3, y3_rest], axis=0)
     y2_swap, y3_swap = swap(y2, *four), swap(y3, *four)
-    stack = jnp.stack([grad_half] + along_x(grad_half, *four))
-    _, backs = spread(
+    grad_some = after(grad_some, *four)
+    chips = [grad_some] + along_x(grad_some)
+    shared = in_order(chips, x_id)
+    _, backs, back_swap = spread(
         dict(zip(names, [own, z1, z2, z3, y0, y1, y2, y3])),
         dict(zip(names, [own_swap, z1_swap, z2_swap, z3_swap, y0_swap, y1_swap, y2_swap, y3_swap])),
-    )
-    there = meet(stack, 1)
-    stack = jnp.concatenate(
-        [jnp.where(upper == 1, there, stack), jnp.where(upper == 1, stack, there)], axis=1
-    )
-    stack = jnp.stack([stack, core_swap(stack, wide)])
-    stack = jnp.where(first, stack, stack[::-1])
-    if xs == 2:
-        stack = jnp.where(x_id == 0, stack, stack[:, ::-1])
-    else:
-        stack = stack[:, (x_id - jnp.arange(xs)) % xs]
+        shared,
+    )
+    shared = after(shared, back_swap)
+    stack = in_order([shared] + [z_shift(shared, k, zs, ys) for k in range(1, zs)], z_id)
+    stack = stack.swapaxes(0, 1).reshape(xs, -1, width)
+    stack = in_order([stack] + [y_shift(stack, j, zs, ys) for j in range(1, ys)], y_id)
+    stack = stack.swapaxes(0, 1).reshape(xs, -1, width)
+    stack = in_order([stack, core_swap(stack, wide)], core)
     agg_grads = stack[:, :, :cols].reshape(CORES, width, width)
     grad_ws = stack[:, :, cols:].swapaxes(0, 1).reshape(width, width)
 
-    grad_feats = dense(scal, [grad_pre] + backs, [w_self, w_in, w_out], cols, 4, 1, True)
+    backs += [back_swap] + [swap(a) for a in backs[1:]]
+    grad_feats = over_rows_call(
+        final_kernel, scal, [grad_pre] + backs, [w_self, w_in, w_out], cols, nodes // 2, 1, True
+    )
     return (hidden, grad_feats, grad_ws, agg_grads[0], agg_grads[1])
 
 

time: 258 us -> 249 us (0.965)
  waiting for transfers between devices: 162 us -> 154 us
  Pallas kernels: 31.5 us -> 28.3 us
  starting transfers between devices: 41.4 us -> 44.3 us
    ppermute x8, waiting for transfers between devices: 59.7 us -> 45.4 us  [x_shift(): lax.ppermute(a, 'wide', [(i, (i + CORES * k) % wide) for i in range(wide)])]
    ppermute x4 -> x3, waiting for transfers between devices: 33.4 us -> 19.9 us  [meet(): return lax.ppermute(a, 'narrow', [(i, i ^ bit) for i in range(narrow)])]
    ppermute x10 -> x13, waiting for transfers between devices: 64.7 us -> 74.2 us  [z_shift(): lax.ppermute(a, 'narrow', [(z * ys + y, (z + k) % zs * ys + y) for z in r...]
    ppermute x9 -> x10, waiting for transfers between devices: 0.39 us -> 9.52 us  [y_shift(): lax.ppermute(a, 'narrow', [(z * ys + y, z * ys + (y + k) % ys) for z in r...]
    ppermute x10 -> x13, starting transfers between devices: 8.24 us -> 12.1 us  [z_shift(): lax.ppermute(a, 'narrow', [(z * ys + y, (z + k) % zs * ys + y) for z in r...]
    pallas_call x2, Pallas kernels: 14.9 us -> 11.5 us  [over_rows_call(): pl.pallas_call(functools.partial(kernel, parts, cols), grid=(rows // step...]
    unnamed x122 -> x123, local copies, waits for them, and re-layouts: 7.56 us -> 4.96 us
    ppermute x4 -> x3, starting transfers between devices: 6.47 us -> 4.02 us  [meet(): return lax.ppermute(a, 'narrow', [(i, i ^ bit) for i in range(narrow)])]
  transfers between devices with their start and end apart: 61 -> 64, of which waited for: 21 -> 26; matrix products, arithmetic and copies ran while one was open for 3% -> 4% of each run, Pallas kernels for 3% -> 0%
where the time goes in v4:
time: 249 us
  waiting for transfers between devices  154 us (62%)
  starting transfers between devices  44.3 us (18%)
  Pallas kernels  28.3 us (11%)
  local copies, waits for them, and re-layouts  12.4 us (5%)
  other arithmetic  6.86 us (3%)
    ppermute x13, waiting for transfers between devices, z_shift(): lax.ppermute(a, 'narrow', [(z * ys + y, (z + k) % zs * ys + y) for z in r...  74.2 us
    ppermute x8, waiting for transfers between devices, x_shift(): lax.ppermute(a, 'wide', [(i, (i + CORES * k) % wide) for i in range(wide)])  45.4 us
    ppermute x3, waiting for transfers between devices, meet(): return lax.ppermute(a, 'narrow', [(i, i ^ bit) for i in range(narrow)])  19.9 us
    pallas_call x2, Pallas kernels, aggregate(): pl.pallas_call(functools.partial(aggregate_kernel, wide, cap, side, block...  16.8 us
    ppermute x13, starting transfers between devices, z_shift(): lax.ppermute(a, 'narrow', [(z * ys + y, (z + k) % zs * ys + y) for z in r...  12.1 us
    pallas_call x2, Pallas kernels, over_rows_call(): pl.pallas_call(functools.partial(kernel, parts, cols), grid=(rows // step...  11.5 us
    ppermute x10, starting transfers between devices, y_shift(): lax.ppermute(a, 'narrow', [(z * ys + y, z * ys + (y + k) % ys) for z in r...  10.7 us
    ppermute x10, waiting for transfers between devices, y_shift(): lax.ppermute(a, 'narrow', [(z * ys + y, z * ys + (y + k) % ys) for z in r...  9.52 us
  transfers between devices with their start and end apart: 64, of which 26 were waited for; matrix products, arithmetic and copies ran while one was open for 4% of the time, Pallas kernels for 0%

profile of v4, /device:TPU:0, one launch (start us, length us, event | category | flops | bytes accessed | tf_op | source)
XLA Modules:
  0.0 248.5 jit_solution(5076382575422067181)
XLA Ops:
  0.7 0.8 compare_convert_fusion
  1.5 0.7 convert_reduce_fusion
  2.3 1.8 dynamic_slice.62
  4.2 1.1 fusion.8
  5.3 2.9 %collective-permute-start = (bf16[4,528,128]{2,1,0:T(8,128)(2,1)}, bf16[4,528,128]{2,1,0:T(8,128)(2,1)}, u32[]{:S(2)}, u32[]{:S(2)}) collective-permute-start(bf16[4,528,128]{2,1,0:T(8,128)(2,1)} %get-tuple-element.56), channel_id=1, source_target_pairs={{0,16},{8,24},{16,0},{24,8},{1,17},{9,25},{17,1},{25,9},{2,18},{10... | collective-permute-start | bytes 1622024 | tf_op jit(solution)/shard_map/ppermute | solution.py:22
  8.3 0.7 copy.55
  9.0 0.9 fusion.9
  9.9 1.5 collective-permute-start.2
  11.4 1.6 collective-permute-start.1
  13.0 12.0 %collective-permute-done.1.refs_22_ = bf16[14,128,128]{2,1,0:T(8,128)(2,1)S(1)} collective-permute-done((bf16[14,128,128]{2,1,0:T(8,128)(2,1)S(1)}, bf16[14,128,128]{2,1,0:T(8,128)(2,1)S(1)}, u32[]{:S(2)}, u32[]{:S(2)}) %collective-permute-start.1) | collective-permute-done | bytes 458784 | tf_op jit(solution)/shard_map/ppermute | solution.py:30
  25.1 0.7 copy-done.35
  26.8 1.2 fusion.16
  28.6 3.3 %collective-permute-start.6 = (bf16[2,528,128]{2,1,0:T(8,128)(2,1)S(1)}, bf16[2,528,128]{2,1,0:T(8,128)(2,1)S(1)}, u32[]{:S(2)}, u32[]{:S(2)}) collective-permute-start(bf16[2,528,128]{2,1,0:T(8,128)(2,1)S(1)} %get-tuple-element.62), channel_id=1, source_target_pairs={{0,6},{1,7},{2,0},{3,1},{4,2},{5,3},{6,4},{7,5},{8,14},{9,15},{10,... | collective-permute-start | bytes 811016 | tf_op jit(solution)/shard_map/ppermute | solution.py:30
  32.0 7.4 %collective-permute-done.5 = bf16[2,528,128]{2,1,0:T(8,128)(2,1)S(1)} collective-permute-done((bf16[2,528,128]{2,1,0:T(8,128)(2,1)S(1)}, bf16[2,528,128]{2,1,0:T(8,128)(2,1)S(1)}, u32[]{:S(2)}, u32[]{:S(2)}) %collective-permute-start.5) | collective-permute-done | bytes 270368 | tf_op jit(solution)/shard_map/ppermute | solution.py:30
  39.4 3.0 %collective-permute-done.6.refs_7_ = bf16[2,528,128]{2,1,0:T(8,128)(2,1)S(1)} collective-permute-done((bf16[2,528,128]{2,1,0:T(8,128)(2,1)S(1)}, bf16[2,528,128]{2,1,0:T(8,128)(2,1)S(1)}, u32[]{:S(2)}, u32[]{:S(2)}) %collective-permute-start.6) | collective-permute-done | bytes 270368 | tf_op jit(solution)/shard_map/ppermute | solution.py:30
  42.5 1.6 collective-permute-start.12
  44.0 1.5 collective-permute-start.8
  45.5 0.6 collective-permute-start.9
  46.6 10.4 %collective-permute-done.8.refs_26_ = bf16[14,128,128]{2,1,0:T(8,128)(2,1)S(1)} collective-permute-done((bf16[14,128,128]{2,1,0:T(8,128)(2,1)S(1)}, bf16[14,128,128]{2,1,0:T(8,128)(2,1)S(1)}, u32[]{:S(2)}, u32[]{:S(2)}) %collective-permute-start.8) | collective-permute-done | bytes 458784 | tf_op jit(solution)/shard_map/ppermute | solution.py:30
  57.4 0.9 copy-done.44
  59.0 1.0 collective-permute-start.17
  59.9 7.9 %collective-permute-done.17.refs_10_ = bf16[2,528,128]{2,1,0:T(8,128)(2,1)S(1)} collective-permute-done((bf16[2,528,128]{2,1,0:T(8,128)(2,1)S(1)}, bf16[2,528,128]{2,1,0:T(8,128)(2,1)S(1)}, u32[]{:S(2)}, u32[]{:S(2)}) %collective-permute-start.17) | collective-permute-done | bytes 270368 | tf_op jit(solution)/shard_map/ppermute | solution.py:22
  67.8 5.2 %collective-permute-done.14.refs_30_ = bf16[14,128,128]{2,1,0:T(8,128)(2,1)S(1)} collective-permute-done((bf16[14,128,128]{2,1,0:T(8,128)(2,1)S(1)}, bf16[14,128,128]{2,1,0:T(8,128)(2,1)S(1)}, u32[]{:S(2)}, u32[]{:S(2)}) %collective-permute-start.14) | collective-permute-done | bytes 458784 | tf_op jit(solution)/shard_map/ppermute | solution.py:30
  74.0 14.3 %collective-permute-done.19.refs_8_ = bf16[2,528,128]{2,1,0:T(8,128)(2,1)S(1)} collective-permute-done((bf16[2,528,128]{2,1,0:T(8,128)(2,1)S(1)}, bf16[2,528,128]{2,1,0:T(8,128)(2,1)S(1)}, u32[]{:S(2)}, u32[]{:S(2)}) %collective-permute-start.19) | collective-permute-done | bytes 270368 | tf_op jit(solution)/shard_map/ppermute | solution.py:30
  90.1 7.9 %collective-permute-done.23.refs_11_ = bf16[2,528,128]{2,1,0:T(8,128)(2,1)S(1)} collective-permute-done((bf16[2,528,128]{2,1,0:T(8,128)(2,1)S(1)}, bf16[2,528,128]{2,1,0:T(8,128)(2,1)S(1)}, u32[]{:S(2)}, u32[]{:S(2)}) %collective-permute-start.23) | collective-permute-done | bytes 270368 | tf_op jit(solution)/shard_map/ppermute | solution.py:22
  99.3 0.6 pad_add_fusion.scal
  101.8 0.7 copy-done.23
  102.7 8.3 %shard_map.128.refs_1_ = bf16[3584,128]{1,0:T(8,128)(2,1)} custom-call(s32[10]{0:T(128)} %pad_add_fusion.scal, bf16[8,528,128]{2,1,0:T(8,128)(2,1)} %copy-done, bf16[4,528,128]{2,1,0:T(8,128)(2,1)} %collective-permute-done.refs_1_, bf16[4,528,128]{2,1,0:T(8,128)(2,1)} %copy-done.7, bf16[8,528,128]{2,1,0:T(8,128)(2,1)} %copy-done.3, ...), custom_call_target="tpu_custom_call" | custom-call | flops 536870912 | bytes 31457280 | tf_op jit(solution)/shard_map/pallas_call | solution.py:169
  111.0 0.6 collective-permute-start.33
  111.6 1.8 collective-permute-start.34
  113.4 19.8 %collective-permute-done.33.refs_2_ = bf16[3584,128]{1,0:T(8,128)(2,1)S(1)} collective-permute-done((bf16[3584,128]{1,0:T(8,128)(2,1)}, bf16[3584,128]{1,0:T(8,128)(2,1)S(1)}, u32[]{:S(2)}, u32[]{:S(2)}) %collective-permute-start.33) | collective-permute-done | bytes 917536 | tf_op jit(solution)/shard_map/ppermute | solution.py:22
  133.3 1.0 collective-permute-start.35
  134.3 2.1 collective-permute-done.35.refs_4_
  136.4 1.0 copy-done.32
  137.4 6.5 %shard_map.129 = (bf16[3584,256]{1,0:T(8,128)(2,1)}, bf16[3584,256]{1,0:T(8,128)(2,1)}) custom-call(s32[10]{0:T(128)} %pad_add_fusion.scal, bf16[3584,256]{1,0:T(8,128)(2,1)} %refs_0_.1, bf16[3584,128]{1,0:T(8,128)(2,1)} %shard_map.128.refs_1_, bf16[3584,128]{1,0:T(8,128)(2,1)} %copy-done.30, bf16[3584,128]{1,0:T(8,128)(2,1)} %copy-done.31, ...), custom_call_target="tpu_custom_call" | custom-call | tf_op jit(solution)/shard_map/pallas_call | solution.py:267
  143.8 1.2 dynamic_slice.70
  145.1 1.9 collective-permute-start.37
  147.3 12.4 %collective-permute-done.36.refs_22_ = bf16[14,128,128]{2,1,0:T(8,128)(2,1)S(1)} collective-permute-done((bf16[14,128,128]{2,1,0:T(8,128)(2,1)S(1)}, bf16[14,128,128]{2,1,0:T(8,128)(2,1)S(1)}, u32[]{:S(2)}, u32[]{:S(2)}) %collective-permute-start.36) | collective-permute-done | bytes 458784 | tf_op jit(solution)/shard_map/ppermute | solution.py:30
  159.8 1.8 collective-permute-start.40
  162.1 0.7 fusion
  163.2 10.8 %collective-permute-done.38 = f32[96,256]{1,0:T(8,128)S(1)} collective-permute-done((f32[96,256]{1,0:T(8,128)S(1)}, f32[96,256]{1,0:T(8,128)S(1)}, u32[]{:S(2)}, u32[]{:S(2)}) %collective-permute-start.38) | collective-permute-done | bytes 98336 | tf_op jit(solution)/shard_map/ppermute | solution.py:327
  174.5 1.7 collective-permute-start.45
  176.7 3.6 %collective-permute-start.43 = (f32[48,256]{1,0:T(8,128)S(1)}, f32[48,256]{1,0:T(8,128)S(1)}, u32[]{:S(2)}, u32[]{:S(2)}) collective-permute-start(f32[48,256]{1,0:T(8,128)S(1)} %dynamic-slice_bitcast_fusion.1), channel_id=1, source_target_pairs={{0,4},{1,5},{2,6},{3,7},{4,0},{5,1},{6,2},{7,3},{8,12},{9,13},{10,... | collective-permute-start | bytes 147464 | tf_op jit(solution)/shard_map/ppermute | solution.py:327
  180.4 9.0 %collective-permute-done.43 = f32[48,256]{1,0:T(8,128)S(1)} collective-permute-done((f32[48,256]{1,0:T(8,128)S(1)}, f32[48,256]{1,0:T(8,128)S(1)}, u32[]{:S(2)}, u32[]{:S(2)}) %collective-permute-start.43) | collective-permute-done | bytes 49184 | tf_op jit(solution)/shard_map/ppermute | solution.py:327
  189.6 1.8 collective-permute-start.49
  191.4 2.1 collective-permute-start.50
  193.7 3.5 %collective-permute-done.49 = bf16[7,128,128]{2,1,0:T(8,128)(2,1)S(1)} collective-permute-done((bf16[7,128,128]{2,1,0:T(8,128)(2,1)S(1)}, bf16[7,128,128]{2,1,0:T(8,128)(2,1)S(1)}, u32[]{:S(2)}, u32[]{:S(2)}) %collective-permute-start.49) | collective-permute-done | bytes 229408 | tf_op jit(solution)/shard_map/ppermute | solution.py:36
  197.3 4.0 %collective-permute-done.50 = bf16[7,128,128]{2,1,0:T(8,128)(2,1)S(1)} collective-permute-done((bf16[7,128,128]{2,1,0:T(8,128)(2,1)S(1)}, bf16[7,128,128]{2,1,0:T(8,128)(2,1)S(1)}, u32[]{:S(2)}, u32[]{:S(2)}) %collective-permute-start.50) | collective-permute-done | bytes 229408 | tf_op jit(solution)/shard_map/ppermute | solution.py:30
  202.5 3.3 %collective-permute-done.53 = f32[24,256]{1,0:T(8,128)S(1)} collective-permute-done((f32[24,256]{1,0:T(8,128)S(1)}, f32[24,256]{1,0:T(8,128)S(1)}, u32[]{:S(2)}, u32[]{:S(2)}) %collective-permute-start.53) | collective-permute-done | bytes 24608 | tf_op jit(solution)/shard_map/ppermute | solution.py:22
  205.9 8.5 %shard_map.130.refs_1_ = bf16[3584,128]{1,0:T(8,128)(2,1)} custom-call(s32[10]{0:T(128)} %pad_add_fusion.scal, bf16[8,528,128]{2,1,0:T(8,128)(2,1)} %copy-done, bf16[4,528,128]{2,1,0:T(8,128)(2,1)} %collective-permute-done.refs_1_, bf16[4,528,128]{2,1,0:T(8,128)(2,1)} %copy-done.7, bf16[8,528,128]{2,1,0:T(8,128)(2,1)} %copy-done.3, ...), custom_call_target="tpu_custom_call" | custom-call | flops 536870912 | bytes 31457280 | tf_op jit(solution)/shard_map/pallas_call | solution.py:169
  214.4 0.9 collective-permute-start.57
  215.9 1.7 collective-permute-done.57.refs_3_
  217.7 1.7 collective-permute-start.60
  219.8 3.0 %collective-permute-done.59 = f32[2,24,256]{2,1,0:T(8,128)S(1)} collective-permute-done((f32[2,24,256]{2,1,0:T(8,128)S(1)}, f32[2,24,256]{2,1,0:T(8,128)S(1)}, u32[]{:S(2)}, u32[]{:S(2)}) %collective-permute-start.59) | collective-permute-done | bytes 49184 | tf_op jit(solution)/shard_map/ppermute | solution.py:30
  222.8 2.4 collective-permute-done.61
  225.8 5.6 %collective-permute-done.62 = f32[2,96,256]{2,1,0:T(8,128)S(1)} collective-permute-done((f32[2,96,256]{2,1,0:T(8,128)S(1)}, f32[2,96,256]{2,1,0:T(8,128)S(1)}, u32[]{:S(2)}, u32[]{:S(2)}) %collective-permute-start.62) | collective-permute-done | bytes 196640 | tf_op jit(solution)/shard_map/ppermute | solution.py:36
  231.5 6.4 %collective-permute-done.56.refs_2_ = bf16[3584,128]{1,0:T(8,128)(2,1)S(1)} collective-permute-done((bf16[3584,128]{1,0:T(8,128)(2,1)}, bf16[3584,128]{1,0:T(8,128)(2,1)S(1)}, u32[]{:S(2)}, u32[]{:S(2)}) %collective-permute-start.56) | collective-permute-done | bytes 917536 | tf_op jit(solution)/shard_map/ppermute | solution.py:22
  238.1 0.8 copy.57
  238.9 0.8 copy.59
  239.7 1.3 fusion.6
  241.0 0.7 copy.66
  241.7 0.8 fusion.42
  242.6 0.9 copy-done.29
  243.5 5.0 %shard_map.131 = bf16[3584,256]{1,0:T(8,128)(2,1)} custom-call(s32[10]{0:T(128)} %pad_add_fusion.scal, bf16[3584,256]{1,0:T(8,128)(2,1)} %get-tuple-element.89.refs_0_, bf16[3584,128]{1,0:T(8,128)(2,1)} %shard_map.130.refs_1_, bf16[3584,128]{1,0:T(8,128)(2,1)} %copy-done.28, bf16[3584,128]{1,0:T(8,128)(2,1)} %copy-done.27, bf16[3584,128]{1,0:T(8,128)(2,1)} %copy-done.29, ...), custom_call_target="tpu_custom_call" | custom-call | tf_op jit(solution)/shard_map/pallas_call | solution.py:267
  (227 shorter events, 15.1 us)
Async XLA Ops:
  5.3 19.7 %collective-permute-start = (bf16[4,528,128]{2,1,0:T(8,128)(2,1)}, bf16[4,528,128]{2,1,0:T(8,128)(2,1)}, u32[]{:S(2)}, u32[]{:S(2)}) collective-permute-start(bf16[4,528,128]{2,1,0:T(8,128)(2,1)} %get-tuple-element.56), channel_id=1, source_target_pairs={{0,16},{8,24},{16,0},{24,8},{1,17},{9,25},{17,1},{25,9},{2,18},{10... | collective-permute-start | bytes 1622024 | tf_op jit(solution)/shard_map/ppermute | solution.py:22
  9.9 15.1 %collective-permute-start.2 = (bf16[4,528,128]{2,1,0:T(8,128)(2,1)S(1)}, bf16[4,528,128]{2,1,0:T(8,128)(2,1)S(1)}, u32[]{:S(2)}, u32[]{:S(2)}) collective-permute-start(bf16[4,528,128]{2,1,0:T(8,128)(2,1)S(1)} %get-tuple-element.110), channel_id=1, source_target_pairs={{0,1},{1,0},{2,3},{3,2},{4,5},{5,4},{6,7},{7,6},{8,9},{9,8},{10,11... | collective-permute-start | bytes 1622024 | tf_op jit(solution)/shard_map/ppermute | solution.py:36
  11.4 13.6 %collective-permute-start.1 = (bf16[14,128,128]{2,1,0:T(8,128)(2,1)S(1)}, bf16[14,128,128]{2,1,0:T(8,128)(2,1)S(1)}, u32[]{:S(2)}, u32[]{:S(2)}) collective-permute-start(bf16[14,128,128]{2,1,0:T(8,128)(2,1)S(1)} %bitcast.89), channel_id=1, source_target_pairs={{0,2},{1,3},{2,4},{3,5},{4,6},{5,7},{6,0},{7,1},{8,10},{9,11},{10,... | collective-permute-start | bytes 1376264 | tf_op jit(solution)/shard_map/ppermute | solution.py:30
  25.0 17.4 %collective-permute-start.4 = (bf16[8,528,128]{2,1,0:T(8,128)(2,1)S(1)}, bf16[8,528,128]{2,1,0:T(8,128)(2,1)S(1)}, u32[]{:S(2)}, u32[]{:S(2)}) collective-permute-start(bf16[8,528,128]{2,1,0:T(8,128)(2,1)S(1)} %pad_maximum_fusion.refs_0_), channel_id=1, source_target_pairs={{0,8},{8,0},{16,24},{24,16},{1,9},{9,1},{17,25},{25,17},{2,10},{10... | collective-permute-start | bytes 3244040 | tf_op jit(solution)/shard_map/ppermute | solution.py:26
  25.8 16.7 %collective-permute-start.3 = (bf16[4,528,128]{2,1,0:T(8,128)(2,1)}, bf16[4,528,128]{2,1,0:T(8,128)(2,1)S(1)}, u32[]{:S(2)}, u32[]{:S(2)}) collective-permute-start(bf16[4,528,128]{2,1,0:T(8,128)(2,1)} %get-tuple-element.58), channel_id=1, source_target_pairs={{0,16},{8,24},{16,0},{24,8},{1,17},{9,25},{17,1},{25,9},{2,18},{10... | collective-permute-start | bytes 1622024 | tf_op jit(solution)/shard_map/ppermute | solution.py:22
  26.3 16.1 %collective-permute-start.7 = (bf16[14,128,128]{2,1,0:T(8,128)(2,1)}, bf16[14,128,128]{2,1,0:T(8,128)(2,1)S(1)}, u32[]{:S(2)}, u32[]{:S(2)}) collective-permute-start(bf16[14,128,128]{2,1,0:T(8,128)(2,1)} %bitcast.87), channel_id=1, source_target_pairs={{0,1},{1,0},{2,3},{3,2},{4,5},{5,4},{6,7},{7,6},{8,9},{9,8},{10,11... | collective-permute-start | bytes 1376264 | tf_op jit(solution)/shard_map/ppermute | solution.py:36
  28.1 11.3 %collective-permute-start.5 = (bf16[2,528,128]{2,1,0:T(8,128)(2,1)S(1)}, bf16[2,528,128]{2,1,0:T(8,128)(2,1)S(1)}, u32[]{:S(2)}, u32[]{:S(2)}) collective-permute-start(bf16[2,528,128]{2,1,0:T(8,128)(2,1)S(1)} %get-tuple-element.61), channel_id=1, source_target_pairs={{0,2},{1,3},{2,4},{3,5},{4,6},{5,7},{6,0},{7,1},{8,10},{9,11},{10,... | collective-permute-start | bytes 811016 | tf_op jit(solution)/shard_map/ppermute | solution.py:30
  28.6 13.8 %collective-permute-start.6 = (bf16[2,528,128]{2,1,0:T(8,128)(2,1)S(1)}, bf16[2,528,128]{2,1,0:T(8,128)(2,1)S(1)}, u32[]{:S(2)}, u32[]{:S(2)}) collective-permute-start(bf16[2,528,128]{2,1,0:T(8,128)(2,1)S(1)} %get-tuple-element.62), channel_id=1, source_target_pairs={{0,6},{1,7},{2,0},{3,1},{4,2},{5,3},{6,4},{7,5},{8,14},{9,15},{10,... | collective-permute-start | bytes 811016 | tf_op jit(solution)/shard_map/ppermute | solution.py:30
  42.5 15.8 %collective-permute-start.12 = (bf16[4,528,128]{2,1,0:T(8,128)(2,1)S(1)}, bf16[4,528,128]{2,1,0:T(8,128)(2,1)S(1)}, u32[]{:S(2)}, u32[]{:S(2)}) collective-permute-start(bf16[4,528,128]{2,1,0:T(8,128)(2,1)S(1)} %constant_dynamic-update-slice_fusion.refs_6_), channel_id=1, source_target_pairs={{0,16},{8,24},{16,0},{24,8},{1,17},{9,25},{17,1},{25,9},{2,18},{10... | collective-permute-start | bytes 1622024 | tf_op jit(solution)/shard_map/ppermute | solution.py:22
  44.0 13.0 %collective-permute-start.8 = (bf16[14,128,128]{2,1,0:T(8,128)(2,1)S(1)}, bf16[14,128,128]{2,1,0:T(8,128)(2,1)S(1)}, u32[]{:S(2)}, u32[]{:S(2)}) collective-permute-start(bf16[14,128,128]{2,1,0:T(8,128)(2,1)S(1)} %copy-done.36), channel_id=1, source_target_pairs={{0,2},{1,3},{2,4},{3,5},{4,6},{5,7},{6,0},{7,1},{8,10},{9,11},{10,... | collective-permute-start | bytes 1376264 | tf_op jit(solution)/shard_map/ppermute | solution.py:30
  45.5 11.9 %collective-permute-start.9 = (bf16[14,128,128]{2,1,0:T(8,128)(2,1)S(1)}, bf16[14,128,128]{2,1,0:T(8,128)(2,1)S(1)}, u32[]{:S(2)}, u32[]{:S(2)}) collective-permute-start(bf16[14,128,128]{2,1,0:T(8,128)(2,1)S(1)} %copy-done.36), channel_id=1, source_target_pairs={{0,1},{1,0},{2,3},{3,2},{4,5},{5,4},{6,7},{7,6},{8,9},{9,8},{10,11... | collective-permute-start | bytes 1376264 | tf_op jit(solution)/shard_map/ppermute | solution.py:36
  46.1 11.3 %collective-permute-start.10 = (bf16[14,128,128]{2,1,0:T(8,128)(2,1)S(1)}, bf16[14,128,128]{2,1,0:T(8,128)(2,1)S(1)}, u32[]{:S(2)}, u32[]{:S(2)}) collective-permute-start(bf16[14,128,128]{2,1,0:T(8,128)(2,1)S(1)} %bitcast.90), channel_id=1, source_target_pairs={{0,8},{8,0},{16,24},{24,16},{1,9},{9,1},{17,25},{25,17},{2,10},{10... | collective-permute-start | bytes 1376264 | tf_op jit(solution)/shard_map/ppermute | solution.py:26
  46.1 11.3 %collective-permute-start.11 = (bf16[14,128,128]{2,1,0:T(8,128)(2,1)S(1)}, bf16[14,128,128]{2,1,0:T(8,128)(2,1)S(1)}, u32[]{:S(2)}, u32[]{:S(2)}) collective-permute-start(bf16[14,128,128]{2,1,0:T(8,128)(2,1)S(1)} %copy-done.36), channel_id=1, source_target_pairs={{0,8},{8,0},{16,24},{24,16},{1,9},{9,1},{17,25},{25,17},{2,10},{10... | collective-permute-start | bytes 1376264 | tf_op jit(solution)/shard_map/ppermute | solution.py:26
  58.3 14.8 %collective-permute-start.13 = (bf16[4,528,128]{2,1,0:T(8,128)(2,1)}, bf16[4,528,128]{2,1,0:T(8,128)(2,1)S(1)}, u32[]{:S(2)}, u32[]{:S(2)}) collective-permute-start(bf16[4,528,128]{2,1,0:T(8,128)(2,1)} %collective-permute-done.refs_1_), channel_id=1, source_target_pairs={{0,8},{8,0},{16,24},{24,16},{1,9},{9,1},{17,25},{25,17},{2,10},{10... | collective-permute-start | bytes 1622024 | tf_op jit(solution)/shard_map/ppermute | solution.py:26
  58.3 14.7 %collective-permute-start.14 = (bf16[14,128,128]{2,1,0:T(8,128)(2,1)S(1)}, bf16[14,128,128]{2,1,0:T(8,128)(2,1)S(1)}, u32[]{:S(2)}, u32[]{:S(2)}) collective-permute-start(bf16[14,128,128]{2,1,0:T(8,128)(2,1)S(1)} %collective-permute-done.8.refs_26_), channel_id=1, source_target_pairs={{0,2},{1,3},{2,4},{3,5},{4,6},{5,7},{6,0},{7,1},{8,10},{9,11},{10,... | collective-permute-start | bytes 1376264 | tf_op jit(solution)/shard_map/ppermute | solution.py:30
  58.8 14.2 %collective-permute-start.15 = (bf16[14,128,128]{2,1,0:T(8,128)(2,1)S(1)}, bf16[14,128,128]{2,1,0:T(8,128)(2,1)S(1)}, u32[]{:S(2)}, u32[]{:S(2)}) collective-permute-start(bf16[14,128,128]{2,1,0:T(8,128)(2,1)S(1)} %collective-permute-done.8.refs_26_), channel_id=1, source_target_pairs={{0,1},{1,0},{2,3},{3,2},{4,5},{5,4},{6,7},{7,6},{8,9},{9,8},{10,11... | collective-permute-start | bytes 1376264 | tf_op jit(solution)/shard_map/ppermute | solution.py:36
  58.9 14.1 %collective-permute-start.16 = (bf16[14,128,128]{2,1,0:T(8,128)(2,1)S(1)}, bf16[14,128,128]{2,1,0:T(8,128)(2,1)S(1)}, u32[]{:S(2)}, u32[]{:S(2)}) collective-permute-start(bf16[14,128,128]{2,1,0:T(8,128)(2,1)S(1)} %collective-permute-done.7.refs_20_), channel_id=1, source_target_pairs={{0,8},{8,0},{16,24},{24,16},{1,9},{9,1},{17,25},{25,17},{2,10},{10... | collective-permute-start | bytes 1376264 | tf_op jit(solution)/shard_map/ppermute | solution.py:26
  59.0 8.9 %collective-permute-start.17 = (bf16[2,528,128]{2,1,0:T(8,128)(2,1)S(1)}, bf16[2,528,128]{2,1,0:T(8,128)(2,1)S(1)}, u32[]{:S(2)}, u32[]{:S(2)}) collective-permute-start(bf16[2,528,128]{2,1,0:T(8,128)(2,1)S(1)} %collective-permute-done.6.refs_7_), channel_id=1, source_target_pairs={{0,16},{8,24},{16,0},{24,8},{1,17},{9,25},{17,1},{25,9},{2,18},{10... | collective-permute-start | bytes 811016 | tf_op jit(solution)/shard_map/ppermute | solution.py:22
  73.1 15.3 %collective-permute-start.18 = (bf16[4,528,128]{2,1,0:T(8,128)(2,1)S(1)}, bf16[4,528,128]{2,1,0:T(8,128)(2,1)S(1)}, u32[]{:S(2)}, u32[]{:S(2)}) collective-permute-start(bf16[4,528,128]{2,1,0:T(8,128)(2,1)S(1)} %collective-permute-done.3.refs_2_), channel_id=1, source_target_pairs={{0,8},{8,0},{16,24},{24,16},{1,9},{9,1},{17,25},{25,17},{2,10},{10... | collective-permute-start | bytes 1622024 | tf_op jit(solution)/shard_map/ppermute | solution.py:26
  73.2 15.2 %collective-permute-start.20 = (bf16[14,128,128]{2,1,0:T(8,128)(2,1)S(1)}, bf16[14,128,128]{2,1,0:T(8,128)(2,1)S(1)}, u32[]{:S(2)}, u32[]{:S(2)}) collective-permute-start(bf16[14,128,128]{2,1,0:T(8,128)(2,1)S(1)} %collective-permute-done.14.refs_30_), channel_id=1, source_target_pairs={{0,1},{1,0},{2,3},{3,2},{4,5},{5,4},{6,7},{7,6},{8,9},{9,8},{10,11... | collective-permute-start | bytes 1376264 | tf_op jit(solution)/shard_map/ppermute | solution.py:36
  73.5 14.8 %collective-permute-start.21 = (bf16[14,128,128]{2,1,0:T(8,128)(2,1)S(1)}, bf16[14,128,128]{2,1,0:T(8,128)(2,1)S(1)}, u32[]{:S(2)}, u32[]{:S(2)}) collective-permute-start(bf16[14,128,128]{2,1,0:T(8,128)(2,1)S(1)} %collective-permute-done.8.refs_26_), channel_id=1, source_target_pairs={{0,8},{8,0},{16,24},{24,16},{1,9},{9,1},{17,25},{25,17},{2,10},{10... | collective-permute-start | bytes 1376264 | tf_op jit(solution)/shard_map/ppermute | solution.py:26
  73.7 14.7 %collective-permute-start.22 = (bf16[14,128,128]{2,1,0:T(8,128)(2,1)S(1)}, bf16[14,128,128]{2,1,0:T(8,128)(2,1)S(1)}, u32[]{:S(2)}, u32[]{:S(2)}) collective-permute-start(bf16[14,128,128]{2,1,0:T(8,128)(2,1)S(1)} %collective-permute-done.9.refs_24_), channel_id=1, source_target_pairs={{0,8},{8,0},{16,24},{24,16},{1,9},{9,1},{17,25},{25,17},{2,10},{10... | collective-permute-start | bytes 1376264 | tf_op jit(solution)/shard_map/ppermute | solution.py:26
  74.0 14.3 %collective-permute-start.19 = (bf16[2,528,128]{2,1,0:T(8,128)(2,1)S(1)}, bf16[2,528,128]{2,1,0:T(8,128)(2,1)S(1)}, u32[]{:S(2)}, u32[]{:S(2)}) collective-permute-start(bf16[2,528,128]{2,1,0:T(8,128)(2,1)S(1)} %get-tuple-element.73), channel_id=1, source_target_pairs={{0,4},{1,5},{2,6},{3,7},{4,0},{5,1},{6,2},{7,3},{8,12},{9,13},{10,... | collective-permute-start | bytes 811016 | tf_op jit(solution)/shard_map/ppermute | solution.py:30
  88.4 9.6 %collective-permute-start.24 = (bf16[4,528,128]{2,1,0:T(8,128)(2,1)S(1)}, bf16[4,528,128]{2,1,0:T(8,128)(2,1)S(1)}, u32[]{:S(2)}, u32[]{:S(2)}) collective-permute-start(bf16[4,528,128]{2,1,0:T(8,128)(2,1)S(1)} %constant_dynamic-update-slice_fusion.refs_6_), channel_id=1, source_target_pairs={{0,8},{8,0},{16,24},{24,16},{1,9},{9,1},{17,25},{25,17},{2,10},{10... | collective-permute-start | bytes 1622024 | tf_op jit(solution)/shard_map/ppermute | solution.py:26
  88.6 9.5 %collective-permute-start.27 = (bf16[4,528,128]{2,1,0:T(8,128)(2,1)S(1)}, bf16[4,528,128]{2,1,0:T(8,128)(2,1)S(1)}, u32[]{:S(2)}, u32[]{:S(2)}) collective-permute-start(bf16[4,528,128]{2,1,0:T(8,128)(2,1)S(1)} %collective-permute-done.12.refs_9_), channel_id=1, source_target_pairs={{0,8},{8,0},{16,24},{24,16},{1,9},{9,1},{17,25},{25,17},{2,10},{10... | collective-permute-start | bytes 1622024 | tf_op jit(solution)/shard_map/ppermute | solution.py:26
  89.0 9.0 %collective-permute-start.25 = (bf16[14,128,128]{2,1,0:T(8,128)(2,1)S(1)}, bf16[14,128,128]{2,1,0:T(8,128)(2,1)S(1)}, u32[]{:S(2)}, u32[]{:S(2)}) collective-permute-start(bf16[14,128,128]{2,1,0:T(8,128)(2,1)S(1)} %collective-permute-done.14.refs_30_), channel_id=1, source_target_pairs={{0,8},{8,0},{16,24},{24,16},{1,9},{9,1},{17,25},{25,17},{2,10},{10... | collective-permute-start | bytes 1376264 | tf_op jit(solution)/shard_map/ppermute | solution.py:26
  89.1 8.9 %collective-permute-start.26 = (bf16[14,128,128]{2,1,0:T(8,128)(2,1)S(1)}, bf16[14,128,128]{2,1,0:T(8,128)(2,1)S(1)}, u32[]{:S(2)}, u32[]{:S(2)}) collective-permute-start(bf16[14,128,128]{2,1,0:T(8,128)(2,1)S(1)} %collective-permute-done.15.refs_28_), channel_id=1, source_target_pairs={{0,8},{8,0},{16,24},{24,16},{1,9},{9,1},{17,25},{25,17},{2,10},{10... | collective-permute-start | bytes 1376264 | tf_op jit(solution)/shard_map/ppermute | solution.py:26
  89.5 8.5 %collective-permute-start.23 = (bf16[2,528,128]{2,1,0:T(8,128)(2,1)S(1)}, bf16[2,528,128]{2,1,0:T(8,128)(2,1)S(1)}, u32[]{:S(2)}, u32[]{:S(2)}) collective-permute-start(bf16[2,528,128]{2,1,0:T(8,128)(2,1)S(1)} %collective-permute-done.19.refs_8_), channel_id=1, source_target_pairs={{0,16},{8,24},{16,0},{24,8},{1,17},{9,25},{17,1},{25,9},{2,18},{10... | collective-permute-start | bytes 811016 | tf_op jit(solution)/shard_map/ppermute | solution.py:22
  98.1 4.5 %collective-permute-start.32 = (bf16[14,128,128]{2,1,0:T(8,128)(2,1)S(1)}, bf16[14,128,128]{2,1,0:T(8,128)(2,1)}, u32[]{:S(2)}, u32[]{:S(2)}) collective-permute-start(bf16[14,128,128]{2,1,0:T(8,128)(2,1)S(1)} %collective-permute-done.20.refs_32_), channel_id=1, source_target_pairs={{0,8},{8,0},{16,24},{24,16},{1,9},{9,1},{17,25},{25,17},{2,10},{10... | collective-permute-start | bytes 1376264 | tf_op jit(solution)/shard_map/ppermute | solution.py:26
  98.1 2.2 collective-permute-start.28
  98.6 2.1 collective-permute-start.29
  98.7 2.4 collective-permute-start.30
  99.2 2.3 collective-permute-start.31
  111.0 22.3 %collective-permute-start.33 = (bf16[3584,128]{1,0:T(8,128)(2,1)}, bf16[3584,128]{1,0:T(8,128)(2,1)S(1)}, u32[]{:S(2)}, u32[]{:S(2)}) collective-permute-start(bf16[3584,128]{1,0:T(8,128)(2,1)} %shard_map.128.refs_1_), channel_id=1, source_target_pairs={{0,16},{8,24},{16,0},{24,8},{1,17},{9,25},{17,1},{25,9},{2,18},{10... | collective-permute-start | bytes 2752520 | tf_op jit(solution)/shard_map/ppermute | solution.py:22
  111.6 22.7 %collective-permute-start.34 = (bf16[3584,128]{1,0:T(8,128)(2,1)}, bf16[3584,128]{1,0:T(8,128)(2,1)S(1)}, u32[]{:S(2)}, u32[]{:S(2)}) collective-permute-start(bf16[3584,128]{1,0:T(8,128)(2,1)} %shard_map.128.refs_1_), channel_id=1, source_target_pairs={{0,8},{8,0},{16,24},{24,16},{1,9},{9,1},{17,25},{25,17},{2,10},{10... | collective-permute-start | bytes 2752520 | tf_op jit(solution)/shard_map/ppermute | solution.py:26
  133.3 3.1 %collective-permute-start.35 = (bf16[3584,128]{1,0:T(8,128)(2,1)S(1)}, bf16[3584,128]{1,0:T(8,128)(2,1)S(1)}, u32[]{:S(2)}, u32[]{:S(2)}) collective-permute-start(bf16[3584,128]{1,0:T(8,128)(2,1)S(1)} %collective-permute-done.33.refs_2_), channel_id=1, source_target_pairs={{0,8},{8,0},{16,24},{24,16},{1,9},{9,1},{17,25},{25,17},{2,10},{10... | collective-permute-start | bytes 2752520 | tf_op jit(solution)/shard_map/ppermute | solution.py:26
  145.1 14.6 %collective-permute-start.36 = (bf16[14,128,128]{2,1,0:T(8,128)(2,1)S(1)}, bf16[14,128,128]{2,1,0:T(8,128)(2,1)S(1)}, u32[]{:S(2)}, u32[]{:S(2)}) collective-permute-start(bf16[14,128,128]{2,1,0:T(8,128)(2,1)S(1)} %bitcast.91), channel_id=1, source_target_pairs={{0,2},{1,3},{2,4},{3,5},{4,6},{5,7},{6,0},{7,1},{8,10},{9,11},{10,... | collective-permute-start | bytes 1376264 | tf_op jit(solution)/shard_map/ppermute | solution.py:30
  145.1 14.6 %collective-permute-start.37 = (bf16[14,128,128]{2,1,0:T(8,128)(2,1)S(1)}, bf16[14,128,128]{2,1,0:T(8,128)(2,1)S(1)}, u32[]{:S(2)}, u32[]{:S(2)}) collective-permute-start(bf16[14,128,128]{2,1,0:T(8,128)(2,1)S(1)} %bitcast.92), channel_id=1, source_target_pairs={{0,1},{1,0},{2,3},{3,2},{4,5},{5,4},{6,7},{7,6},{8,9},{9,8},{10,11... | collective-permute-start | bytes 1376264 | tf_op jit(solution)/shard_map/ppermute | solution.py:36
  159.7 14.3 %collective-permute-start.39 = (bf16[14,128,128]{2,1,0:T(8,128)(2,1)S(1)}, bf16[14,128,128]{2,1,0:T(8,128)(2,1)}, u32[]{:S(2)}, u32[]{:S(2)}) collective-permute-start(bf16[14,128,128]{2,1,0:T(8,128)(2,1)S(1)} %collective-permute-done.36.refs_22_), channel_id=1, source_target_pairs={{0,2},{1,3},{2,4},{3,5},{4,6},{5,7},{6,0},{7,1},{8,10},{9,11},{10,... | collective-permute-start | bytes 1376264 | tf_op jit(solution)/shard_map/ppermute | solution.py:30
  159.8 14.2 %collective-permute-start.40 = (bf16[14,128,128]{2,1,0:T(8,128)(2,1)S(1)}, bf16[14,128,128]{2,1,0:T(8,128)(2,1)}, u32[]{:S(2)}, u32[]{:S(2)}) collective-permute-start(bf16[14,128,128]{2,1,0:T(8,128)(2,1)S(1)} %collective-permute-done.36.refs_22_), channel_id=1, source_target_pairs={{0,1},{1,0},{2,3},{3,2},{4,5},{5,4},{6,7},{7,6},{8,9},{9,8},{10,11... | collective-permute-start | bytes 1376264 | tf_op jit(solution)/shard_map/ppermute | solution.py:36
  161.6 12.4 %collective-permute-start.42 = (bf16[14,128,128]{2,1,0:T(8,128)(2,1)S(1)}, bf16[14,128,128]{2,1,0:T(8,128)(2,1)}, u32[]{:S(2)}, u32[]{:S(2)}) collective-permute-start(bf16[14,128,128]{2,1,0:T(8,128)(2,1)S(1)} %collective-permute-done.36.refs_22_), channel_id=1, source_target_pairs={{0,8},{8,0},{16,24},{24,16},{1,9},{9,1},{17,25},{25,17},{2,10},{10... | collective-permute-start | bytes 1376264 | tf_op jit(solution)/shard_map/ppermute | solution.py:26
  161.6 12.4 %collective-permute-start.41 = (bf16[14,128,128]{2,1,0:T(8,128)(2,1)S(1)}, bf16[14,128,128]{2,1,0:T(8,128)(2,1)}, u32[]{:S(2)}, u32[]{:S(2)}) collective-permute-start(bf16[14,128,128]{2,1,0:T(8,128)(2,1)S(1)} %bitcast.93), channel_id=1, source_target_pairs={{0,8},{8,0},{16,24},{24,16},{1,9},{9,1},{17,25},{25,17},{2,10},{10... | collective-permute-start | bytes 1376264 | tf_op jit(solution)/shard_map/ppermute | solution.py:26
  162.9 11.1 %collective-permute-start.38 = (f32[96,256]{1,0:T(8,128)S(1)}, f32[96,256]{1,0:T(8,128)S(1)}, u32[]{:S(2)}, u32[]{:S(2)}) collective-permute-start(f32[96,256]{1,0:T(8,128)S(1)} %dynamic-slice_bitcast_fusion), channel_id=1, source_target_pairs={{0,1},{1,0},{2,3},{3,2},{4,5},{5,4},{6,7},{7,6},{8,9},{9,8},{10,11... | collective-permute-start | bytes 294920 | tf_op jit(solution)/shard_map/ppermute | solution.py:327
  174.0 15.4 %collective-permute-start.44 = (bf16[14,128,128]{2,1,0:T(8,128)(2,1)}, bf16[14,128,128]{2,1,0:T(8,128)(2,1)S(1)}, u32[]{:S(2)}, u32[]{:S(2)}) collective-permute-start(bf16[14,128,128]{2,1,0:T(8,128)(2,1)} %collective-permute-done.39.refs_26_), channel_id=1, source_target_pairs={{0,2},{1,3},{2,4},{3,5},{4,6},{5,7},{6,0},{7,1},{8,10},{9,11},{10,... | collective-permute-start | bytes 1376264 | tf_op jit(solution)/shard_map/ppermute | solution.py:30
  174.5 15.0 %collective-permute-start.45 = (bf16[14,128,128]{2,1,0:T(8,128)(2,1)}, bf16[14,128,128]{2,1,0:T(8,128)(2,1)S(1)}, u32[]{:S(2)}, u32[]{:S(2)}) collective-permute-start(bf16[14,128,128]{2,1,0:T(8,128)(2,1)} %collective-permute-done.39.refs_26_), channel_id=1, source_target_pairs={{0,1},{1,0},{2,3},{3,2},{4,5},{5,4},{6,7},{7,6},{8,9},{9,8},{10,11... | collective-permute-start | bytes 1376264 | tf_op jit(solution)/shard_map/ppermute | solution.py:36
  176.2 13.3 %collective-permute-start.46 = (bf16[14,128,128]{2,1,0:T(8,128)(2,1)S(1)}, bf16[14,128,128]{2,1,0:T(8,128)(2,1)S(1)}, u32[]{:S(2)}, u32[]{:S(2)}) collective-permute-start(bf16[14,128,128]{2,1,0:T(8,128)(2,1)S(1)} %collective-permute-done.37.refs_20_), channel_id=1, source_target_pairs={{0,8},{8,0},{16,24},{24,16},{1,9},{9,1},{17,25},{25,17},{2,10},{10... | collective-permute-start | bytes 1376264 | tf_op jit(solution)/shard_map/ppermute | solution.py:26
  176.2 13.3 %collective-permute-start.47 = (bf16[14,128,128]{2,1,0:T(8,128)(2,1)}, bf16[14,128,128]{2,1,0:T(8,128)(2,1)S(1)}, u32[]{:S(2)}, u32[]{:S(2)}) collective-permute-start(bf16[14,128,128]{2,1,0:T(8,128)(2,1)} %collective-permute-done.39.refs_26_), channel_id=1, source_target_pairs={{0,8},{8,0},{16,24},{24,16},{1,9},{9,1},{17,25},{25,17},{2,10},{10... | collective-permute-start | bytes 1376264 | tf_op jit(solution)/shard_map/ppermute | solution.py:26
  176.7 12.7 %collective-permute-start.43 = (f32[48,256]{1,0:T(8,128)S(1)}, f32[48,256]{1,0:T(8,128)S(1)}, u32[]{:S(2)}, u32[]{:S(2)}) collective-permute-start(f32[48,256]{1,0:T(8,128)S(1)} %dynamic-slice_bitcast_fusion.1), channel_id=1, source_target_pairs={{0,4},{1,5},{2,6},{3,7},{4,0},{5,1},{6,2},{7,3},{8,12},{9,13},{10,... | collective-permute-start | bytes 147464 | tf_op jit(solution)/shard_map/ppermute | solution.py:327
  189.5 4.2 %collective-permute-start.48 = (f32[24,256]{1,0:T(8,128)S(1)}, f32[24,256]{1,0:T(8,128)S(1)}, u32[]{:S(2)}, u32[]{:S(2)}) collective-permute-start(f32[24,256]{1,0:T(8,128)S(1)} %dynamic-slice_bitcast_fusion.2), channel_id=1, source_target_pairs={{0,2},{1,3},{2,0},{3,1},{4,6},{5,7},{6,4},{7,5},{8,10},{9,11},{10,... | collective-permute-start | bytes 73736 | tf_op jit(solution)/shard_map/ppermute | solution.py:327
  189.6 7.6 %collective-permute-start.49 = (bf16[7,128,128]{2,1,0:T(8,128)(2,1)S(1)}, bf16[7,128,128]{2,1,0:T(8,128)(2,1)S(1)}, u32[]{:S(2)}, u32[]{:S(2)}) collective-permute-start(bf16[7,128,128]{2,1,0:T(8,128)(2,1)S(1)} %slice.28), channel_id=1, source_target_pairs={{0,1},{1,0},{2,3},{3,2},{4,5},{5,4},{6,7},{7,6},{8,9},{9,8},{10,11... | collective-permute-start | bytes 688136 | tf_op jit(solution)/shard_map/ppermute | solution.py:36
  191.4 10.0 %collective-permute-start.52 = (bf16[14,128,128]{2,1,0:T(8,128)(2,1)S(1)}, bf16[14,128,128]{2,1,0:T(8,128)(2,1)S(1)}, u32[]{:S(2)}, u32[]{:S(2)}) collective-permute-start(bf16[14,128,128]{2,1,0:T(8,128)(2,1)S(1)} %collective-permute-done.44.refs_30_), channel_id=1, source_target_pairs={{0,8},{8,0},{16,24},{24,16},{1,9},{9,1},{17,25},{25,17},{2,10},{10... | collective-permute-start | bytes 1376264 | tf_op jit(solution)/shard_map/ppermute | solution.py:26
  191.4 9.9 %collective-permute-start.50 = (bf16[7,128,128]{2,1,0:T(8,128)(2,1)S(1)}, bf16[7,128,128]{2,1,0:T(8,128)(2,1)S(1)}, u32[]{:S(2)}, u32[]{:S(2)}) collective-permute-start(bf16[7,128,128]{2,1,0:T(8,128)(2,1)S(1)} %slice.29), channel_id=1, source_target_pairs={{0,2},{1,3},{2,4},{3,5},{4,6},{5,7},{6,0},{7,1},{8,10},{9,11},{10,... | collective-permute-start | bytes 688136 | tf_op jit(solution)/shard_map/ppermute | solution.py:30
  193.5 7.9 %collective-permute-start.51 = (bf16[14,128,128]{2,1,0:T(8,128)(2,1)}, bf16[14,128,128]{2,1,0:T(8,128)(2,1)S(1)}, u32[]{:S(2)}, u32[]{:S(2)}) collective-permute-start(bf16[14,128,128]{2,1,0:T(8,128)(2,1)} %collective-permute-done.40.refs_24_), channel_id=1, source_target_pairs={{0,8},{8,0},{16,24},{24,16},{1,9},{9,1},{17,25},{25,17},{2,10},{10... | collective-permute-start | bytes 1376264 | tf_op jit(solution)/shard_map/ppermute | solution.py:26
  201.4 4.4 %collective-permute-start.54 = (bf16[14,128,128]{2,1,0:T(8,128)(2,1)S(1)}, bf16[14,128,128]{2,1,0:T(8,128)(2,1)}, u32[]{:S(2)}, u32[]{:S(2)}) collective-permute-start(bf16[14,128,128]{2,1,0:T(8,128)(2,1)S(1)} %collective-permute-done.45.refs_28_), channel_id=1, source_target_pairs={{0,8},{8,0},{16,24},{24,16},{1,9},{9,1},{17,25},{25,17},{2,10},{10... | collective-permute-start | bytes 1376264 | tf_op jit(solution)/shard_map/ppermute | solution.py:26
  201.4 4.4 %collective-permute-start.55 = (bf16[14,128,128]{2,1,0:T(8,128)(2,1)S(1)}, bf16[14,128,128]{2,1,0:T(8,128)(2,1)}, u32[]{:S(2)}, u32[]{:S(2)}) collective-permute-start(bf16[14,128,128]{2,1,0:T(8,128)(2,1)S(1)} %constant_dynamic-update-slice_fusion.2.refs_32_), channel_id=1, source_target_pairs={{0,8},{8,0},{16,24},{24,16},{1,9},{9,1},{17,25},{25,17},{2,10},{10... | collective-permute-start | bytes 1376264 | tf_op jit(solution)/shard_map/ppermute | solution.py:26
  201.9 3.8 %collective-permute-start.53 = (f32[24,256]{1,0:T(8,128)S(1)}, f32[24,256]{1,0:T(8,128)S(1)}, u32[]{:S(2)}, u32[]{:S(2)}) collective-permute-start(f32[24,256]{1,0:T(8,128)S(1)} %bitcast_add_fusion.2), channel_id=1, source_target_pairs={{0,16},{8,24},{16,0},{24,8},{1,17},{9,25},{17,1},{25,9},{2,18},{10... | collective-permute-start | bytes 73736 | tf_op jit(solution)/shard_map/ppermute | solution.py:22
  214.4 3.2 %collective-permute-start.57 = (bf16[3584,128]{1,0:T(8,128)(2,1)}, bf16[3584,128]{1,0:T(8,128)(2,1)S(1)}, u32[]{:S(2)}, u32[]{:S(2)}) collective-permute-start(bf16[3584,128]{1,0:T(8,128)(2,1)} %shard_map.130.refs_1_), channel_id=1, source_target_pairs={{0,8},{8,0},{16,24},{24,16},{1,9},{9,1},{17,25},{25,17},{2,10},{10... | collective-permute-start | bytes 2752520 | tf_op jit(solution)/shard_map/ppermute | solution.py:26
  215.3 22.6 %collective-permute-start.56 = (bf16[3584,128]{1,0:T(8,128)(2,1)}, bf16[3584,128]{1,0:T(8,128)(2,1)S(1)}, u32[]{:S(2)}, u32[]{:S(2)}) collective-permute-start(bf16[3584,128]{1,0:T(8,128)(2,1)} %shard_map.130.refs_1_), channel_id=1, source_target_pairs={{0,16},{8,24},{16,0},{24,8},{1,17},{9,25},{17,1},{25,9},{2,18},{10... | collective-permute-start | bytes 2752520 | tf_op jit(solution)/shard_map/ppermute | solution.py:22
  217.6 5.2 %collective-permute-start.59 = (f32[2,24,256]{2,1,0:T(8,128)S(1)}, f32[2,24,256]{2,1,0:T(8,128)S(1)}, u32[]{:S(2)}, u32[]{:S(2)}) collective-permute-start(f32[2,24,256]{2,1,0:T(8,128)S(1)} %fusion.29), channel_id=1, source_target_pairs={{0,6},{1,7},{2,0},{3,1},{4,2},{5,3},{6,4},{7,5},{8,14},{9,15},{10,... | collective-permute-start | bytes 147464 | tf_op jit(solution)/shard_map/ppermute | solution.py:30
  217.7 5.1 %collective-permute-start.60 = (f32[2,24,256]{2,1,0:T(8,128)S(1)}, f32[2,24,256]{2,1,0:T(8,128)S(1)}, u32[]{:S(2)}, u32[]{:S(2)}) collective-permute-start(f32[2,24,256]{2,1,0:T(8,128)S(1)} %fusion.29), channel_id=1, source_target_pairs={{0,4},{1,5},{2,6},{3,7},{4,0},{5,1},{6,2},{7,3},{8,12},{9,13},{10,... | collective-permute-start | bytes 147464 | tf_op jit(solution)/shard_map/ppermute | solution.py:30
  219.4 5.9 %collective-permute-start.61 = (f32[2,24,256]{2,1,0:T(8,128)S(1)}, f32[2,24,256]{2,1,0:T(8,128)S(1)}, u32[]{:S(2)}, u32[]{:S(2)}) collective-permute-start(f32[2,24,256]{2,1,0:T(8,128)S(1)} %fusion.29), channel_id=1, source_target_pairs={{0,2},{1,3},{2,4},{3,5},{4,6},{5,7},{6,0},{7,1},{8,10},{9,11},{10,... | collective-permute-start | bytes 147464 | tf_op jit(solution)/shard_map/ppermute | solution.py:30
  225.3 6.0 %collective-permute-start.62 = (f32[2,96,256]{2,1,0:T(8,128)S(1)}, f32[2,96,256]{2,1,0:T(8,128)S(1)}, u32[]{:S(2)}, u32[]{:S(2)}) collective-permute-start(f32[2,96,256]{2,1,0:T(8,128)S(1)} %bitcast.97), channel_id=1, source_target_pairs={{0,1},{1,0},{2,3},{3,2},{4,5},{5,4},{6,7},{7,6},{8,9},{9,8},{10,11... | collective-permute-start | bytes 589832 | tf_op jit(solution)/shard_map/ppermute | solution.py:36
  231.4 8.2 %collective-permute-start.63 = (f32[2,192,256]{2,1,0:T(8,128)S(1)}, f32[2,192,256]{2,1,0:T(8,128)}, u32[]{:S(2)}, u32[]{:S(2)}) collective-permute-start(f32[2,192,256]{2,1,0:T(8,128)S(1)} %bitcast.95), channel_id=1, source_target_pairs={{0,8},{8,0},{16,24},{24,16},{1,9},{9,1},{17,25},{25,17},{2,10},{10... | collective-permute-start | bytes 1179656 | tf_op jit(solution)/shard_map/ppermute | solution.py:26
  237.9 4.7 %collective-permute-start.58 = (bf16[3584,128]{1,0:T(8,128)(2,1)S(1)}, bf16[3584,128]{1,0:T(8,128)(2,1)S(1)}, u32[]{:S(2)}, u32[]{:S(2)}) collective-permute-start(bf16[3584,128]{1,0:T(8,128)(2,1)S(1)} %collective-permute-done.56.refs_2_), channel_id=1, source_target_pairs={{0,8},{8,0},{16,24},{24,16},{1,9},{9,1},{17,25},{25,17},{2,10},{10... | collective-permute-start | bytes 2752520 | tf_op jit(solution)/shard_map/ppermute | solution.py:26
  (56 other events, 968.7 us)

commit v5 on v4

--- a/solution.py
+++ b/solution.py
@@ -219,7 +219,7 @@
 
 def layer_kernel(parts, cols, scal, *refs):
     ins = refs[:parts]
-    cotangent, *weights, hidden_ref, grad_ref, scratch = refs[parts:]
+    cotangent, *weights, hidden_ref, grad_ref, piece_ref, scratch = refs[parts:]
 
     @pl.when(pl.program_id(0) == 0)
     def _():
@@ -228,7 +228,15 @@
     pre = jnp.dot(joined(ins), scratch[...], preferred_element_type=F32)
     sigma = 1.0 / (1.0 + jnp.exp(-pre))
     hidden_ref[...] = (pre * sigma).astype(BF)
-    grad_ref[...] = (cotangent[...].astype(F32) * sigma * (1.0 + pre * (1.0 - sigma))).astype(BF)
+    slope = (cotangent[...].astype(F32) * sigma * (1.0 + pre * (1.0 - sigma))).astype(BF)
+    grad_ref[...] = slope
+
+    @pl.when(pl.program_id(0) == scal[0])
+    def _():
+        piece = slope[:, :cols]
+        for e in range(1, slope.shape[1] // cols):
+            piece = jnp.where(scal[1] == e, slope[:, e * cols : (e + 1) * cols], piece)
+        piece_ref[...] = piece
 
 
 def final_kernel(parts, cols, scal, *refs):
@@ -264,14 +272,15 @@
     weights = [weights[0]] + split
     shape = jax.ShapeDtypeStruct((rows, width), BF)
     parts = 1 + CORES * xs
+    extra = (jax.ShapeDtypeStruct((step, cols), BF),) if outs > 1 else ()
     result = pl.pallas_call(
         functools.partial(kernel, parts, cols),
         grid=(rows // step,),
-        out_shape=(shape,) * outs,
+        out_shape=(shape,) * outs + extra,
         in_specs=[pl.BlockSpec(memory_space=pltpu.SMEM)]
         + row_specs(ins, step)
         + [whole(w) for w in weights],
-        out_specs=tuple(row_specs([shape] * outs, step)),
+        out_specs=tuple(row_specs([shape] * outs, step)) + tuple(whole(e) for e in extra),
         scratch_shapes=[pltpu.VMEM(scratch, BF)],
         compiler_params=pltpu.CompilerParams(vmem_limit_bytes=58 << 20),
     )(scal, *ins, *weights)
@@ -416,12 +425,12 @@
         dict(zip(names, [own_swap, z1_swap, z2_swap, z3_swap, y0_swap, y1_swap, y2_swap, y3_swap])),
     )
     aggs += [agg_swap] + [swap(a) for a in aggs[1:]]
-    hidden, grad_pre = over_rows_call(
+    hidden, grad_pre, own = over_rows_call(
         layer_kernel, scal, [node_feats] + aggs + [grad_out], [w_self, w_out, w_in], cols,
-        nodes // 2, 2, False,
-    )
-
-    own = own_piece(grad_pre)
+        nodes // CORES, 2, False,
+    )
+
+    own = own.reshape(half, side, cols)
     z1 = z_shift(own, 1, zs, ys)
     y0 = y_shift(own, 1, zs, ys)
     share = width // wide
@@ -470,9 +479,9 @@
     agg_grads = stack[:, :, :cols].reshape(CORES, width, width)
     grad_ws = stack[:, :, cols:].swapaxes(0, 1).reshape(width, width)
 
-    backs += [back_swap] + [swap(a) for a in backs[1:]]
+    backs += [back_swap] + [swap(a, stack) for a in backs[1:]]
     grad_feats = over_rows_call(
-        final_kernel, scal, [grad_pre] + backs, [w_self, w_in, w_out], cols, nodes // 2, 1, True
+        final_kernel, scal, [grad_pre] + backs, [w_self, w_in, w_out], cols, nodes // CORES, 1, True
     )
     return (hidden, grad_feats, grad_ws, agg_grads[0], agg_grads[1])
 

time: 249 us -> 249 us (level)
  waiting for transfers between devices: 154 us -> 151 us
    ppermute x8, waiting for transfers between devices: 45.4 us -> 41.7 us  [x_shift(): lax.ppermute(a, 'wide', [(i, (i + CORES * k) % wide) for i in range(wide)])]
    unnamed x123 -> x129, local copies, waits for them, and re-layouts: 4.96 us -> 8.02 us
  transfers between devices with their start and end apart: 64 -> 64, of which waited for: 26 -> 27; matrix products, arithmetic and copies ran while one was open for 4% -> 4% of each run, Pallas kernels for 0% -> 0%
where the time goes in v5:
time: 249 us; the launch traced here: 248 us
  waiting for transfers between devices  151 us (61%)
  starting transfers between devices  44.1 us (18%)
  Pallas kernels  28.4 us (11%)
  local copies, waits for them, and re-layouts  14.2 us (6%)
  other arithmetic  6.76 us (3%)
    ppermute x13, waiting for transfers between devices, z_shift(): lax.ppermute(a, 'narrow', [(z * ys + y, (z + k) % zs * ys + y) for z in r...  74.7 us
    ppermute x8, waiting for transfers between devices, x_shift(): lax.ppermute(a, 'wide', [(i, (i + CORES * k) % wide) for i in range(wide)])  41.7 us
    ppermute x3, waiting for transfers between devices, meet(): return lax.ppermute(a, 'narrow', [(i, i ^ bit) for i in range(narrow)])  18.1 us
    pallas_call x2, Pallas kernels, aggregate(): pl.pallas_call(functools.partial(aggregate_kernel, wide, cap, side, block...  16.5 us
    ppermute x13, starting transfers between devices, z_shift(): lax.ppermute(a, 'narrow', [(z * ys + y, (z + k) % zs * ys + y) for z in r...  12.3 us
    pallas_call x2, Pallas kernels, over_rows_call(): pl.pallas_call(functools.partial(kernel, parts, cols), grid=(rows // step...  11.8 us
    ppermute x10, starting transfers between devices, y_shift(): lax.ppermute(a, 'narrow', [(z * ys + y, z * ys + (y + k) % ys) for z in r...  10.6 us
    ppermute x10, waiting for transfers between devices, y_shift(): lax.ppermute(a, 'narrow', [(z * ys + y, z * ys + (y + k) % ys) for z in r...  9.32 us
  transfers between devices with their start and end apart: 64, of which 27 were waited for; matrix products, arithmetic and copies ran while one was open for 4% of the time, Pallas kernels for 0%

profile of v5, /device:TPU:0, one launch (start us, length us, event | category | flops | bytes accessed | tf_op | source)
XLA Modules:
  0.0 248.3 jit_solution(6603865122531398848)
XLA Ops:
  0.7 0.8 compare_convert_fusion
  1.5 0.7 convert_reduce_fusion
  2.3 1.8 dynamic_slice.59
  4.2 1.0 fusion.8
  5.3 2.9 %collective-permute-start = (bf16[4,528,128]{2,1,0:T(8,128)(2,1)}, bf16[4,528,128]{2,1,0:T(8,128)(2,1)}, u32[]{:S(2)}, u32[]{:S(2)}) collective-permute-start(bf16[4,528,128]{2,1,0:T(8,128)(2,1)} %get-tuple-element.58), channel_id=1, source_target_pairs={{0,16},{8,24},{16,0},{24,8},{1,17},{9,25},{17,1},{25,9},{2,18},{10... | collective-permute-start | bytes 1622024 | tf_op jit(solution)/shard_map/ppermute | solution.py:22
  9.0 0.9 fusion.9
  9.9 1.5 collective-permute-start.2
  11.4 1.6 collective-permute-start.1
  13.0 12.0 %collective-permute-done.1.refs_22_ = bf16[14,128,128]{2,1,0:T(8,128)(2,1)S(1)} collective-permute-done((bf16[14,128,128]{2,1,0:T(8,128)(2,1)S(1)}, bf16[14,128,128]{2,1,0:T(8,128)(2,1)S(1)}, u32[]{:S(2)}, u32[]{:S(2)}) %collective-permute-start.1) | collective-permute-done | bytes 458784 | tf_op jit(solution)/shard_map/ppermute | solution.py:30
  25.1 0.7 copy-done.33
  26.8 1.2 fusion.16
  28.6 3.3 %collective-permute-start.6 = (bf16[2,528,128]{2,1,0:T(8,128)(2,1)S(1)}, bf16[2,528,128]{2,1,0:T(8,128)(2,1)S(1)}, u32[]{:S(2)}, u32[]{:S(2)}) collective-permute-start(bf16[2,528,128]{2,1,0:T(8,128)(2,1)S(1)} %get-tuple-element.64), channel_id=1, source_target_pairs={{0,6},{1,7},{2,0},{3,1},{4,2},{5,3},{6,4},{7,5},{8,14},{9,15},{10,... | collective-permute-start | bytes 811016 | tf_op jit(solution)/shard_map/ppermute | solution.py:30
  31.9 7.4 %collective-permute-done.5 = bf16[2,528,128]{2,1,0:T(8,128)(2,1)S(1)} collective-permute-done((bf16[2,528,128]{2,1,0:T(8,128)(2,1)S(1)}, bf16[2,528,128]{2,1,0:T(8,128)(2,1)S(1)}, u32[]{:S(2)}, u32[]{:S(2)}) %collective-permute-start.5) | collective-permute-done | bytes 270368 | tf_op jit(solution)/shard_map/ppermute | solution.py:30
  39.4 3.0 %collective-permute-done.6.refs_7_ = bf16[2,528,128]{2,1,0:T(8,128)(2,1)S(1)} collective-permute-done((bf16[2,528,128]{2,1,0:T(8,128)(2,1)S(1)}, bf16[2,528,128]{2,1,0:T(8,128)(2,1)S(1)}, u32[]{:S(2)}, u32[]{:S(2)}) %collective-permute-start.6) | collective-permute-done | bytes 270368 | tf_op jit(solution)/shard_map/ppermute | solution.py:30
  42.5 1.6 collective-permute-start.12
  44.0 1.5 collective-permute-start.8
  46.6 10.4 %collective-permute-done.8.refs_26_ = bf16[14,128,128]{2,1,0:T(8,128)(2,1)S(1)} collective-permute-done((bf16[14,128,128]{2,1,0:T(8,128)(2,1)S(1)}, bf16[14,128,128]{2,1,0:T(8,128)(2,1)S(1)}, u32[]{:S(2)}, u32[]{:S(2)}) %collective-permute-start.8) | collective-permute-done | bytes 458784 | tf_op jit(solution)/shard_map/ppermute | solution.py:30
  57.4 0.9 copy-done.45
  59.0 1.0 collective-permute-start.17
  59.9 7.9 %collective-permute-done.17.refs_10_ = bf16[2,528,128]{2,1,0:T(8,128)(2,1)S(1)} collective-permute-done((bf16[2,528,128]{2,1,0:T(8,128)(2,1)S(1)}, bf16[2,528,128]{2,1,0:T(8,128)(2,1)S(1)}, u32[]{:S(2)}, u32[]{:S(2)}) %collective-permute-start.17) | collective-permute-done | bytes 270368 | tf_op jit(solution)/shard_map/ppermute | solution.py:22
  67.8 5.2 %collective-permute-done.14.refs_30_ = bf16[14,128,128]{2,1,0:T(8,128)(2,1)S(1)} collective-permute-done((bf16[14,128,128]{2,1,0:T(8,128)(2,1)S(1)}, bf16[14,128,128]{2,1,0:T(8,128)(2,1)S(1)}, u32[]{:S(2)}, u32[]{:S(2)}) %collective-permute-start.14) | collective-permute-done | bytes 458784 | tf_op jit(solution)/shard_map/ppermute | solution.py:30
  74.0 14.3 %collective-permute-done.19.refs_8_ = bf16[2,528,128]{2,1,0:T(8,128)(2,1)S(1)} collective-permute-done((bf16[2,528,128]{2,1,0:T(8,128)(2,1)S(1)}, bf16[2,528,128]{2,1,0:T(8,128)(2,1)S(1)}, u32[]{:S(2)}, u32[]{:S(2)}) %collective-permute-start.19) | collective-permute-done | bytes 270368 | tf_op jit(solution)/shard_map/ppermute | solution.py:30
  90.1 7.9 %collective-permute-done.23.refs_11_ = bf16[2,528,128]{2,1,0:T(8,128)(2,1)S(1)} collective-permute-done((bf16[2,528,128]{2,1,0:T(8,128)(2,1)S(1)}, bf16[2,528,128]{2,1,0:T(8,128)(2,1)S(1)}, u32[]{:S(2)}, u32[]{:S(2)}) %collective-permute-start.23) | collective-permute-done | bytes 270368 | tf_op jit(solution)/shard_map/ppermute | solution.py:22
  101.8 0.7 copy-done.21
  102.6 8.3 %shard_map.128.refs_1_ = bf16[3584,128]{1,0:T(8,128)(2,1)} custom-call(s32[10]{0:T(128)} %pad_add_fusion.scal, bf16[8,528,128]{2,1,0:T(8,128)(2,1)} %copy-done, bf16[4,528,128]{2,1,0:T(8,128)(2,1)} %collective-permute-done.refs_1_, bf16[4,528,128]{2,1,0:T(8,128)(2,1)} %copy-done.6, bf16[8,528,128]{2,1,0:T(8,128)(2,1)} %copy-done.3, ...), custom_call_target="tpu_custom_call" | custom-call | flops 536870912 | bytes 31457280 | tf_op jit(solution)/shard_map/pallas_call | solution.py:169
  111.5 1.8 collective-permute-start.34
  113.4 19.9 %collective-permute-done.33.refs_2_ = bf16[3584,128]{1,0:T(8,128)(2,1)S(1)} collective-permute-done((bf16[3584,128]{1,0:T(8,128)(2,1)}, bf16[3584,128]{1,0:T(8,128)(2,1)S(1)}, u32[]{:S(2)}, u32[]{:S(2)}) %collective-permute-start.33) | collective-permute-done | bytes 917536 | tf_op jit(solution)/shard_map/ppermute | solution.py:22
  133.3 1.0 collective-permute-start.35
  134.3 2.1 collective-permute-done.35.refs_4_
  136.4 1.0 copy-done.29
  137.3 6.8 %shard_map.129 = (bf16[3584,256]{1,0:T(8,128)(2,1)}, bf16[3584,256]{1,0:T(8,128)(2,1)}, bf16[1792,128]{1,0:T(8,128)(2,1)}) custom-call(s32[10]{0:T(128)} %pad_add_fusion.scal, bf16[3584,256]{1,0:T(8,128)(2,1)} %refs_0_.1, bf16[3584,128]{1,0:T(8,128)(2,1)} %shard_map.128.refs_1_, bf16[3584,128]{1,0:T(8,128)(2,1)} %copy-done.27, bf16[3584,128]{1,0:T(8,128)(2,1)} %copy-done.28, ...), custom_call_target="tpu_custom_call" | custom-call | tf_op jit(solution)/shard_map/pallas_call | solution.py:276
  144.2 1.8 collective-permute-start.37
  146.4 12.7 %collective-permute-done.36.refs_22_ = bf16[14,128,128]{2,1,0:T(8,128)(2,1)S(1)} collective-permute-done((bf16[14,128,128]{2,1,0:T(8,128)(2,1)}, bf16[14,128,128]{2,1,0:T(8,128)(2,1)S(1)}, u32[]{:S(2)}, u32[]{:S(2)}) %collective-permute-start.36) | collective-permute-done | bytes 458784 | tf_op jit(solution)/shard_map/ppermute | solution.py:30
  159.1 1.8 collective-permute-start.40
  161.4 2.2 fusion
  164.0 9.3 %collective-permute-done.38 = f32[96,256]{1,0:T(8,128)S(1)} collective-permute-done((f32[96,256]{1,0:T(8,128)S(1)}, f32[96,256]{1,0:T(8,128)S(1)}, u32[]{:S(2)}, u32[]{:S(2)}) %collective-permute-start.38) | collective-permute-done | bytes 98336 | tf_op jit(solution)/shard_map/ppermute | solution.py:336
  173.3 0.8 copy-done.39
  174.6 1.7 collective-permute-start.45
  176.7 3.7 %collective-permute-start.43 = (f32[48,256]{1,0:T(8,128)S(1)}, f32[48,256]{1,0:T(8,128)S(1)}, u32[]{:S(2)}, u32[]{:S(2)}) collective-permute-start(f32[48,256]{1,0:T(8,128)S(1)} %dynamic-slice_bitcast_fusion.1), channel_id=1, source_target_pairs={{0,4},{1,5},{2,6},{3,7},{4,0},{5,1},{6,2},{7,3},{8,12},{9,13},{10,... | collective-permute-start | bytes 147464 | tf_op jit(solution)/shard_map/ppermute | solution.py:336
  180.4 8.8 %collective-permute-done.43 = f32[48,256]{1,0:T(8,128)S(1)} collective-permute-done((f32[48,256]{1,0:T(8,128)S(1)}, f32[48,256]{1,0:T(8,128)S(1)}, u32[]{:S(2)}, u32[]{:S(2)}) %collective-permute-start.43) | collective-permute-done | bytes 49184 | tf_op jit(solution)/shard_map/ppermute | solution.py:336
  189.4 1.8 collective-permute-start.49
  191.3 2.2 collective-permute-start.50
  193.7 3.3 %collective-permute-done.49 = bf16[7,128,128]{2,1,0:T(8,128)(2,1)S(1)} collective-permute-done((bf16[7,128,128]{2,1,0:T(8,128)(2,1)S(1)}, bf16[7,128,128]{2,1,0:T(8,128)(2,1)S(1)}, u32[]{:S(2)}, u32[]{:S(2)}) %collective-permute-start.49) | collective-permute-done | bytes 229408 | tf_op jit(solution)/shard_map/ppermute | solution.py:36
  197.1 4.2 %collective-permute-done.50 = bf16[7,128,128]{2,1,0:T(8,128)(2,1)S(1)} collective-permute-done((bf16[7,128,128]{2,1,0:T(8,128)(2,1)S(1)}, bf16[7,128,128]{2,1,0:T(8,128)(2,1)S(1)}, u32[]{:S(2)}, u32[]{:S(2)}) %collective-permute-start.50) | collective-permute-done | bytes 229408 | tf_op jit(solution)/shard_map/ppermute | solution.py:30
  201.4 0.8 copy-done.54
  203.3 3.3 %collective-permute-done.53 = f32[24,256]{1,0:T(8,128)S(1)} collective-permute-done((f32[24,256]{1,0:T(8,128)S(1)}, f32[24,256]{1,0:T(8,128)S(1)}, u32[]{:S(2)}, u32[]{:S(2)}) %collective-permute-start.53) | collective-permute-done | bytes 24608 | tf_op jit(solution)/shard_map/ppermute | solution.py:22
  206.6 0.7 copy-done.57
  207.4 8.2 %shard_map.130.refs_1_ = bf16[3584,128]{1,0:T(8,128)(2,1)} custom-call(s32[10]{0:T(128)} %pad_add_fusion.scal, bf16[8,528,128]{2,1,0:T(8,128)(2,1)} %copy-done, bf16[4,528,128]{2,1,0:T(8,128)(2,1)} %collective-permute-done.refs_1_, bf16[4,528,128]{2,1,0:T(8,128)(2,1)} %copy-done.6, bf16[8,528,128]{2,1,0:T(8,128)(2,1)} %copy-done.3, ...), custom_call_target="tpu_custom_call" | custom-call | flops 536870912 | bytes 31457280 | tf_op jit(solution)/shard_map/pallas_call | solution.py:169
  215.6 0.9 collective-permute-start.57
  217.0 1.8 collective-permute-done.57.refs_3_
  218.8 1.7 collective-permute-start.59
  220.9 3.1 %collective-permute-done.58 = f32[2,24,256]{2,1,0:T(8,128)S(1)} collective-permute-done((f32[2,24,256]{2,1,0:T(8,128)S(1)}, f32[2,24,256]{2,1,0:T(8,128)S(1)}, u32[]{:S(2)}, u32[]{:S(2)}) %collective-permute-start.58) | collective-permute-done | bytes 49184 | tf_op jit(solution)/shard_map/ppermute | solution.py:30
  224.0 2.4 collective-permute-done.60
  226.8 5.6 %collective-permute-done.61 = f32[2,96,256]{2,1,0:T(8,128)S(1)} collective-permute-done((f32[2,96,256]{2,1,0:T(8,128)S(1)}, f32[2,96,256]{2,1,0:T(8,128)S(1)}, u32[]{:S(2)}, u32[]{:S(2)}) %collective-permute-start.61) | collective-permute-done | bytes 196640 | tf_op jit(solution)/shard_map/ppermute | solution.py:36
  232.6 1.7 collective-permute-done.62
  234.3 0.7 copy-done.58
  235.1 1.3 fusion.6
  236.3 2.7 %collective-permute-done.56.refs_2_ = bf16[3584,128]{1,0:T(8,128)(2,1)S(1)} collective-permute-done((bf16[3584,128]{1,0:T(8,128)(2,1)}, bf16[3584,128]{1,0:T(8,128)(2,1)S(1)}, u32[]{:S(2)}, u32[]{:S(2)}) %collective-permute-start.56) | collective-permute-done | bytes 917536 | tf_op jit(solution)/shard_map/ppermute | solution.py:22
  239.3 0.8 copy.63
  240.0 0.7 copy.65
  240.8 0.7 copy.66
  241.5 0.8 fusion.42
  242.4 0.9 copy-done.30
  243.3 5.0 %shard_map.131 = bf16[3584,256]{1,0:T(8,128)(2,1)} custom-call(s32[10]{0:T(128)} %pad_add_fusion.scal, bf16[3584,256]{1,0:T(8,128)(2,1)} %get-tuple-element.92.refs_0_, bf16[3584,128]{1,0:T(8,128)(2,1)} %shard_map.130.refs_1_, bf16[3584,128]{1,0:T(8,128)(2,1)} %copy-done.26, bf16[3584,128]{1,0:T(8,128)(2,1)} %copy-done.25, bf16[3584,128]{1,0:T(8,128)(2,1)} %copy-done.30, ...), custom_call_target="tpu_custom_call" | custom-call | tf_op jit(solution)/shard_map/pallas_call | solution.py:276
  (232 shorter events, 17.5 us)
Async XLA Ops:
  5.3 19.7 %collective-permute-start = (bf16[4,528,128]{2,1,0:T(8,128)(2,1)}, bf16[4,528,128]{2,1,0:T(8,128)(2,1)}, u32[]{:S(2)}, u32[]{:S(2)}) collective-permute-start(bf16[4,528,128]{2,1,0:T(8,128)(2,1)} %get-tuple-element.58), channel_id=1, source_target_pairs={{0,16},{8,24},{16,0},{24,8},{1,17},{9,25},{17,1},{25,9},{2,18},{10... | collective-permute-start | bytes 1622024 | tf_op jit(solution)/shard_map/ppermute | solution.py:22
  9.9 15.1 %collective-permute-start.2 = (bf16[4,528,128]{2,1,0:T(8,128)(2,1)S(1)}, bf16[4,528,128]{2,1,0:T(8,128)(2,1)S(1)}, u32[]{:S(2)}, u32[]{:S(2)}) collective-permute-start(bf16[4,528,128]{2,1,0:T(8,128)(2,1)S(1)} %get-tuple-element.114), channel_id=1, source_target_pairs={{0,1},{1,0},{2,3},{3,2},{4,5},{5,4},{6,7},{7,6},{8,9},{9,8},{10,11... | collective-permute-start | bytes 1622024 | tf_op jit(solution)/shard_map/ppermute | solution.py:36
  11.4 13.6 %collective-permute-start.1 = (bf16[14,128,128]{2,1,0:T(8,128)(2,1)S(1)}, bf16[14,128,128]{2,1,0:T(8,128)(2,1)S(1)}, u32[]{:S(2)}, u32[]{:S(2)}) collective-permute-start(bf16[14,128,128]{2,1,0:T(8,128)(2,1)S(1)} %bitcast.89), channel_id=1, source_target_pairs={{0,2},{1,3},{2,4},{3,5},{4,6},{5,7},{6,0},{7,1},{8,10},{9,11},{10,... | collective-permute-start | bytes 1376264 | tf_op jit(solution)/shard_map/ppermute | solution.py:30
  25.0 17.4 %collective-permute-start.4 = (bf16[8,528,128]{2,1,0:T(8,128)(2,1)S(1)}, bf16[8,528,128]{2,1,0:T(8,128)(2,1)S(1)}, u32[]{:S(2)}, u32[]{:S(2)}) collective-permute-start(bf16[8,528,128]{2,1,0:T(8,128)(2,1)S(1)} %pad_maximum_fusion.refs_0_), channel_id=1, source_target_pairs={{0,8},{8,0},{16,24},{24,16},{1,9},{9,1},{17,25},{25,17},{2,10},{10... | collective-permute-start | bytes 3244040 | tf_op jit(solution)/shard_map/ppermute | solution.py:26
  25.8 16.7 %collective-permute-start.3 = (bf16[4,528,128]{2,1,0:T(8,128)(2,1)}, bf16[4,528,128]{2,1,0:T(8,128)(2,1)S(1)}, u32[]{:S(2)}, u32[]{:S(2)}) collective-permute-start(bf16[4,528,128]{2,1,0:T(8,128)(2,1)} %get-tuple-element.60), channel_id=1, source_target_pairs={{0,16},{8,24},{16,0},{24,8},{1,17},{9,25},{17,1},{25,9},{2,18},{10... | collective-permute-start | bytes 1622024 | tf_op jit(solution)/shard_map/ppermute | solution.py:22
  26.3 16.1 %collective-permute-start.7 = (bf16[14,128,128]{2,1,0:T(8,128)(2,1)}, bf16[14,128,128]{2,1,0:T(8,128)(2,1)S(1)}, u32[]{:S(2)}, u32[]{:S(2)}) collective-permute-start(bf16[14,128,128]{2,1,0:T(8,128)(2,1)} %bitcast.87), channel_id=1, source_target_pairs={{0,1},{1,0},{2,3},{3,2},{4,5},{5,4},{6,7},{7,6},{8,9},{9,8},{10,11... | collective-permute-start | bytes 1376264 | tf_op jit(solution)/shard_map/ppermute | solution.py:36
  28.0 11.3 %collective-permute-start.5 = (bf16[2,528,128]{2,1,0:T(8,128)(2,1)S(1)}, bf16[2,528,128]{2,1,0:T(8,128)(2,1)S(1)}, u32[]{:S(2)}, u32[]{:S(2)}) collective-permute-start(bf16[2,528,128]{2,1,0:T(8,128)(2,1)S(1)} %get-tuple-element.63), channel_id=1, source_target_pairs={{0,2},{1,3},{2,4},{3,5},{4,6},{5,7},{6,0},{7,1},{8,10},{9,11},{10,... | collective-permute-start | bytes 811016 | tf_op jit(solution)/shard_map/ppermute | solution.py:30
  28.6 13.8 %collective-permute-start.6 = (bf16[2,528,128]{2,1,0:T(8,128)(2,1)S(1)}, bf16[2,528,128]{2,1,0:T(8,128)(2,1)S(1)}, u32[]{:S(2)}, u32[]{:S(2)}) collective-permute-start(bf16[2,528,128]{2,1,0:T(8,128)(2,1)S(1)} %get-tuple-element.64), channel_id=1, source_target_pairs={{0,6},{1,7},{2,0},{3,1},{4,2},{5,3},{6,4},{7,5},{8,14},{9,15},{10,... | collective-permute-start | bytes 811016 | tf_op jit(solution)/shard_map/ppermute | solution.py:30
  42.5 15.8 %collective-permute-start.12 = (bf16[4,528,128]{2,1,0:T(8,128)(2,1)S(1)}, bf16[4,528,128]{2,1,0:T(8,128)(2,1)S(1)}, u32[]{:S(2)}, u32[]{:S(2)}) collective-permute-start(bf16[4,528,128]{2,1,0:T(8,128)(2,1)S(1)} %constant_dynamic-update-slice_fusion.refs_6_), channel_id=1, source_target_pairs={{0,16},{8,24},{16,0},{24,8},{1,17},{9,25},{17,1},{25,9},{2,18},{10... | collective-permute-start | bytes 1622024 | tf_op jit(solution)/shard_map/ppermute | solution.py:22
  44.0 13.0 %collective-permute-start.8 = (bf16[14,128,128]{2,1,0:T(8,128)(2,1)S(1)}, bf16[14,128,128]{2,1,0:T(8,128)(2,1)S(1)}, u32[]{:S(2)}, u32[]{:S(2)}) collective-permute-start(bf16[14,128,128]{2,1,0:T(8,128)(2,1)S(1)} %copy-done.34), channel_id=1, source_target_pairs={{0,2},{1,3},{2,4},{3,5},{4,6},{5,7},{6,0},{7,1},{8,10},{9,11},{10,... | collective-permute-start | bytes 1376264 | tf_op jit(solution)/shard_map/ppermute | solution.py:30
  45.5 11.9 %collective-permute-start.9 = (bf16[14,128,128]{2,1,0:T(8,128)(2,1)S(1)}, bf16[14,128,128]{2,1,0:T(8,128)(2,1)S(1)}, u32[]{:S(2)}, u32[]{:S(2)}) collective-permute-start(bf16[14,128,128]{2,1,0:T(8,128)(2,1)S(1)} %copy-done.34), channel_id=1, source_target_pairs={{0,1},{1,0},{2,3},{3,2},{4,5},{5,4},{6,7},{7,6},{8,9},{9,8},{10,11... | collective-permute-start | bytes 1376264 | tf_op jit(solution)/shard_map/ppermute | solution.py:36
  46.1 11.3 %collective-permute-start.10 = (bf16[14,128,128]{2,1,0:T(8,128)(2,1)S(1)}, bf16[14,128,128]{2,1,0:T(8,128)(2,1)S(1)}, u32[]{:S(2)}, u32[]{:S(2)}) collective-permute-start(bf16[14,128,128]{2,1,0:T(8,128)(2,1)S(1)} %bitcast.90), channel_id=1, source_target_pairs={{0,8},{8,0},{16,24},{24,16},{1,9},{9,1},{17,25},{25,17},{2,10},{10... | collective-permute-start | bytes 1376264 | tf_op jit(solution)/shard_map/ppermute | solution.py:26
  46.1 11.3 %collective-permute-start.11 = (bf16[14,128,128]{2,1,0:T(8,128)(2,1)S(1)}, bf16[14,128,128]{2,1,0:T(8,128)(2,1)S(1)}, u32[]{:S(2)}, u32[]{:S(2)}) collective-permute-start(bf16[14,128,128]{2,1,0:T(8,128)(2,1)S(1)} %copy-done.34), channel_id=1, source_target_pairs={{0,8},{8,0},{16,24},{24,16},{1,9},{9,1},{17,25},{25,17},{2,10},{10... | collective-permute-start | bytes 1376264 | tf_op jit(solution)/shard_map/ppermute | solution.py:26
  58.3 14.8 %collective-permute-start.13 = (bf16[4,528,128]{2,1,0:T(8,128)(2,1)}, bf16[4,528,128]{2,1,0:T(8,128)(2,1)S(1)}, u32[]{:S(2)}, u32[]{:S(2)}) collective-permute-start(bf16[4,528,128]{2,1,0:T(8,128)(2,1)} %collective-permute-done.refs_1_), channel_id=1, source_target_pairs={{0,8},{8,0},{16,24},{24,16},{1,9},{9,1},{17,25},{25,17},{2,10},{10... | collective-permute-start | bytes 1622024 | tf_op jit(solution)/shard_map/ppermute | solution.py:26
  58.3 14.7 %collective-permute-start.14 = (bf16[14,128,128]{2,1,0:T(8,128)(2,1)S(1)}, bf16[14,128,128]{2,1,0:T(8,128)(2,1)S(1)}, u32[]{:S(2)}, u32[]{:S(2)}) collective-permute-start(bf16[14,128,128]{2,1,0:T(8,128)(2,1)S(1)} %collective-permute-done.8.refs_26_), channel_id=1, source_target_pairs={{0,2},{1,3},{2,4},{3,5},{4,6},{5,7},{6,0},{7,1},{8,10},{9,11},{10,... | collective-permute-start | bytes 1376264 | tf_op jit(solution)/shard_map/ppermute | solution.py:30
  58.8 14.2 %collective-permute-start.15 = (bf16[14,128,128]{2,1,0:T(8,128)(2,1)S(1)}, bf16[14,128,128]{2,1,0:T(8,128)(2,1)S(1)}, u32[]{:S(2)}, u32[]{:S(2)}) collective-permute-start(bf16[14,128,128]{2,1,0:T(8,128)(2,1)S(1)} %collective-permute-done.8.refs_26_), channel_id=1, source_target_pairs={{0,1},{1,0},{2,3},{3,2},{4,5},{5,4},{6,7},{7,6},{8,9},{9,8},{10,11... | collective-permute-start | bytes 1376264 | tf_op jit(solution)/shard_map/ppermute | solution.py:36
  58.9 14.1 %collective-permute-start.16 = (bf16[14,128,128]{2,1,0:T(8,128)(2,1)S(1)}, bf16[14,128,128]{2,1,0:T(8,128)(2,1)S(1)}, u32[]{:S(2)}, u32[]{:S(2)}) collective-permute-start(bf16[14,128,128]{2,1,0:T(8,128)(2,1)S(1)} %collective-permute-done.7.refs_20_), channel_id=1, source_target_pairs={{0,8},{8,0},{16,24},{24,16},{1,9},{9,1},{17,25},{25,17},{2,10},{10... | collective-permute-start | bytes 1376264 | tf_op jit(solution)/shard_map/ppermute | solution.py:26
  59.0 8.9 %collective-permute-start.17 = (bf16[2,528,128]{2,1,0:T(8,128)(2,1)S(1)}, bf16[2,528,128]{2,1,0:T(8,128)(2,1)S(1)}, u32[]{:S(2)}, u32[]{:S(2)}) collective-permute-start(bf16[2,528,128]{2,1,0:T(8,128)(2,1)S(1)} %collective-permute-done.6.refs_7_), channel_id=1, source_target_pairs={{0,16},{8,24},{16,0},{24,8},{1,17},{9,25},{17,1},{25,9},{2,18},{10... | collective-permute-start | bytes 811016 | tf_op jit(solution)/shard_map/ppermute | solution.py:22
  73.1 15.3 %collective-permute-start.18 = (bf16[4,528,128]{2,1,0:T(8,128)(2,1)S(1)}, bf16[4,528,128]{2,1,0:T(8,128)(2,1)S(1)}, u32[]{:S(2)}, u32[]{:S(2)}) collective-permute-start(bf16[4,528,128]{2,1,0:T(8,128)(2,1)S(1)} %collective-permute-done.3.refs_2_), channel_id=1, source_target_pairs={{0,8},{8,0},{16,24},{24,16},{1,9},{9,1},{17,25},{25,17},{2,10},{10... | collective-permute-start | bytes 1622024 | tf_op jit(solution)/shard_map/ppermute | solution.py:26
  73.2 15.2 %collective-permute-start.20 = (bf16[14,128,128]{2,1,0:T(8,128)(2,1)S(1)}, bf16[14,128,128]{2,1,0:T(8,128)(2,1)S(1)}, u32[]{:S(2)}, u32[]{:S(2)}) collective-permute-start(bf16[14,128,128]{2,1,0:T(8,128)(2,1)S(1)} %collective-permute-done.14.refs_30_), channel_id=1, source_target_pairs={{0,1},{1,0},{2,3},{3,2},{4,5},{5,4},{6,7},{7,6},{8,9},{9,8},{10,11... | collective-permute-start | bytes 1376264 | tf_op jit(solution)/shard_map/ppermute | solution.py:36
  73.5 14.8 %collective-permute-start.21 = (bf16[14,128,128]{2,1,0:T(8,128)(2,1)S(1)}, bf16[14,128,128]{2,1,0:T(8,128)(2,1)S(1)}, u32[]{:S(2)}, u32[]{:S(2)}) collective-permute-start(bf16[14,128,128]{2,1,0:T(8,128)(2,1)S(1)} %collective-permute-done.8.refs_26_), channel_id=1, source_target_pairs={{0,8},{8,0},{16,24},{24,16},{1,9},{9,1},{17,25},{25,17},{2,10},{10... | collective-permute-start | bytes 1376264 | tf_op jit(solution)/shard_map/ppermute | solution.py:26
  73.7 14.7 %collective-permute-start.22 = (bf16[14,128,128]{2,1,0:T(8,128)(2,1)S(1)}, bf16[14,128,128]{2,1,0:T(8,128)(2,1)S(1)}, u32[]{:S(2)}, u32[]{:S(2)}) collective-permute-start(bf16[14,128,128]{2,1,0:T(8,128)(2,1)S(1)} %collective-permute-done.9.refs_24_), channel_id=1, source_target_pairs={{0,8},{8,0},{16,24},{24,16},{1,9},{9,1},{17,25},{25,17},{2,10},{10... | collective-permute-start | bytes 1376264 | tf_op jit(solution)/shard_map/ppermute | solution.py:26
  74.0 14.3 %collective-permute-start.19 = (bf16[2,528,128]{2,1,0:T(8,128)(2,1)S(1)}, bf16[2,528,128]{2,1,0:T(8,128)(2,1)S(1)}, u32[]{:S(2)}, u32[]{:S(2)}) collective-permute-start(bf16[2,528,128]{2,1,0:T(8,128)(2,1)S(1)} %get-tuple-element.75), channel_id=1, source_target_pairs={{0,4},{1,5},{2,6},{3,7},{4,0},{5,1},{6,2},{7,3},{8,12},{9,13},{10,... | collective-permute-start | bytes 811016 | tf_op jit(solution)/shard_map/ppermute | solution.py:30
  88.4 9.6 %collective-permute-start.24 = (bf16[4,528,128]{2,1,0:T(8,128)(2,1)S(1)}, bf16[4,528,128]{2,1,0:T(8,128)(2,1)S(1)}, u32[]{:S(2)}, u32[]{:S(2)}) collective-permute-start(bf16[4,528,128]{2,1,0:T(8,128)(2,1)S(1)} %constant_dynamic-update-slice_fusion.refs_6_), channel_id=1, source_target_pairs={{0,8},{8,0},{16,24},{24,16},{1,9},{9,1},{17,25},{25,17},{2,10},{10... | collective-permute-start | bytes 1622024 | tf_op jit(solution)/shard_map/ppermute | solution.py:26
  88.5 9.5 %collective-permute-start.27 = (bf16[4,528,128]{2,1,0:T(8,128)(2,1)S(1)}, bf16[4,528,128]{2,1,0:T(8,128)(2,1)S(1)}, u32[]{:S(2)}, u32[]{:S(2)}) collective-permute-start(bf16[4,528,128]{2,1,0:T(8,128)(2,1)S(1)} %collective-permute-done.12.refs_9_), channel_id=1, source_target_pairs={{0,8},{8,0},{16,24},{24,16},{1,9},{9,1},{17,25},{25,17},{2,10},{10... | collective-permute-start | bytes 1622024 | tf_op jit(solution)/shard_map/ppermute | solution.py:26
  89.0 9.0 %collective-permute-start.25 = (bf16[14,128,128]{2,1,0:T(8,128)(2,1)S(1)}, bf16[14,128,128]{2,1,0:T(8,128)(2,1)S(1)}, u32[]{:S(2)}, u32[]{:S(2)}) collective-permute-start(bf16[14,128,128]{2,1,0:T(8,128)(2,1)S(1)} %collective-permute-done.14.refs_30_), channel_id=1, source_target_pairs={{0,8},{8,0},{16,24},{24,16},{1,9},{9,1},{17,25},{25,17},{2,10},{10... | collective-permute-start | bytes 1376264 | tf_op jit(solution)/shard_map/ppermute | solution.py:26
  89.1 8.9 %collective-permute-start.26 = (bf16[14,128,128]{2,1,0:T(8,128)(2,1)S(1)}, bf16[14,128,128]{2,1,0:T(8,128)(2,1)S(1)}, u32[]{:S(2)}, u32[]{:S(2)}) collective-permute-start(bf16[14,128,128]{2,1,0:T(8,128)(2,1)S(1)} %collective-permute-done.15.refs_28_), channel_id=1, source_target_pairs={{0,8},{8,0},{16,24},{24,16},{1,9},{9,1},{17,25},{25,17},{2,10},{10... | collective-permute-start | bytes 1376264 | tf_op jit(solution)/shard_map/ppermute | solution.py:26
  89.5 8.5 %collective-permute-start.23 = (bf16[2,528,128]{2,1,0:T(8,128)(2,1)S(1)}, bf16[2,528,128]{2,1,0:T(8,128)(2,1)S(1)}, u32[]{:S(2)}, u32[]{:S(2)}) collective-permute-start(bf16[2,528,128]{2,1,0:T(8,128)(2,1)S(1)} %collective-permute-done.19.refs_8_), channel_id=1, source_target_pairs={{0,16},{8,24},{16,0},{24,8},{1,17},{9,25},{17,1},{25,9},{2,18},{10... | collective-permute-start | bytes 811016 | tf_op jit(solution)/shard_map/ppermute | solution.py:22
  98.1 4.5 %collective-permute-start.32 = (bf16[14,128,128]{2,1,0:T(8,128)(2,1)S(1)}, bf16[14,128,128]{2,1,0:T(8,128)(2,1)}, u32[]{:S(2)}, u32[]{:S(2)}) collective-permute-start(bf16[14,128,128]{2,1,0:T(8,128)(2,1)S(1)} %collective-permute-done.20.refs_32_), channel_id=1, source_target_pairs={{0,8},{8,0},{16,24},{24,16},{1,9},{9,1},{17,25},{25,17},{2,10},{10... | collective-permute-start | bytes 1376264 | tf_op jit(solution)/shard_map/ppermute | solution.py:26
  98.1 2.2 collective-permute-start.28
  98.6 2.1 collective-permute-start.29
  98.7 2.4 collective-permute-start.30
  99.2 2.3 collective-permute-start.31
  111.0 22.3 %collective-permute-start.33 = (bf16[3584,128]{1,0:T(8,128)(2,1)}, bf16[3584,128]{1,0:T(8,128)(2,1)S(1)}, u32[]{:S(2)}, u32[]{:S(2)}) collective-permute-start(bf16[3584,128]{1,0:T(8,128)(2,1)} %shard_map.128.refs_1_), channel_id=1, source_target_pairs={{0,16},{8,24},{16,0},{24,8},{1,17},{9,25},{17,1},{25,9},{2,18},{10... | collective-permute-start | bytes 2752520 | tf_op jit(solution)/shard_map/ppermute | solution.py:22
  111.5 22.7 %collective-permute-start.34 = (bf16[3584,128]{1,0:T(8,128)(2,1)}, bf16[3584,128]{1,0:T(8,128)(2,1)S(1)}, u32[]{:S(2)}, u32[]{:S(2)}) collective-permute-start(bf16[3584,128]{1,0:T(8,128)(2,1)} %shard_map.128.refs_1_), channel_id=1, source_target_pairs={{0,8},{8,0},{16,24},{24,16},{1,9},{9,1},{17,25},{25,17},{2,10},{10... | collective-permute-start | bytes 2752520 | tf_op jit(solution)/shard_map/ppermute | solution.py:26
  133.3 3.1 %collective-permute-start.35 = (bf16[3584,128]{1,0:T(8,128)(2,1)S(1)}, bf16[3584,128]{1,0:T(8,128)(2,1)S(1)}, u32[]{:S(2)}, u32[]{:S(2)}) collective-permute-start(bf16[3584,128]{1,0:T(8,128)(2,1)S(1)} %collective-permute-done.33.refs_2_), channel_id=1, source_target_pairs={{0,8},{8,0},{16,24},{24,16},{1,9},{9,1},{17,25},{25,17},{2,10},{10... | collective-permute-start | bytes 2752520 | tf_op jit(solution)/shard_map/ppermute | solution.py:26
  144.2 14.9 %collective-permute-start.36 = (bf16[14,128,128]{2,1,0:T(8,128)(2,1)}, bf16[14,128,128]{2,1,0:T(8,128)(2,1)S(1)}, u32[]{:S(2)}, u32[]{:S(2)}) collective-permute-start(bf16[14,128,128]{2,1,0:T(8,128)(2,1)} %bitcast.103), channel_id=1, source_target_pairs={{0,2},{1,3},{2,4},{3,5},{4,6},{5,7},{6,0},{7,1},{8,10},{9,11},{10,... | collective-permute-start | bytes 1376264 | tf_op jit(solution)/shard_map/ppermute | solution.py:30
  144.2 14.8 %collective-permute-start.37 = (bf16[14,128,128]{2,1,0:T(8,128)(2,1)}, bf16[14,128,128]{2,1,0:T(8,128)(2,1)S(1)}, u32[]{:S(2)}, u32[]{:S(2)}) collective-permute-start(bf16[14,128,128]{2,1,0:T(8,128)(2,1)} %bitcast.104), channel_id=1, source_target_pairs={{0,1},{1,0},{2,3},{3,2},{4,5},{5,4},{6,7},{7,6},{8,9},{9,8},{10,11... | collective-permute-start | bytes 1376264 | tf_op jit(solution)/shard_map/ppermute | solution.py:36
  159.0 14.2 %collective-permute-start.39 = (bf16[14,128,128]{2,1,0:T(8,128)(2,1)S(1)}, bf16[14,128,128]{2,1,0:T(8,128)(2,1)S(1)}, u32[]{:S(2)}, u32[]{:S(2)}) collective-permute-start(bf16[14,128,128]{2,1,0:T(8,128)(2,1)S(1)} %collective-permute-done.36.refs_22_), channel_id=1, source_target_pairs={{0,2},{1,3},{2,4},{3,5},{4,6},{5,7},{6,0},{7,1},{8,10},{9,11},{10,... | collective-permute-start | bytes 1376264 | tf_op jit(solution)/shard_map/ppermute | solution.py:30
  159.1 14.2 %collective-permute-start.40 = (bf16[14,128,128]{2,1,0:T(8,128)(2,1)S(1)}, bf16[14,128,128]{2,1,0:T(8,128)(2,1)}, u32[]{:S(2)}, u32[]{:S(2)}) collective-permute-start(bf16[14,128,128]{2,1,0:T(8,128)(2,1)S(1)} %collective-permute-done.36.refs_22_), channel_id=1, source_target_pairs={{0,1},{1,0},{2,3},{3,2},{4,5},{5,4},{6,7},{7,6},{8,9},{9,8},{10,11... | collective-permute-start | bytes 1376264 | tf_op jit(solution)/shard_map/ppermute | solution.py:36
  160.9 13.2 %collective-permute-start.42 = (bf16[14,128,128]{2,1,0:T(8,128)(2,1)S(1)}, bf16[14,128,128]{2,1,0:T(8,128)(2,1)}, u32[]{:S(2)}, u32[]{:S(2)}) collective-permute-start(bf16[14,128,128]{2,1,0:T(8,128)(2,1)S(1)} %collective-permute-done.36.refs_22_), channel_id=1, source_target_pairs={{0,8},{8,0},{16,24},{24,16},{1,9},{9,1},{17,25},{25,17},{2,10},{10... | collective-permute-start | bytes 1376264 | tf_op jit(solution)/shard_map/ppermute | solution.py:26
  160.9 12.4 %collective-permute-start.41 = (bf16[14,128,128]{2,1,0:T(8,128)(2,1)S(1)}, bf16[14,128,128]{2,1,0:T(8,128)(2,1)S(1)}, u32[]{:S(2)}, u32[]{:S(2)}) collective-permute-start(bf16[14,128,128]{2,1,0:T(8,128)(2,1)S(1)} %bitcast.106), channel_id=1, source_target_pairs={{0,8},{8,0},{16,24},{24,16},{1,9},{9,1},{17,25},{25,17},{2,10},{10... | collective-permute-start | bytes 1376264 | tf_op jit(solution)/shard_map/ppermute | solution.py:26
  163.6 9.6 %collective-permute-start.38 = (f32[96,256]{1,0:T(8,128)S(1)}, f32[96,256]{1,0:T(8,128)S(1)}, u32[]{:S(2)}, u32[]{:S(2)}) collective-permute-start(f32[96,256]{1,0:T(8,128)S(1)} %dynamic-slice_bitcast_fusion), channel_id=1, source_target_pairs={{0,1},{1,0},{2,3},{3,2},{4,5},{5,4},{6,7},{7,6},{8,9},{9,8},{10,11... | collective-permute-start | bytes 294920 | tf_op jit(solution)/shard_map/ppermute | solution.py:336
  174.1 15.1 %collective-permute-start.44 = (bf16[14,128,128]{2,1,0:T(8,128)(2,1)S(1)}, bf16[14,128,128]{2,1,0:T(8,128)(2,1)S(1)}, u32[]{:S(2)}, u32[]{:S(2)}) collective-permute-start(bf16[14,128,128]{2,1,0:T(8,128)(2,1)S(1)} %collective-permute-done.39.refs_26_), channel_id=1, source_target_pairs={{0,2},{1,3},{2,4},{3,5},{4,6},{5,7},{6,0},{7,1},{8,10},{9,11},{10,... | collective-permute-start | bytes 1376264 | tf_op jit(solution)/shard_map/ppermute | solution.py:30
  174.6 14.7 %collective-permute-start.45 = (bf16[14,128,128]{2,1,0:T(8,128)(2,1)S(1)}, bf16[14,128,128]{2,1,0:T(8,128)(2,1)S(1)}, u32[]{:S(2)}, u32[]{:S(2)}) collective-permute-start(bf16[14,128,128]{2,1,0:T(8,128)(2,1)S(1)} %collective-permute-done.39.refs_26_), channel_id=1, source_target_pairs={{0,1},{1,0},{2,3},{3,2},{4,5},{5,4},{6,7},{7,6},{8,9},{9,8},{10,11... | collective-permute-start | bytes 1376264 | tf_op jit(solution)/shard_map/ppermute | solution.py:36
  176.2 13.1 %collective-permute-start.46 = (bf16[14,128,128]{2,1,0:T(8,128)(2,1)S(1)}, bf16[14,128,128]{2,1,0:T(8,128)(2,1)S(1)}, u32[]{:S(2)}, u32[]{:S(2)}) collective-permute-start(bf16[14,128,128]{2,1,0:T(8,128)(2,1)S(1)} %collective-permute-done.37.refs_20_), channel_id=1, source_target_pairs={{0,8},{8,0},{16,24},{24,16},{1,9},{9,1},{17,25},{25,17},{2,10},{10... | collective-permute-start | bytes 1376264 | tf_op jit(solution)/shard_map/ppermute | solution.py:26
  176.2 13.1 %collective-permute-start.47 = (bf16[14,128,128]{2,1,0:T(8,128)(2,1)S(1)}, bf16[14,128,128]{2,1,0:T(8,128)(2,1)S(1)}, u32[]{:S(2)}, u32[]{:S(2)}) collective-permute-start(bf16[14,128,128]{2,1,0:T(8,128)(2,1)S(1)} %collective-permute-done.39.refs_26_), channel_id=1, source_target_pairs={{0,8},{8,0},{16,24},{24,16},{1,9},{9,1},{17,25},{25,17},{2,10},{10... | collective-permute-start | bytes 1376264 | tf_op jit(solution)/shard_map/ppermute | solution.py:26
  176.7 12.5 %collective-permute-start.43 = (f32[48,256]{1,0:T(8,128)S(1)}, f32[48,256]{1,0:T(8,128)S(1)}, u32[]{:S(2)}, u32[]{:S(2)}) collective-permute-start(f32[48,256]{1,0:T(8,128)S(1)} %dynamic-slice_bitcast_fusion.1), channel_id=1, source_target_pairs={{0,4},{1,5},{2,6},{3,7},{4,0},{5,1},{6,2},{7,3},{8,12},{9,13},{10,... | collective-permute-start | bytes 147464 | tf_op jit(solution)/shard_map/ppermute | solution.py:336
  189.3 4.4 %collective-permute-start.48 = (f32[24,256]{1,0:T(8,128)S(1)}, f32[24,256]{1,0:T(8,128)S(1)}, u32[]{:S(2)}, u32[]{:S(2)}) collective-permute-start(f32[24,256]{1,0:T(8,128)S(1)} %dynamic-slice_bitcast_fusion.2), channel_id=1, source_target_pairs={{0,2},{1,3},{2,0},{3,1},{4,6},{5,7},{6,4},{7,5},{8,10},{9,11},{10,... | collective-permute-start | bytes 73736 | tf_op jit(solution)/shard_map/ppermute | solution.py:336
  189.4 7.6 %collective-permute-start.49 = (bf16[7,128,128]{2,1,0:T(8,128)(2,1)S(1)}, bf16[7,128,128]{2,1,0:T(8,128)(2,1)S(1)}, u32[]{:S(2)}, u32[]{:S(2)}) collective-permute-start(bf16[7,128,128]{2,1,0:T(8,128)(2,1)S(1)} %slice.28), channel_id=1, source_target_pairs={{0,1},{1,0},{2,3},{3,2},{4,5},{5,4},{6,7},{7,6},{8,9},{9,8},{10,11... | collective-permute-start | bytes 688136 | tf_op jit(solution)/shard_map/ppermute | solution.py:36
  191.2 10.1 %collective-permute-start.52 = (bf16[14,128,128]{2,1,0:T(8,128)(2,1)S(1)}, bf16[14,128,128]{2,1,0:T(8,128)(2,1)S(1)}, u32[]{:S(2)}, u32[]{:S(2)}) collective-permute-start(bf16[14,128,128]{2,1,0:T(8,128)(2,1)S(1)} %collective-permute-done.44.refs_30_), channel_id=1, source_target_pairs={{0,8},{8,0},{16,24},{24,16},{1,9},{9,1},{17,25},{25,17},{2,10},{10... | collective-permute-start | bytes 1376264 | tf_op jit(solution)/shard_map/ppermute | solution.py:26
  191.3 10.0 %collective-permute-start.50 = (bf16[7,128,128]{2,1,0:T(8,128)(2,1)S(1)}, bf16[7,128,128]{2,1,0:T(8,128)(2,1)S(1)}, u32[]{:S(2)}, u32[]{:S(2)}) collective-permute-start(bf16[7,128,128]{2,1,0:T(8,128)(2,1)S(1)} %slice.29), channel_id=1, source_target_pairs={{0,2},{1,3},{2,4},{3,5},{4,6},{5,7},{6,0},{7,1},{8,10},{9,11},{10,... | collective-permute-start | bytes 688136 | tf_op jit(solution)/shard_map/ppermute | solution.py:30
  193.5 7.9 %collective-permute-start.51 = (bf16[14,128,128]{2,1,0:T(8,128)(2,1)}, bf16[14,128,128]{2,1,0:T(8,128)(2,1)S(1)}, u32[]{:S(2)}, u32[]{:S(2)}) collective-permute-start(bf16[14,128,128]{2,1,0:T(8,128)(2,1)} %collective-permute-done.40.refs_24_), channel_id=1, source_target_pairs={{0,8},{8,0},{16,24},{24,16},{1,9},{9,1},{17,25},{25,17},{2,10},{10... | collective-permute-start | bytes 1376264 | tf_op jit(solution)/shard_map/ppermute | solution.py:26
  202.2 4.4 %collective-permute-start.54 = (bf16[14,128,128]{2,1,0:T(8,128)(2,1)S(1)}, bf16[14,128,128]{2,1,0:T(8,128)(2,1)S(1)}, u32[]{:S(2)}, u32[]{:S(2)}) collective-permute-start(bf16[14,128,128]{2,1,0:T(8,128)(2,1)S(1)} %collective-permute-done.45.refs_28_), channel_id=1, source_target_pairs={{0,8},{8,0},{16,24},{24,16},{1,9},{9,1},{17,25},{25,17},{2,10},{10... | collective-permute-start | bytes 1376264 | tf_op jit(solution)/shard_map/ppermute | solution.py:26
  202.2 4.4 %collective-permute-start.55 = (bf16[14,128,128]{2,1,0:T(8,128)(2,1)S(1)}, bf16[14,128,128]{2,1,0:T(8,128)(2,1)}, u32[]{:S(2)}, u32[]{:S(2)}) collective-permute-start(bf16[14,128,128]{2,1,0:T(8,128)(2,1)S(1)} %constant_dynamic-update-slice_fusion.2.refs_32_), channel_id=1, source_target_pairs={{0,8},{8,0},{16,24},{24,16},{1,9},{9,1},{17,25},{25,17},{2,10},{10... | collective-permute-start | bytes 1376264 | tf_op jit(solution)/shard_map/ppermute | solution.py:26
  202.7 3.8 %collective-permute-start.53 = (f32[24,256]{1,0:T(8,128)S(1)}, f32[24,256]{1,0:T(8,128)S(1)}, u32[]{:S(2)}, u32[]{:S(2)}) collective-permute-start(f32[24,256]{1,0:T(8,128)S(1)} %bitcast_add_fusion.2), channel_id=1, source_target_pairs={{0,16},{8,24},{16,0},{24,8},{1,17},{9,25},{17,1},{25,9},{2,18},{10... | collective-permute-start | bytes 73736 | tf_op jit(solution)/shard_map/ppermute | solution.py:22
  215.6 3.2 %collective-permute-start.57 = (bf16[3584,128]{1,0:T(8,128)(2,1)}, bf16[3584,128]{1,0:T(8,128)(2,1)S(1)}, u32[]{:S(2)}, u32[]{:S(2)}) collective-permute-start(bf16[3584,128]{1,0:T(8,128)(2,1)} %shard_map.130.refs_1_), channel_id=1, source_target_pairs={{0,8},{8,0},{16,24},{24,16},{1,9},{9,1},{17,25},{25,17},{2,10},{10... | collective-permute-start | bytes 2752520 | tf_op jit(solution)/shard_map/ppermute | solution.py:26
  216.5 22.6 %collective-permute-start.56 = (bf16[3584,128]{1,0:T(8,128)(2,1)}, bf16[3584,128]{1,0:T(8,128)(2,1)S(1)}, u32[]{:S(2)}, u32[]{:S(2)}) collective-permute-start(bf16[3584,128]{1,0:T(8,128)(2,1)} %shard_map.130.refs_1_), channel_id=1, source_target_pairs={{0,16},{8,24},{16,0},{24,8},{1,17},{9,25},{17,1},{25,9},{2,18},{10... | collective-permute-start | bytes 2752520 | tf_op jit(solution)/shard_map/ppermute | solution.py:22
  218.8 5.2 %collective-permute-start.58 = (f32[2,24,256]{2,1,0:T(8,128)S(1)}, f32[2,24,256]{2,1,0:T(8,128)S(1)}, u32[]{:S(2)}, u32[]{:S(2)}) collective-permute-start(f32[2,24,256]{2,1,0:T(8,128)S(1)} %fusion.29), channel_id=1, source_target_pairs={{0,6},{1,7},{2,0},{3,1},{4,2},{5,3},{6,4},{7,5},{8,14},{9,15},{10,... | collective-permute-start | bytes 147464 | tf_op jit(solution)/shard_map/ppermute | solution.py:30
  218.8 5.2 %collective-permute-start.59 = (f32[2,24,256]{2,1,0:T(8,128)S(1)}, f32[2,24,256]{2,1,0:T(8,128)S(1)}, u32[]{:S(2)}, u32[]{:S(2)}) collective-permute-start(f32[2,24,256]{2,1,0:T(8,128)S(1)} %fusion.29), channel_id=1, source_target_pairs={{0,4},{1,5},{2,6},{3,7},{4,0},{5,1},{6,2},{7,3},{8,12},{9,13},{10,... | collective-permute-start | bytes 147464 | tf_op jit(solution)/shard_map/ppermute | solution.py:30
  220.5 5.9 %collective-permute-start.60 = (f32[2,24,256]{2,1,0:T(8,128)S(1)}, f32[2,24,256]{2,1,0:T(8,128)S(1)}, u32[]{:S(2)}, u32[]{:S(2)}) collective-permute-start(f32[2,24,256]{2,1,0:T(8,128)S(1)} %fusion.29), channel_id=1, source_target_pairs={{0,2},{1,3},{2,4},{3,5},{4,6},{5,7},{6,0},{7,1},{8,10},{9,11},{10,... | collective-permute-start | bytes 147464 | tf_op jit(solution)/shard_map/ppermute | solution.py:30
  226.5 6.0 %collective-permute-start.61 = (f32[2,96,256]{2,1,0:T(8,128)S(1)}, f32[2,96,256]{2,1,0:T(8,128)S(1)}, u32[]{:S(2)}, u32[]{:S(2)}) collective-permute-start(f32[2,96,256]{2,1,0:T(8,128)S(1)} %bitcast.93), channel_id=1, source_target_pairs={{0,1},{1,0},{2,3},{3,2},{4,5},{5,4},{6,7},{7,6},{8,9},{9,8},{10,11... | collective-permute-start | bytes 589832 | tf_op jit(solution)/shard_map/ppermute | solution.py:36
  232.5 1.8 collective-permute-start.62
  239.0 3.3 %collective-permute-start.63 = (bf16[3584,128]{1,0:T(8,128)(2,1)S(1)}, bf16[3584,128]{1,0:T(8,128)(2,1)S(1)}, u32[]{:S(2)}, u32[]{:S(2)}) collective-permute-start(bf16[3584,128]{1,0:T(8,128)(2,1)S(1)} %collective-permute-done.56.refs_2_), channel_id=1, source_target_pairs={{0,8},{8,0},{16,24},{24,16},{1,9},{9,1},{17,25},{25,17},{2,10},{10... | collective-permute-start | bytes 2752520 | tf_op jit(solution)/shard_map/ppermute | solution.py:26
  (59 other events, 948.6 us)
